TPU v7x, 32 devices: a whole 2x2x4 slice. The times are simulated.
32 devices in a mesh: groups: 2 (over y), row: 4 (over z), col: 4 (over x, core).
Axes of the slice: x: 2, y: 2, z: 4, core: 2. Of those that a mesh axis runs over, the one named last changes fastest.
Arguments:
- xval: bfloat16 [192, 12, 128, 128], P(('groups', 'row', 'col')), parts along dimension 0, may hold values from -5 to 5
- cols: int32 [192, 12], P(('groups', 'row', 'col')), parts along dimension 0, may hold values from 0 to 95, as said below
- keep: int32 [192, 12], P(('groups', 'row', 'col')), parts along dimension 0, may hold values 0 or 1
- flag: int32 [2], P('groups'), parts along dimension 0, may hold values from 0 to 1
Outputs:
- purified: bfloat16 [192, 12, 128, 128], P(('groups', 'row', 'col')), parts along dimension 0
- occupation: float32 [2], P('groups'), parts along dimension 0
There are 2 independent parts, one for each index of `groups`. A program takes and returns all parts, laid end to end along the dimension named above; each array names one. Nothing has to cross between parts.
Inputs may be any that keep to these rules, and one draw needn't show every extreme that they name: cols[i, 0] = i. The entries of one list are distinct. Device d in the order row+col holds block rows d * 6 to d * 6 + 5. Every list names all 6 rows of its own device; its other entries lie in the rows of the 1 device on either side of it in that order, wrapping at the ends, and the lists of one device name exactly 4 distinct rows of each of those 2 devices.
All inputs are finite; a program needn't handle non-finite values. No bound on the sum of `keep` on one device may be relied on, other than what follows from the above.
Results may differ from a plain program's by a relative error of at most 0.001.
Values may be sent and summed in bfloat16 or wider, within the bound.
No kernel may reach another device: no remote copies, remote signals or barrier semaphores. Data moves between devices by JAX's collectives and lax.ppermute only.
A program may use at most 128 MiB of HBM per device.

v0:
```python
import jax
import jax.numpy as jnp
from jax import lax
from jax.sharding import PartitionSpec as P

PEERS = 1
CAP = 4


def from_behind(block, axis, distance):
    devices = range(lax.axis_size(axis))
    route = [((i - distance) % len(devices), i) for i in devices]
    return lax.ppermute(block, axis, route)


def fetch_rows(asked_for, xval, cols):
    clipped = jnp.clip(asked_for, 0, xval.shape[0] - 1)
    valid = asked_for >= 0
    values = jnp.take(xval, clipped, axis=0)
    values = jnp.where(valid[:, None, None, None], values, jnp.zeros((), values.dtype))
    indices = jnp.where(valid[:, None], jnp.take(cols, clipped, axis=0), -1)
    return (values, indices)


def body(xval, cols, keep, flag):
    rows_dev, slot_count, block_width = (xval.shape[0], xval.shape[1], xval.shape[2])
    device_count = lax.axis_size("row") * lax.axis_size("col")
    my_device = cols[0, 0] // rows_dev
    owners = cols // rows_dev
    within = cols % rows_dev
    ahead_by = (owners - my_device) % device_count
    relative = jnp.where(2 * ahead_by > device_count, ahead_by - device_count, ahead_by)
    row_ids = jnp.arange(rows_dev, dtype=jnp.int32)
    offset_list = list(range(1, PEERS + 1)) + list(range(-PEERS, 0))
    slot_ids = jnp.arange(CAP, dtype=jnp.int32)
    source_index = within
    value_parts = [xval]
    list_parts = [cols]
    for peer_order, offset in enumerate(offset_list):
        from_peer = relative == offset
        named_rows = jnp.any(
            from_peer[:, :, None] & (within[:, :, None] == row_ids[None, None, :]), axis=(0, 1)
        )
        named_count = named_rows.astype(jnp.int32)
        slot_rank = jnp.cumsum(named_count) - named_count
        chosen = named_rows[:, None] & (slot_rank[:, None] == slot_ids[None, :])
        wanted = jnp.sum(jnp.where(chosen, row_ids[:, None] + 1, 0), axis=0) - 1
        asked_for = from_behind(wanted, ("row", "col"), offset)
        values, indices = fetch_rows(asked_for, xval, cols)
        got_vals, got_cols = from_behind((values, indices), ("row", "col"), -offset)
        value_parts.append(got_vals)
        list_parts.append(got_cols)
        slot_of = jnp.take(slot_rank, within)
        source_index = jnp.where(from_peer, rows_dev + peer_order * CAP + slot_of, source_index)
    source_vals = jnp.concatenate(value_parts, axis=0)
    source_cols = jnp.concatenate(list_parts, axis=0)

    def square_row(local_row):
        left_row = xval[local_row]
        source_rows = source_index[local_row]
        right_rows = jnp.take(source_vals, source_rows, axis=0)
        right_cols = jnp.take(source_cols, source_rows, axis=0)
        targets = cols[local_row]
        selector = (right_cols[:, None, :] == targets[None, :, None]).astype(jnp.bfloat16)
        picked = jnp.einsum(
            "tsu,tubc->tbsc", selector, right_rows, preferred_element_type=jnp.float32
        ).astype(jnp.bfloat16)
        stacked = picked.reshape(slot_count * block_width, slot_count * block_width)
        left_flat = jnp.transpose(left_row, (1, 0, 2)).reshape(
            block_width, slot_count * block_width
        )
        product = jnp.dot(left_flat, stacked, preferred_element_type=jnp.float32)
        return jnp.transpose(product.reshape(block_width, slot_count, block_width), (1, 0, 2))

    square = lax.map(square_row, row_ids)
    kept_mask = keep[:, :, None, None].astype(jnp.float32)
    square = square * kept_mask
    flag_on = flag[0] == 1
    fresh_values = jnp.where(flag_on, square, 2.0 * xval.astype(jnp.float32) * kept_mask - square)
    trace_term = jnp.sum(jnp.trace(fresh_values[:, 0], axis1=1, axis2=2))
    trace_total = lax.psum(trace_term, ("row", "col"))
    normalizer = 1.0 / (rows_dev * device_count * block_width)
    occupation = jnp.reshape(trace_total * normalizer, (1,)).astype(jnp.float32)
    return (fresh_values.astype(jnp.bfloat16), occupation)


def solution(mesh):
    placed = (
        P(("groups", "row", "col"), None, None, None),
        P(("groups", "row", "col"), None),
        P(("groups", "row", "col"), None),
        P("groups"),
    )
    return jax.shard_map(
        body,
        mesh=mesh,
        in_specs=placed,
        out_specs=(P(("groups", "row", "col"), None, None, None), P("groups")),
        check_vma=False,
    )
```

profile of v0, /device:TPU:0, one launch (start us, length us, event | category | flops | bytes accessed | tf_op | source)
XLA Modules:
  0.0 315.4 jit_solution(18186819616752483857)
XLA Ops:
  6.6 5.0 %collective-permute-start.2 = (s32[4]{0:T(128)S(1)}, s32[4]{0:T(128)S(1)}, u32[]{:S(2)}, u32[]{:S(2)}) collective-permute-start(s32[4]{0:T(128)S(1)} %broadcast_add_fusion), channel_id=1, source_target_pairs={{1,0},{2,1},{3,2},{4,3},{5,4},{6,5},{7,6},{8,7},{9,8},{10,9},{11,1... | collective-permute-start | bytes 56 | tf_op jit(solution)/shard_map/ppermute | solution.py:13
  37.5 9.4 %collective-permute-done.5 = s32[4,12]{1,0:T(4,128)S(1)} collective-permute-done((s32[4,12]{1,0:T(4,128)S(1)}, s32[4,12]{1,0:T(4,128)S(1)}, u32[]{:S(2)}, u32[]{:S(2)}) %collective-permute-start.5) | collective-permute-done | bytes 224 | tf_op jit(solution)/shard_map/ppermute | solution.py:13
  47.0 4.9 %pad_maximum_fusion = bf16[14,12,128,128]{3,2,1,0:T(8,128)(2,1)} fusion(bf16[4,12,128,128]{3,2,1,0:T(8,128)(2,1)} %collective-permute-done.3, bf16[4,12,128,128]{3,2,1,0:T(8,128)(2,1)} %collective-permute-done.1, bf16[6,12,128,128]{3,2,1,0:T(8,128)(2,1)S(1)} %copy-done), kind=kLoop, calls=%fused_computation.30 | loop fusion | flops 5505024 | bytes 11010048 | tf_op jit(solution)/shard_map/concatenate | solution.py:55
  51.9 218.3 %while.10 = (s32[]{:T(128)}, f32[6,12,128,128]{3,2,1,0:T(8,128)}, s32[6]{0:T(128)S(1)}, bf16[6,12,128,128]{3,2,1,0:T(8,128)(2,1)S(1)}, s32[6,12]{1,0:T(8,128)S(1...) while((s32[]{:T(128)}, f32[6,12,128,128]{3,2,1,0:T(8,128)}, ...), condition=%wide.region_7.11_spmd, body=%wide.region_6.10_spmd.sunk | while | flops 665324480 | bytes 54665152 | solution.py:75
  54.4 6.1 %gather_fusion = bf16[12,12,128,128]{3,2,1,0:T(8,128)(2,1)} fusion(bf16[14,12,128,128]{3,2,1,0:T(8,128)(2,1)} %get-tuple-element.190, s32[1024]{0:T(1024)S(1)} %pad_clamp_fusion.5), kind=kCustom, calls=%fused_computation.3.clone.1 | custom fusion | bytes 9437232 | tf_op jit(solution)/shard_map/while/body/eval_jaxpr/jit(_take)/gather | solution.py:61
  60.5 5.1 %broadcast_select_fusion.4 = bf16[12,12,128,128]{3,2,1,0:T(8,128)(2,1)} fusion(bf16[12,12,128,128]{3,2,1,0:T(8,128)(2,1)} %gather_fusion, pred[12]{0:T(512)(128)(4,1)S(1)} %compare_and_fusion.4), kind=kLoop, calls=%fused_computation.11.clone.1 | loop fusion | flops 2359296 | bytes 9437196 | tf_op jit(solution)/shard_map/while/body/eval_jaxpr/jit(_take)/select_n | solution.py:61
  66.2 5.7 %fusion.42 = bf16[12,128,128,12]{2,3,1,0:T(8,128)(2,1)S(1)} fusion(bf16[12,12,128,128]{3,2,1,0:T(8,128)(2,1)} %broadcast_select_fusion.4, s32[12,12]{1,0:T(8,128)S(1)} %broadcast_select_fusion.5, s32[12]{0:T(128)S(1)} %fusion.41), kind=kOutput, calls=%fused_computation.12.clone.1 | convolution fusion | flops 58984128 | bytes 9437808 | tf_op jit(solution)/shard_map/while/body/eval_jaxpr/tsu,tubc->tbsc/dot_general | solution.py:65
  76.5 6.6 %copy.39 = bf16[1536,1536]{1,0:T(8,128)(2,1)} copy(bf16[1536,1536]{0,1:T(8,128)(2,1)} %bitcast.87) | data formatting | bytes 9437184 | tf_op jit(solution)/shard_map/while/body/eval_jaxpr/dot_general | solution.py:72
  83.3 4.9 %fusion.43 = f32[6,12,128,128]{3,2,1,0:T(8,128)} fusion(f32[6,12,128,128]{3,2,1,0:T(8,128)} %get-tuple-element.175, s32[]{:T(128)} %get-tuple-element.174, bf16[128,1536,1]{0,1,2:T(8,128)(2,1)S(1)} %bitcast.88, bf16[12,128,1536]{2,1,0:T(8,128)(2,1)} %bitcast.86), kind=kOutput, calls=%fused_computation.14.clone.1 | convolution fusion | flops 603979776 | bytes 5898752 | tf_op jit(solution)/shard_map/while/body/eval_jaxpr/dot_general | solution.py:72
  90.8 6.1 %gather_fusion = bf16[12,12,128,128]{3,2,1,0:T(8,128)(2,1)} fusion(bf16[14,12,128,128]{3,2,1,0:T(8,128)(2,1)} %get-tuple-element.190, s32[1024]{0:T(1024)S(1)} %pad_clamp_fusion.5), kind=kCustom, calls=%fused_computation.3.clone.1 | custom fusion | bytes 9437232 | tf_op jit(solution)/shard_map/while/body/eval_jaxpr/jit(_take)/gather | solution.py:61
  96.9 5.1 %broadcast_select_fusion.4 = bf16[12,12,128,128]{3,2,1,0:T(8,128)(2,1)} fusion(bf16[12,12,128,128]{3,2,1,0:T(8,128)(2,1)} %gather_fusion, pred[12]{0:T(512)(128)(4,1)S(1)} %compare_and_fusion.4), kind=kLoop, calls=%fused_computation.11.clone.1 | loop fusion | flops 2359296 | bytes 9437196 | tf_op jit(solution)/shard_map/while/body/eval_jaxpr/jit(_take)/select_n | solution.py:61
  102.6 5.7 %fusion.42 = bf16[12,128,128,12]{2,3,1,0:T(8,128)(2,1)S(1)} fusion(bf16[12,12,128,128]{3,2,1,0:T(8,128)(2,1)} %broadcast_select_fusion.4, s32[12,12]{1,0:T(8,128)S(1)} %broadcast_select_fusion.5, s32[12]{0:T(128)S(1)} %fusion.41), kind=kOutput, calls=%fused_computation.12.clone.1 | convolution fusion | flops 58984128 | bytes 9437808 | tf_op jit(solution)/shard_map/while/body/eval_jaxpr/tsu,tubc->tbsc/dot_general | solution.py:65
  112.9 6.6 %copy.39 = bf16[1536,1536]{1,0:T(8,128)(2,1)} copy(bf16[1536,1536]{0,1:T(8,128)(2,1)} %bitcast.87) | data formatting | bytes 9437184 | tf_op jit(solution)/shard_map/while/body/eval_jaxpr/dot_general | solution.py:72
  127.2 6.1 %gather_fusion = bf16[12,12,128,128]{3,2,1,0:T(8,128)(2,1)} fusion(bf16[14,12,128,128]{3,2,1,0:T(8,128)(2,1)} %get-tuple-element.190, s32[1024]{0:T(1024)S(1)} %pad_clamp_fusion.5), kind=kCustom, calls=%fused_computation.3.clone.1 | custom fusion | bytes 9437232 | tf_op jit(solution)/shard_map/while/body/eval_jaxpr/jit(_take)/gather | solution.py:61
  133.3 5.1 %broadcast_select_fusion.4 = bf16[12,12,128,128]{3,2,1,0:T(8,128)(2,1)} fusion(bf16[12,12,128,128]{3,2,1,0:T(8,128)(2,1)} %gather_fusion, pred[12]{0:T(512)(128)(4,1)S(1)} %compare_and_fusion.4), kind=kLoop, calls=%fused_computation.11.clone.1 | loop fusion | flops 2359296 | bytes 9437196 | tf_op jit(solution)/shard_map/while/body/eval_jaxpr/jit(_take)/select_n | solution.py:61
  139.0 5.7 %fusion.42 = bf16[12,128,128,12]{2,3,1,0:T(8,128)(2,1)S(1)} fusion(bf16[12,12,128,128]{3,2,1,0:T(8,128)(2,1)} %broadcast_select_fusion.4, s32[12,12]{1,0:T(8,128)S(1)} %broadcast_select_fusion.5, s32[12]{0:T(128)S(1)} %fusion.41), kind=kOutput, calls=%fused_computation.12.clone.1 | convolution fusion | flops 58984128 | bytes 9437808 | tf_op jit(solution)/shard_map/while/body/eval_jaxpr/tsu,tubc->tbsc/dot_general | solution.py:65
  149.2 6.6 %copy.39 = bf16[1536,1536]{1,0:T(8,128)(2,1)} copy(bf16[1536,1536]{0,1:T(8,128)(2,1)} %bitcast.87) | data formatting | bytes 9437184 | tf_op jit(solution)/shard_map/while/body/eval_jaxpr/dot_general | solution.py:72
  163.5 6.1 %gather_fusion = bf16[12,12,128,128]{3,2,1,0:T(8,128)(2,1)} fusion(bf16[14,12,128,128]{3,2,1,0:T(8,128)(2,1)} %get-tuple-element.190, s32[1024]{0:T(1024)S(1)} %pad_clamp_fusion.5), kind=kCustom, calls=%fused_computation.3.clone.1 | custom fusion | bytes 9437232 | tf_op jit(solution)/shard_map/while/body/eval_jaxpr/jit(_take)/gather | solution.py:61
  169.6 5.1 %broadcast_select_fusion.4 = bf16[12,12,128,128]{3,2,1,0:T(8,128)(2,1)} fusion(bf16[12,12,128,128]{3,2,1,0:T(8,128)(2,1)} %gather_fusion, pred[12]{0:T(512)(128)(4,1)S(1)} %compare_and_fusion.4), kind=kLoop, calls=%fused_computation.11.clone.1 | loop fusion | flops 2359296 | bytes 9437196 | tf_op jit(solution)/shard_map/while/body/eval_jaxpr/jit(_take)/select_n | solution.py:61
  175.3 5.7 %fusion.42 = bf16[12,128,128,12]{2,3,1,0:T(8,128)(2,1)S(1)} fusion(bf16[12,12,128,128]{3,2,1,0:T(8,128)(2,1)} %broadcast_select_fusion.4, s32[12,12]{1,0:T(8,128)S(1)} %broadcast_select_fusion.5, s32[12]{0:T(128)S(1)} %fusion.41), kind=kOutput, calls=%fused_computation.12.clone.1 | convolution fusion | flops 58984128 | bytes 9437808 | tf_op jit(solution)/shard_map/while/body/eval_jaxpr/tsu,tubc->tbsc/dot_general | solution.py:65
  185.6 6.6 %copy.39 = bf16[1536,1536]{1,0:T(8,128)(2,1)} copy(bf16[1536,1536]{0,1:T(8,128)(2,1)} %bitcast.87) | data formatting | bytes 9437184 | tf_op jit(solution)/shard_map/while/body/eval_jaxpr/dot_general | solution.py:72
  192.4 5.0 %fusion.43 = f32[6,12,128,128]{3,2,1,0:T(8,128)} fusion(f32[6,12,128,128]{3,2,1,0:T(8,128)} %get-tuple-element.175, s32[]{:T(128)} %get-tuple-element.174, bf16[128,1536,1]{0,1,2:T(8,128)(2,1)S(1)} %bitcast.88, bf16[12,128,1536]{2,1,0:T(8,128)(2,1)} %bitcast.86), kind=kOutput, calls=%fused_computation.14.clone.1 | convolution fusion | flops 603979776 | bytes 5898752 | tf_op jit(solution)/shard_map/while/body/eval_jaxpr/dot_general | solution.py:72
  200.0 6.1 %gather_fusion = bf16[12,12,128,128]{3,2,1,0:T(8,128)(2,1)} fusion(bf16[14,12,128,128]{3,2,1,0:T(8,128)(2,1)} %get-tuple-element.190, s32[1024]{0:T(1024)S(1)} %pad_clamp_fusion.5), kind=kCustom, calls=%fused_computation.3.clone.1 | custom fusion | bytes 9437232 | tf_op jit(solution)/shard_map/while/body/eval_jaxpr/jit(_take)/gather | solution.py:61
  206.0 5.1 %broadcast_select_fusion.4 = bf16[12,12,128,128]{3,2,1,0:T(8,128)(2,1)} fusion(bf16[12,12,128,128]{3,2,1,0:T(8,128)(2,1)} %gather_fusion, pred[12]{0:T(512)(128)(4,1)S(1)} %compare_and_fusion.4), kind=kLoop, calls=%fused_computation.11.clone.1 | loop fusion | flops 2359296 | bytes 9437196 | tf_op jit(solution)/shard_map/while/body/eval_jaxpr/jit(_take)/select_n | solution.py:61
  211.8 5.7 %fusion.42 = bf16[12,128,128,12]{2,3,1,0:T(8,128)(2,1)S(1)} fusion(bf16[12,12,128,128]{3,2,1,0:T(8,128)(2,1)} %broadcast_select_fusion.4, s32[12,12]{1,0:T(8,128)S(1)} %broadcast_select_fusion.5, s32[12]{0:T(128)S(1)} %fusion.41), kind=kOutput, calls=%fused_computation.12.clone.1 | convolution fusion | flops 58984128 | bytes 9437808 | tf_op jit(solution)/shard_map/while/body/eval_jaxpr/tsu,tubc->tbsc/dot_general | solution.py:65
  222.0 6.6 %copy.39 = bf16[1536,1536]{1,0:T(8,128)(2,1)} copy(bf16[1536,1536]{0,1:T(8,128)(2,1)} %bitcast.87) | data formatting | bytes 9437184 | tf_op jit(solution)/shard_map/while/body/eval_jaxpr/dot_general | solution.py:72
  228.9 5.0 %fusion.43 = f32[6,12,128,128]{3,2,1,0:T(8,128)} fusion(f32[6,12,128,128]{3,2,1,0:T(8,128)} %get-tuple-element.175, s32[]{:T(128)} %get-tuple-element.174, bf16[128,1536,1]{0,1,2:T(8,128)(2,1)S(1)} %bitcast.88, bf16[12,128,1536]{2,1,0:T(8,128)(2,1)} %bitcast.86), kind=kOutput, calls=%fused_computation.14.clone.1 | convolution fusion | flops 603979776 | bytes 5898752 | tf_op jit(solution)/shard_map/while/body/eval_jaxpr/dot_general | solution.py:72
  236.4 6.1 %gather_fusion = bf16[12,12,128,128]{3,2,1,0:T(8,128)(2,1)} fusion(bf16[14,12,128,128]{3,2,1,0:T(8,128)(2,1)} %get-tuple-element.190, s32[1024]{0:T(1024)S(1)} %pad_clamp_fusion.5), kind=kCustom, calls=%fused_computation.3.clone.1 | custom fusion | bytes 9437232 | tf_op jit(solution)/shard_map/while/body/eval_jaxpr/jit(_take)/gather | solution.py:61
  242.5 5.1 %broadcast_select_fusion.4 = bf16[12,12,128,128]{3,2,1,0:T(8,128)(2,1)} fusion(bf16[12,12,128,128]{3,2,1,0:T(8,128)(2,1)} %gather_fusion, pred[12]{0:T(512)(128)(4,1)S(1)} %compare_and_fusion.4), kind=kLoop, calls=%fused_computation.11.clone.1 | loop fusion | flops 2359296 | bytes 9437196 | tf_op jit(solution)/shard_map/while/body/eval_jaxpr/jit(_take)/select_n | solution.py:61
  248.2 5.7 %fusion.42 = bf16[12,128,128,12]{2,3,1,0:T(8,128)(2,1)S(1)} fusion(bf16[12,12,128,128]{3,2,1,0:T(8,128)(2,1)} %broadcast_select_fusion.4, s32[12,12]{1,0:T(8,128)S(1)} %broadcast_select_fusion.5, s32[12]{0:T(128)S(1)} %fusion.41), kind=kOutput, calls=%fused_computation.12.clone.1 | convolution fusion | flops 58984128 | bytes 9437808 | tf_op jit(solution)/shard_map/while/body/eval_jaxpr/tsu,tubc->tbsc/dot_general | solution.py:65
  258.4 6.6 %copy.39 = bf16[1536,1536]{1,0:T(8,128)(2,1)} copy(bf16[1536,1536]{0,1:T(8,128)(2,1)} %bitcast.87) | data formatting | bytes 9437184 | tf_op jit(solution)/shard_map/while/body/eval_jaxpr/dot_general | solution.py:72
  275.7 37.9 %psum.7 = f32[]{:T(128)} all-reduce(f32[]{:T(128)} %fusion.13), channel_id=1, replica_groups=mesh['groups'=2,'row'=4,'col'=4] {'row','col'}, use_global_device_ids=true, to_apply=%region_9.13 | all-reduce | flops 1 | bytes 8 | tf_op jit(solution)/shard_map/psum | solution.py:81
  (120 shorter events, 85.4 us)
Async XLA Ops:
  0.6 18.6 %copy-start = (bf16[6,12,128,128]{3,2,1,0:T(8,128)(2,1)S(1)}, bf16[6,12,128,128]{3,2,1,0:T(8,128)(2,1)}, u32[]{:S(2)}) copy-start(bf16[6,12,128,128]{3,2,1,0:T(8,128)(2,1)} %param.12) | copy-start | bytes 7077892
  6.1 6.7 %collective-permute-start = (s32[4]{0:T(128)S(1)}, s32[4]{0:T(128)S(1)}, u32[]{:S(2)}, u32[]{:S(2)}) collective-permute-start(s32[4]{0:T(128)S(1)} %broadcast_add_fusion.1), channel_id=1, source_target_pairs={{15,0},{0,1},{1,2},{2,3},{3,4},{4,5},{5,6},{6,7},{7,8},{8,9},{9,10... | collective-permute-start | bytes 56 | tf_op jit(solution)/shard_map/ppermute | solution.py:13
  6.6 12.6 %collective-permute-start.2 = (s32[4]{0:T(128)S(1)}, s32[4]{0:T(128)S(1)}, u32[]{:S(2)}, u32[]{:S(2)}) collective-permute-start(s32[4]{0:T(128)S(1)} %broadcast_add_fusion), channel_id=1, source_target_pairs={{1,0},{2,1},{3,2},{4,3},{5,4},{6,5},{7,6},{8,7},{9,8},{10,9},{11,1... | collective-permute-start | bytes 56 | tf_op jit(solution)/shard_map/ppermute | solution.py:13
  19.2 27.8 %collective-permute-start.1 = (bf16[4,12,128,128]{3,2,1,0:T(8,128)(2,1)}, bf16[4,12,128,128]{3,2,1,0:T(8,128)(2,1)}, u32[]{:S(2)}, u32[]{:S(2)}) collective-permute-start(bf16[4,12,128,128]{3,2,1,0:T(8,128)(2,1)} %select_select_fusion.1), channel_id=1, source_target_pairs={{1,0},{2,1},{3,2},{4,3},{5,4},{6,5},{7,6},{8,7},{9,8},{10,9},{11,1... | collective-permute-start | bytes 4718600 | tf_op jit(solution)/shard_map/ppermute | solution.py:13
  24.0 3.2 %copy-start.2 = (s32[6,12]{1,0:T(8,128)S(1)}, s32[6,12]{1,0:T(8,128)}, u32[]{:S(2)}) copy-start(s32[6,12]{1,0:T(8,128)} %param.14) | copy-start | bytes 868
  24.0 3.9 %copy-start.1 = (s32[6,12]{1,0:T(8,128)S(1)}, s32[6,12]{1,0:T(8,128)}, u32[]{:S(2)}) copy-start(s32[6,12]{1,0:T(8,128)} %param.13) | copy-start | bytes 868
  24.0 23.0 %collective-permute-start.3 = (bf16[4,12,128,128]{3,2,1,0:T(8,128)(2,1)}, bf16[4,12,128,128]{3,2,1,0:T(8,128)(2,1)}, u32[]{:S(2)}, u32[]{:S(2)}) collective-permute-start(bf16[4,12,128,128]{3,2,1,0:T(8,128)(2,1)} %select_select_fusion), channel_id=1, source_target_pairs={{15,0},{0,1},{1,2},{2,3},{3,4},{4,5},{5,6},{6,7},{7,8},{8,9},{9,10... | collective-permute-start | bytes 4718600 | tf_op jit(solution)/shard_map/ppermute | solution.py:13
  29.1 8.4 %collective-permute-start.4 = (s32[4,12]{1,0:T(4,128)S(1)}, s32[4,12]{1,0:T(4,128)S(1)}, u32[]{:S(2)}, u32[]{:S(2)}) collective-permute-start(s32[4,12]{1,0:T(4,128)S(1)} %select_select_fusion.3), channel_id=1, source_target_pairs={{1,0},{2,1},{3,2},{4,3},{5,4},{6,5},{7,6},{8,7},{9,8},{10,9},{11,1... | collective-permute-start | bytes 584 | tf_op jit(solution)/shard_map/ppermute | solution.py:13
  33.1 13.8 %collective-permute-start.5 = (s32[4,12]{1,0:T(4,128)S(1)}, s32[4,12]{1,0:T(4,128)S(1)}, u32[]{:S(2)}, u32[]{:S(2)}) collective-permute-start(s32[4,12]{1,0:T(4,128)S(1)} %select_select_fusion.2), channel_id=1, source_target_pairs={{15,0},{0,1},{1,2},{2,3},{3,4},{4,5},{5,6},{6,7},{7,8},{8,9},{9,10... | collective-permute-start | bytes 584 | tf_op jit(solution)/shard_map/ppermute | solution.py:13
where the time goes:
time: 318 us; the launch traced here: 315 us
  local copies, waits for them, and re-layouts  122 us (38%)
  matrix products  63.7 us (20%)
  other arithmetic  49.3 us (16%)
  blocking collectives  37.9 us (12%)
  waiting for transfers between devices  15 us (5%)
  loops' own time  11.9 us (4%)
  starting transfers between devices  10.1 us (3%)
  between operations  5.19 us (2%)
    dot_general x6, local copies, waits for them, and re-layouts, square_row(): product = jnp.dot(left_flat, stacked, preferred_element_type=jnp.float32)  39.6 us
    psum x1, blocking collectives, body(): trace_total = lax.psum(trace_term, ('row', 'col'))  37.9 us
    gather x6, local copies, waits for them, and re-layouts, square_row(): right_rows = jnp.take(source_vals, source_rows, axis=0)  36.5 us
    dot_general x6, matrix products, square_row(): jnp.einsum('tsu,tubc->tbsc', selector, right_rows, preferred_element_type...  34.1 us
    select_n x12, other arithmetic, square_row(): right_rows = jnp.take(source_vals, source_rows, axis=0)  30.5 us
    dot_general x6, matrix products, square_row(): product = jnp.dot(left_flat, stacked, preferred_element_type=jnp.float32)  29.5 us
    while x6, local copies, waits for them, and re-layouts  27.1 us
    ppermute x6, waiting for transfers between devices, from_behind(): return lax.ppermute(block, axis, route)  15 us
  transfers between devices with their start and end apart: 6, of which 3 were waited for; matrix products, arithmetic and copies ran while one was open for 5% of the time, Pallas kernels for 0%

commit v1 on v0

v1 whole, which is shorter than its diff:
```python
import jax
import jax.numpy as jnp
from jax import lax
from jax.experimental import pallas as pl
from jax.experimental.pallas import tpu as pltpu
from jax.sharding import PartitionSpec as P

CAP = 4
RING = ("row", "col")
SMEM = pl.BlockSpec(memory_space=pltpu.SMEM)
VMEM = pl.BlockSpec(memory_space=pltpu.VMEM)
ANY = pl.BlockSpec(memory_space=pl.ANY)


def shift(block, distance):
    n = lax.axis_size(RING)
    return lax.ppermute(block, RING, [(i, (i + distance) % n) for i in range(n)])


def ring_sum(value):
    n = lax.axis_size(RING)
    if n & (n - 1):
        return lax.psum(value, RING)
    step = 1
    while step < n:
        value = value + lax.ppermute(value, RING, [(i, i ^ step) for i in range(n)])
        step *= 2
    return value


def scan_own(cols, table, names, total_rows):
    rows, slots = cols.shape
    wide = 3 * rows
    base = cols[0, 0]
    for q in range(rows * wide):
        table[q] = -1
    for q in range(wide):
        names[q] = 0
    for i in range(rows):
        for s in range(slots):
            rel = cols[i, s] - base
            rel = jnp.where(rel < 0, rel + total_rows, rel)
            rel = jnp.where(rel >= 2 * rows, rel - (total_rows - wide), rel)
            table[i * wide + rel] = s
            names[rel] = 1


def scan_peer(cols, names, base):
    rows, slots = cols.shape
    for q in range(rows + 1):
        names[q] = 0
    for i in range(rows):
        for s in range(slots):
            rel = cols[i, s] - base
            inside = (rel >= 0) & (rel < rows)
            names[jnp.where(inside, rel, rows)] = 1


def rank(names, start, rows, order):
    count = 0
    for r in range(rows):
        named = names[start + r]
        order[jnp.where(named > 0, jnp.minimum(count, CAP), CAP)] = r
        count = count + named


def put_block(x, zeros, table, row, column, wide, target, a, b, sem):
    block = x.shape[-1]
    slot = table[row * wide + column]
    place = target.at[pl.ds(a * block, block), pl.ds(b * block, block)]

    @pl.when(slot >= 0)
    def _():
        pltpu.make_async_copy(x.at[row, slot], place, sem).start()

    @pl.when(slot < 0)
    def _():
        pltpu.make_async_copy(zeros, place, sem).start()


def pack_ahead(total_rows, cols, x, far, zeros, table, names, order, sem):
    rows = cols.shape[0]
    wide = 3 * rows
    zeros[...] = jnp.zeros_like(zeros)
    scan_own(cols, table, names, total_rows)
    rank(names, rows, rows, order)
    for i in range(rows):
        for c in range(CAP):
            put_block(x, zeros, table, i, rows + order[c], wide, far, i, c, sem)
    pltpu.make_async_copy(far, far, sem).wait()


def pack_named(total_rows, cols, cols_ahead, cols_behind, x, near_ahead, far_behind, near_behind,
               zeros, table, names, order, peer, asked_ahead, asked_behind, sem):
    rows = cols.shape[0]
    wide = 3 * rows
    zeros[...] = jnp.zeros_like(zeros)
    scan_own(cols, table, names, total_rows)
    rank(names, 2 * rows, rows, order)
    base = cols[0, 0]
    scan_peer(cols_ahead, peer, base)
    rank(peer, 0, rows, asked_ahead)
    scan_peer(cols_behind, peer, base)
    rank(peer, 0, rows, asked_behind)
    for a in range(CAP):
        for b in range(CAP):
            put_block(x, zeros, table, asked_ahead[a], asked_ahead[b], wide, near_ahead, a, b, sem.at[0])
            put_block(x, zeros, table, asked_behind[a], 2 * rows + order[b], wide, far_behind, a, b, sem.at[1])
            put_block(x, zeros, table, asked_behind[a], asked_behind[b], wide, near_behind, a, b, sem.at[2])
    for k, out in enumerate((near_ahead, far_behind, near_behind)):
        pltpu.make_async_copy(out, out, sem.at[k]).wait()


def eye_sum(blocks):
    n = blocks.shape[-1]
    on = lax.broadcasted_iota(jnp.int32, (n, n), 0) == lax.broadcasted_iota(jnp.int32, (n, n), 1)
    return jnp.where(on, blocks, 0.0)


def own_part(total_rows, cols, keep, flag, x, lo, lp, lm, so, sp, sm, trace, table, names, order_p, order_m):
    rows = cols.shape[0]
    wide = 3 * rows
    block = x.shape[-1]
    scan_own(cols, table, names, total_rows)
    rank(names, rows, rows, order_p)
    rank(names, 2 * rows, rows, order_m)
    for i in range(rows):
        span = pl.ds(i * block, block)
        for k in range(rows):
            lo[span, pl.ds(k * block, block)] = x[i, table[i * wide + k]]
        for c in range(CAP):
            for out, start, order in ((lp, rows, order_p), (lm, 2 * rows, order_m)):
                slot = table[i * wide + start + order[c]]
                value = x[i, jnp.maximum(slot, 0)]
                out[span, pl.ds(c * block, block)] = jnp.where(slot >= 0, value, jnp.zeros_like(value))
    left = lo[...]
    so[...] = jnp.dot(left, left, preferred_element_type=jnp.float32)
    sp[...] = jnp.dot(left, lp[...], preferred_element_type=jnp.float32)
    sm[...] = jnp.dot(left, lm[...], preferred_element_type=jnp.float32)
    twice = jnp.where(flag[0] == 1, 0.0, 2.0)
    sign = jnp.where(flag[0] == 1, 1.0, -1.0)
    total = jnp.zeros((block, block), jnp.float32)
    for i in range(rows):
        span = pl.ds(i * block, block)
        kept = keep[i, 0].astype(jnp.float32)
        total = total + (kept * twice) * lo[span, span].astype(jnp.float32) + (kept * sign) * so[span, span]
    trace[...] = jnp.sum(eye_sum(total), axis=0, keepdims=True)


def trace_part(total_rows, cols, keep, flag, cols_behind, keep_behind, lm, far, trace_own, trace, table, names, order, peer, asked):
    rows = cols.shape[0]
    block = lm.shape[0] // rows
    scan_own(cols, table, names, total_rows)
    rank(names, 2 * rows, rows, order)
    scan_peer(cols_behind, peer, cols[0, 0])
    rank(peer, 0, rows, asked)
    sign = jnp.where(flag[0] == 1, 1.0, -1.0)
    total = jnp.zeros((block, block), jnp.float32)
    for r in range(CAP):
        theirs = order[r]
        for c in range(CAP):
            mine = asked[c]
            weight = sign * (keep[mine, 0] + keep_behind[theirs, 0]).astype(jnp.float32)
            left = far[pl.ds(pl.multiple_of(theirs * block, block), block), pl.ds(c * block, block)]
            right = lm[pl.ds(pl.multiple_of(mine * block, block), block), pl.ds(r * block, block)]
            total = total + weight * jnp.dot(left, right, preferred_element_type=jnp.float32)
    trace[...] = trace_own[...] + jnp.sum(eye_sum(total), axis=0, keepdims=True)


def finish(keep, flag, i, slot, value, square):
    kept = keep[i, slot].astype(jnp.float32)
    twice = kept * jnp.where(flag[0] == 1, 0.0, 2.0)
    sign = kept * jnp.where(flag[0] == 1, 1.0, -1.0)
    return (twice * value.astype(jnp.float32) + sign * square).astype(jnp.bfloat16)


def middle_part(total_rows, cols, keep, flag, cols_ahead, cols_behind, lo, lp, lm, so, sm, far, near_m, far_p, out,
                own, behind, stage, table, names, order_m, peer, asked_p, asked_m, sem):
    rows = cols.shape[0]
    wide = 3 * rows
    block = lo.shape[0] // rows
    scan_own(cols, table, names, total_rows)
    rank(names, 2 * rows, rows, order_m)
    scan_peer(cols_ahead, peer, cols[0, 0])
    rank(peer, 0, rows, asked_p)
    scan_peer(cols_behind, peer, cols[0, 0])
    rank(peer, 0, rows, asked_m)
    own[...] = so[...]
    picked = jnp.concatenate(
        [far[pl.ds(pl.multiple_of(order_m[r] * block, block), block), :] for r in range(CAP)], axis=0)
    for left, right, asked in ((lm, picked, asked_m), (lp, far_p[...], asked_p)):
        part = jnp.dot(left[...], right, preferred_element_type=jnp.float32)
        for c in range(CAP):
            place = pl.ds(pl.multiple_of(asked[c] * block, block), block)
            own[:, place] = own[:, place] + part[:, c * block:(c + 1) * block]
    behind[...] = sm[...] + jnp.dot(lm[...], near_m[...], preferred_element_type=jnp.float32)
    for i in range(rows):
        span = pl.ds(i * block, block)
        for k in range(rows):
            slot = table[i * wide + k]
            col = pl.ds(k * block, block)
            stage[i, k] = finish(keep, flag, i, slot, lo[span, col], own[span, col])
            pltpu.make_async_copy(stage.at[i, k], out.at[i, slot], sem).start()
        for c in range(CAP):
            slot = table[i * wide + 2 * rows + order_m[c]]
            col = pl.ds(c * block, block)
            stage[i, rows + c] = finish(keep, flag, i, jnp.maximum(slot, 0), lm[span, col], behind[span, col])

            @pl.when(slot >= 0)
            def _():
                pltpu.make_async_copy(stage.at[i, rows + c], out.at[i, slot], sem).start()
    for i in range(rows):
        for k in range(rows):
            pltpu.make_async_copy(stage.at[i, k], out.at[i, 0], sem).wait()
        for c in range(CAP):
            slot = table[i * wide + 2 * rows + order_m[c]]

            @pl.when(slot >= 0)
            def _():
                pltpu.make_async_copy(stage.at[i, rows + c], out.at[i, slot], sem).wait()


def last_part(total_rows, cols, keep, flag, lp, sp, near_p, _, out, stage, table, names, order_p, sem):
    rows = cols.shape[0]
    wide = 3 * rows
    block = lp.shape[0] // rows
    scan_own(cols, table, names, total_rows)
    rank(names, rows, rows, order_p)
    for i in range(rows):
        span = pl.ds(i * block, block)
        square = sp[span, :] + jnp.dot(lp[span, :], near_p[...], preferred_element_type=jnp.float32)
        for c in range(CAP):
            slot = table[i * wide + rows + order_p[c]]
            col = pl.ds(c * block, block)
            stage[i, c] = finish(keep, flag, i, jnp.maximum(slot, 0), lp[span, col], square[:, c * block:(c + 1) * block])

            @pl.when(slot >= 0)
            def _():
                pltpu.make_async_copy(stage.at[i, c], out.at[i, slot], sem).start()
    for i in range(rows):
        for c in range(CAP):
            slot = table[i * wide + rows + order_p[c]]

            @pl.when(slot >= 0)
            def _():
                pltpu.make_async_copy(stage.at[i, c], out.at[i, slot], sem).wait()


def body(x, cols, keep, flag):
    rows, slots, block = x.shape[0], x.shape[1], x.shape[2]
    total_rows = rows * lax.axis_size(RING)
    table = pltpu.SMEM((rows * 3 * rows,), jnp.int32)
    names = pltpu.SMEM((3 * rows,), jnp.int32)
    peer = pltpu.SMEM((rows + 1,), jnp.int32)
    order = pltpu.SMEM((CAP + 1,), jnp.int32)
    zeros = pltpu.VMEM((block, block), x.dtype)
    bf16, f32 = jnp.bfloat16, jnp.float32
    wide, narrow = rows * block, CAP * block

    def call(kernel, shapes, out_specs, in_specs, scratch, name, aliases=None):
        def named(*refs):
            kernel(total_rows, *refs)
        return pl.pallas_call(
            named, out_shape=[jax.ShapeDtypeStruct(*s) for s in shapes], in_specs=in_specs, out_specs=out_specs,
            scratch_shapes=scratch, name=name, input_output_aliases=aliases or {},
            compiler_params=pltpu.CompilerParams(vmem_limit_bytes=48 * 1024 * 1024))

    both = jnp.concatenate([cols, keep], axis=0)
    from_behind = shift(both, 1)
    cols_ahead = shift(cols, -1)
    cols_behind, keep_behind = from_behind[:rows], from_behind[rows:]
    far_send, = call(pack_ahead, [((wide, narrow), bf16)], [ANY], [SMEM, ANY],
                     [zeros, table, names, order, pltpu.SemaphoreType.DMA], "pack_ahead")(cols, x)
    far = shift(far_send, 1)
    near_ahead, far_behind, near_behind = call(
        pack_named, [((narrow, narrow), bf16)] * 3, [ANY] * 3, [SMEM] * 3 + [ANY],
        [zeros, table, names, order, peer, order, order, pltpu.SemaphoreType.DMA((3,))], "pack_named",
    )(cols, cols_ahead, cols_behind, x)
    near_m = shift(near_ahead, 1)
    far_p = shift(far_behind, -1)
    near_p = shift(near_behind, -1)
    lo, lp, lm, so, sp, sm, trace = call(
        own_part,
        [((wide, wide), bf16), ((wide, narrow), bf16), ((wide, narrow), bf16),
         ((wide, wide), f32), ((wide, narrow), f32), ((wide, narrow), f32), ((1, block), f32)],
        [VMEM] * 7, [SMEM] * 3 + [VMEM], [table, names, order, order], "own_part")(cols, keep, flag, x)
    trace, = call(trace_part, [((1, block), f32)], [VMEM], [SMEM] * 5 + [VMEM] * 3,
                  [table, names, order, peer, order], "trace_part",
                  )(cols, keep, flag, cols_behind, keep_behind, lm, far, trace)
    partial = jnp.sum(trace).reshape(1) * (1.0 / (total_rows * block))
    occupation = ring_sum(partial)
    out, = call(
        middle_part, [(x.shape, bf16)], [ANY], [SMEM] * 5 + [VMEM] * 8,
        [pltpu.VMEM((wide, wide), f32), pltpu.VMEM((wide, narrow), f32),
         pltpu.VMEM((rows, rows + CAP, block, block), bf16), table, names, order, peer, order, order,
         pltpu.SemaphoreType.DMA],
        "middle_part")(cols, keep, flag, cols_ahead, cols_behind, lo, lp, lm, so, sm, far, near_m, far_p)
    out, = call(
        last_part, [(x.shape, bf16)], [ANY], [SMEM] * 3 + [VMEM] * 3 + [ANY],
        [pltpu.VMEM((rows, CAP, block, block), bf16), table, names, order, pltpu.SemaphoreType.DMA],
        "last_part", {6: 0})(cols, keep, flag, lp, sp, near_p, out)
    return out, occupation


def solution(mesh):
    placed = (
        P(("groups", "row", "col"), None, None, None),
        P(("groups", "row", "col"), None),
        P(("groups", "row", "col"), None),
        P("groups"),
    )
    return jax.shard_map(
        body,
        mesh=mesh,
        in_specs=placed,
        out_specs=(P(("groups", "row", "col"), None, None, None), P("groups")),
        check_vma=False,
    )
```

time: 318 us -> 65.8 us (0.21)
  local copies, waits for them, and re-layouts: 122 us -> 6.56 us
  matrix products: 63.7 us -> 0 us
  other arithmetic: 49.3 us -> 1.34 us
  blocking collectives: 37.9 us -> 0 us
  Pallas kernels: 0 us -> 18.9 us
  loops' own time: 11.9 us -> 0 us
  starting transfers between devices: 10.1 us -> 19 us
    dot_general x12 -> x0, matrix products: 63.7 us -> none  [the longest x6 34.1 us: square_row(): jnp.einsum('tsu,tubc->tbsc', selector, right_rows, preferred_element_type...]
    gather x20 -> x0, local copies, waits for them, and re-layouts: 49 us -> none  [the longest x6 36.5 us: square_row(): right_rows = jnp.take(source_vals, source_rows, axis=0)]
    dot_general x6 -> x0, local copies, waits for them, and re-layouts: 39.6 us -> none  [square_row(): product = jnp.dot(left_flat, stacked, preferred_element_type=jnp.float32)]
    psum x1 -> x0, blocking collectives: 37.9 us -> none  [body(): trace_total = lax.psum(trace_term, ('row', 'col'))]
    select_n x24 -> x0, other arithmetic: 37.4 us -> none  [the longest x12 30.5 us: square_row(): right_rows = jnp.take(source_vals, source_rows, axis=0)]
    while x6 -> x0, local copies, waits for them, and re-layouts: 27.1 us -> none
    pallas_call x0 -> x6, Pallas kernels: none -> 18.9 us  [the longest x1 5.55 us: body(): call(own_part, [((wide, wide), bf16), ((wide, narrow), bf16), ((wide, nar...]
    another operation x1 -> x0, loops' own time: 11.9 us -> none  [body(): square = lax.map(square_row, row_ids)]
  transfers between devices with their start and end apart: 6 -> 10, of which waited for: 3 -> 4; matrix products, arithmetic and copies ran while one was open for 5% -> 2% of each run, Pallas kernels for 0% -> 27%
where the time goes in v1:
time: 65.8 us; the launch traced here: 65.4 us
  starting transfers between devices  19 us (29%)
  Pallas kernels  18.9 us (29%)
  waiting for transfers between devices  13.7 us (21%)
  local copies, waits for them, and re-layouts  6.56 us (10%)
  between operations  5.89 us (9%)
  other arithmetic  1.34 us (2%)
    ppermute x6, starting transfers between devices, shift(): lax.ppermute(block, RING, [(i, (i + distance) % n) for i in range(n)])  10.1 us
    ppermute x6, waiting for transfers between devices, shift(): lax.ppermute(block, RING, [(i, (i + distance) % n) for i in range(n)])  9.62 us
    ppermute x4, starting transfers between devices, ring_sum(): value = value + lax.ppermute(value, RING, [(i, i ^ step) for i in range(n)])  8.83 us
    unnamed x18, local copies, waits for them, and re-layouts  6.56 us
    pallas_call x1, Pallas kernels, body(): call(own_part, [((wide, wide), bf16), ((wide, narrow), bf16), ((wide, nar...  5.55 us
    pallas_call x1, Pallas kernels, body(): call(middle_part, [(x.shape, bf16)], [ANY], [SMEM] * 5 + [VMEM] * 8, [plt...  5.32 us
    ppermute x4, waiting for transfers between devices, ring_sum(): value = value + lax.ppermute(value, RING, [(i, i ^ step) for i in range(n)])  4.11 us
    pallas_call x1, Pallas kernels, body(): call(pack_named, [((narrow, narrow), bf16)] * 3, [ANY] * 3, [SMEM] * 3 +...  2.58 us
  transfers between devices with their start and end apart: 10, of which 4 were waited for; matrix products, arithmetic and copies ran while one was open for 2% of the time, Pallas kernels for 27%

profile of v1, /device:TPU:0, one launch (start us, length us, event | category | flops | bytes accessed | tf_op | source)
XLA Modules:
  0.0 65.4 jit_solution(14798875576175432758)
XLA Ops:
  0.6 0.0 copy-start
  0.6 1.7 %copy-done = bf16[6,12,128,128]{3,2,1,0:T(8,128)(2,1)S(1)} copy-done((bf16[6,12,128,128]{3,2,1,0:T(8,128)(2,1)S(1)}, bf16[6,12,128,128]{3,2,1,0:T(8,128)(2,1)}, u32[]{:S(2)}) %copy-start) | copy-done | bytes 2359320
  2.3 0.7 %copy-done.5 = s32[6,12]{1,0:T(8,128)S(1)} copy-done((s32[6,12]{1,0:T(8,128)S(1)}, s32[6,12]{1,0:T(8,128)}, u32[]{:S(2)}) %copy-start.5) | copy-done | bytes 312
  3.0 1.5 %pack_ahead.1 = bf16[768,512]{1,0:T(8,128)(2,1)S(1)} custom-call(s32[6,12]{1,0:T(8,128)S(1)} %copy-done.5, bf16[6,12,128,128]{3,2,1,0:T(8,128)(2,1)S(1)} %copy-done), custom_call_target="tpu_custom_call" | custom-call | tf_op jit(solution)/shard_map/pack_ahead/pallas_call | solution.py:272
  4.4 0.5 collective-permute-start.3
  5.0 2.7 %collective-permute-start.1 = (s32[12,12]{1,0:T(8,128)S(1)}, s32[12,12]{1,0:T(8,128)S(1)}, u32[]{:S(2)}, u32[]{:S(2)}) collective-permute-start(s32[12,12]{1,0:T(8,128)S(1)} %pad_add_fusion), channel_id=1, source_target_pairs={{0,1},{1,2},{2,3},{3,4},{4,5},{5,6},{6,7},{7,8},{8,9},{9,10},{10,1... | collective-permute-start | bytes 1736 | tf_op jit(solution)/shard_map/ppermute | solution.py:17
  7.6 2.5 %collective-permute-start = (s32[6,12]{1,0:T(8,128)S(1)}, s32[6,12]{1,0:T(8,128)S(1)}, u32[]{:S(2)}, u32[]{:S(2)}) collective-permute-start(s32[6,12]{1,0:T(8,128)S(1)} %copy-done.5), channel_id=1, source_target_pairs={{0,15},{1,0},{2,1},{3,2},{4,3},{5,4},{6,5},{7,6},{8,7},{9,8},{10,9... | collective-permute-start | bytes 872 | tf_op jit(solution)/shard_map/ppermute | solution.py:17
  10.1 9.6 %collective-permute-done.1 = s32[12,12]{1,0:T(8,128)S(1)} collective-permute-done((s32[12,12]{1,0:T(8,128)S(1)}, s32[12,12]{1,0:T(8,128)S(1)}, u32[]{:S(2)}, u32[]{:S(2)}) %collective-permute-start.1) | collective-permute-done | bytes 608 | tf_op jit(solution)/shard_map/ppermute | solution.py:17
  19.7 2.6 %pack_named.1 = (bf16[512,512]{1,0:T(8,128)(2,1)}, bf16[512,512]{1,0:T(8,128)(2,1)}, bf16[512,512]{1,0:T(8,128)(2,1)}) custom-call(s32[6,12]{1,0:T(8,128)S(1)} %copy-done.5, s32[6,12]{1,0:T(8,128)S(1)} %collective-permute-done.refs_1_.refs_3_, s32[6,12]{1,0:T(8,128)S(1)} %get-tuple-element.23.refs_2_.refs_4_.refs_3_, bf16[6,12,128,128]{3,2,1,0:T(8,128)(2,1)S(1)} %copy-done), custom_call_target="tpu_custom_call" | custom-call | tf_op jit(solution)/shard_map/pack_named/pallas_call | solution.py:275
  22.3 0.0 copy-start.6
  22.3 0.1 collective-permute-start.4
  22.4 4.4 %collective-permute-start.5 = (bf16[512,512]{1,0:T(8,128)(2,1)}, bf16[512,512]{1,0:T(8,128)(2,1)}, u32[]{:S(2)}, u32[]{:S(2)}) collective-permute-start(bf16[512,512]{1,0:T(8,128)(2,1)} %get-tuple-element.20), channel_id=1, source_target_pairs={{0,15},{1,0},{2,1},{3,2},{4,3},{5,4},{6,5},{7,6},{8,7},{9,8},{10,9... | collective-permute-start | bytes 1572872 | tf_op jit(solution)/shard_map/ppermute | solution.py:17
  26.8 0.0 collective-permute-start.2
  27.5 5.6 %own_part.1 = (bf16[768,768]{1,0:T(8,128)(2,1)S(1)}, bf16[768,512]{1,0:T(8,128)(2,1)S(1)}, bf16[768,512]{1,0:T(8,128)(2,1)S(1)}, f32[768,768]{1,0:T(8,128)}, f32...) custom-call(s32[6,12]{1,0:T(8,128)S(1)} %copy-done.5, s32[6,12]{1,0:T(8,128)S(1)} %copy-done.7, ...), custom_call_target="tpu_custom_call" | custom-call | tf_op jit(solution)/shard_map/own_part/pallas_call | solution.py:282
  33.0 1.1 %copy-done.1 = f32[768,512]{1,0:T(8,128)} copy-done((f32[768,512]{1,0:T(8,128)}, f32[768,512]{1,0:T(8,128)S(1)}, u32[]{:S(2)}) %copy-start.1) | copy-done | bytes 1572888
  34.2 1.1 %copy-done.3 = f32[768,512]{1,0:T(8,128)} copy-done((f32[768,512]{1,0:T(8,128)}, f32[768,512]{1,0:T(8,128)S(1)}, u32[]{:S(2)}) %copy-start.3) | copy-done | bytes 1572888
  35.3 1.6 %trace_part.1 = f32[1,128]{1,0:T(1,128)S(1)} custom-call(s32[6,12]{1,0:T(8,128)S(1)} %copy-done.5, s32[6,12]{1,0:T(8,128)S(1)} %copy-done.7, s32[1]{0:T(128)S(6)} %copy.8.refs_2_, s32[6,12]{1,0:T(8,128)S(1)} %get-tuple-element.23.refs_2_.refs_4_.refs_3_, s32[6,12]{1,0:T(8,128)S(1)} %get-tuple-element.22.refs_4_, ...), custom_call_target="tpu_custom_call" | custom-call | tf_op jit(solution)/shard_map/trace_part/pallas_call | solution.py:287
  36.9 0.0 copy-start.8
  36.9 0.5 copy-done.8
  37.4 1.3 %reduce_sum.9 = f32[]{:T(128)} reduce(f32[1,128]{1,0:T(1,128)} %copy-done.8, f32[]{:T(128)} %constant.1.clone.1), dimensions={0,1}, to_apply=%region_0.0 | reduce | flops 127 | bytes 520 | tf_op jit(solution)/shard_map/reduce_sum | solution.py:290
  39.4 1.4 %collective-permute-start.6 = (f32[1]{0:T(128)}, f32[1]{0:T(128)}, u32[]{:S(2)}, u32[]{:S(2)}) collective-permute-start(f32[1]{0:T(128)} %bitcast), channel_id=1, source_target_pairs={{0,1},{1,0},{2,3},{3,2},{4,5},{5,4},{6,7},{7,6},{8,9},{9,8},{10,11... | collective-permute-start | bytes 20 | tf_op jit(solution)/shard_map/ppermute | solution.py:26
  40.7 0.0 collective-permute-done.5.refs_12_
  40.7 0.0 copy-start.4
  40.8 1.4 %copy-done.4 = f32[768,512]{1,0:T(8,128)S(1)} copy-done((f32[768,512]{1,0:T(8,128)S(1)}, f32[768,512]{1,0:T(8,128)}, u32[]{:S(2)}) %copy-start.4) | copy-done | bytes 1572888
  42.2 5.3 %middle_part.1.refs_6_ = bf16[6,12,128,128]{3,2,1,0:T(8,128)(2,1)} custom-call(s32[6,12]{1,0:T(8,128)S(1)} %copy-done.6, s32[6,12]{1,0:T(8,128)S(1)} %copy-done.7, s32[1]{0:T(128)S(6)} %copy.8.refs_2_, s32[6,12]{1,0:T(8,128)S(1)} %collective-permute-done.refs_1_.refs_3_, s32[6,12]{1,0:T(8,128)S(1)} %get-tuple-element.23.refs_2_.refs_4_.refs_3_, ...), custom_call_target="tpu_custom_call" | custom-call | tf_op jit(solution)/shard_map/middle_part/pallas_call | solution.py:292
  47.5 2.5 %last_part.1 = bf16[6,12,128,128]{3,2,1,0:T(8,128)(2,1)} custom-call(s32[6,12]{1,0:T(8,128)S(1)} %copy-done.6, s32[6,12]{1,0:T(8,128)S(1)} %copy-done.7, s32[1]{0:T(128)S(6)} %copy.8.refs_2_, bf16[768,512]{1,0:T(8,128)(2,1)S(1)} %get-tuple-element.12.refs_6_.refs_3_, f32[768,512]{1,0:T(8,128)S(1)} %copy-done.2, ...), custom_call_target="tpu_custom_call", output_to_operand_aliasing={{}: (6, {})} | custom-call | tf_op jit(solution)/shard_map/last_part/pallas_call | solution.py:298
  50.6 2.5 %collective-permute-start.7 = (f32[1]{0:T(128)}, f32[1]{0:T(128)}, u32[]{:S(2)}, u32[]{:S(2)}) collective-permute-start(f32[1]{0:T(128)} %add.12), channel_id=1, source_target_pairs={{0,2},{1,3},{2,0},{3,1},{4,6},{5,7},{6,4},{7,5},{8,10},{9,11},{10,... | collective-permute-start | bytes 20 | tf_op jit(solution)/shard_map/ppermute | solution.py:26
  53.1 1.1 %collective-permute-done.7 = f32[1]{0:T(128)} collective-permute-done((f32[1]{0:T(128)}, f32[1]{0:T(128)}, u32[]{:S(2)}, u32[]{:S(2)}) %collective-permute-start.7) | collective-permute-done | bytes 36 | tf_op jit(solution)/shard_map/ppermute | solution.py:26
  54.9 2.0 %collective-permute-start.8 = (f32[1]{0:T(128)}, f32[1]{0:T(128)}, u32[]{:S(2)}, u32[]{:S(2)}) collective-permute-start(f32[1]{0:T(128)} %add.13), channel_id=1, source_target_pairs={{0,4},{1,5},{2,6},{3,7},{4,0},{5,1},{6,2},{7,3},{8,12},{9,13},{10,... | collective-permute-start | bytes 20 | tf_op jit(solution)/shard_map/ppermute | solution.py:26
  56.9 1.5 %collective-permute-done.8 = f32[1]{0:T(128)} collective-permute-done((f32[1]{0:T(128)}, f32[1]{0:T(128)}, u32[]{:S(2)}, u32[]{:S(2)}) %collective-permute-start.8) | collective-permute-done | bytes 36 | tf_op jit(solution)/shard_map/ppermute | solution.py:26
  59.1 3.0 %collective-permute-start.9 = (f32[1]{0:T(128)}, f32[1]{0:T(128)}, u32[]{:S(2)}, u32[]{:S(2)}) collective-permute-start(f32[1]{0:T(128)} %add.14), channel_id=1, source_target_pairs={{0,8},{1,9},{2,10},{3,11},{4,12},{5,13},{6,14},{7,15},{8,0},{9,1},... | collective-permute-start | bytes 20 | tf_op jit(solution)/shard_map/ppermute | solution.py:26
  62.1 1.5 %collective-permute-done.9 = f32[1]{0:T(128)} collective-permute-done((f32[1]{0:T(128)}, f32[1]{0:T(128)}, u32[]{:S(2)}, u32[]{:S(2)}) %collective-permute-start.9) | collective-permute-done | bytes 36 | tf_op jit(solution)/shard_map/ppermute | solution.py:26
  (15 shorter events, 0.0 us)
Async XLA Ops:
  0.6 1.7 %copy-start = (bf16[6,12,128,128]{3,2,1,0:T(8,128)(2,1)S(1)}, bf16[6,12,128,128]{3,2,1,0:T(8,128)(2,1)}, u32[]{:S(2)}) copy-start(bf16[6,12,128,128]{3,2,1,0:T(8,128)(2,1)} %refs_1_.6) | copy-start | bytes 7077892
  2.3 0.7 %copy-start.5 = (s32[6,12]{1,0:T(8,128)S(1)}, s32[6,12]{1,0:T(8,128)}, u32[]{:S(2)}) copy-start(s32[6,12]{1,0:T(8,128)} %refs_0_.11) | copy-start | bytes 868
  3.0 2.0 %copy-start.7 = (s32[6,12]{1,0:T(8,128)S(1)}, s32[6,12]{1,0:T(8,128)}, u32[]{:S(2)}) copy-start(s32[6,12]{1,0:T(8,128)} %refs_1_.9) | copy-start | bytes 868
  4.4 30.9 %collective-permute-start.3 = (bf16[768,512]{1,0:T(8,128)(2,1)S(1)}, bf16[768,512]{1,0:T(8,128)(2,1)S(1)}, u32[]{:S(2)}, u32[]{:S(2)}) collective-permute-start(bf16[768,512]{1,0:T(8,128)(2,1)S(1)} %pack_ahead.1), channel_id=1, source_target_pairs={{0,1},{1,2},{2,3},{3,4},{4,5},{5,6},{6,7},{7,8},{8,9},{9,10},{10,1... | collective-permute-start | bytes 2359304 | tf_op jit(solution)/shard_map/ppermute | solution.py:17
  5.0 14.7 %collective-permute-start.1 = (s32[12,12]{1,0:T(8,128)S(1)}, s32[12,12]{1,0:T(8,128)S(1)}, u32[]{:S(2)}, u32[]{:S(2)}) collective-permute-start(s32[12,12]{1,0:T(8,128)S(1)} %pad_add_fusion), channel_id=1, source_target_pairs={{0,1},{1,2},{2,3},{3,4},{4,5},{5,6},{6,7},{7,8},{8,9},{9,10},{10,1... | collective-permute-start | bytes 1736 | tf_op jit(solution)/shard_map/ppermute | solution.py:17
  7.6 12.1 %collective-permute-start = (s32[6,12]{1,0:T(8,128)S(1)}, s32[6,12]{1,0:T(8,128)S(1)}, u32[]{:S(2)}, u32[]{:S(2)}) collective-permute-start(s32[6,12]{1,0:T(8,128)S(1)} %copy-done.5), channel_id=1, source_target_pairs={{0,15},{1,0},{2,1},{3,2},{4,3},{5,4},{6,5},{7,6},{8,7},{9,8},{10,9... | collective-permute-start | bytes 872 | tf_op jit(solution)/shard_map/ppermute | solution.py:17
  22.3 18.5 %copy-start.6 = (s32[6,12]{1,0:T(8,128)S(1)}, s32[6,12]{1,0:T(8,128)}, u32[]{:S(2)}) copy-start(s32[6,12]{1,0:T(8,128)} %refs_0_.11) | copy-start | bytes 868
  22.3 18.4 %collective-permute-start.4 = (bf16[512,512]{1,0:T(8,128)(2,1)}, bf16[512,512]{1,0:T(8,128)(2,1)}, u32[]{:S(2)}, u32[]{:S(2)}) collective-permute-start(bf16[512,512]{1,0:T(8,128)(2,1)} %get-tuple-element.19), channel_id=1, source_target_pairs={{0,1},{1,2},{2,3},{3,4},{4,5},{5,6},{6,7},{7,8},{8,9},{9,10},{10,1... | collective-permute-start | bytes 1572872 | tf_op jit(solution)/shard_map/ppermute | solution.py:17
  22.4 18.4 %collective-permute-start.5 = (bf16[512,512]{1,0:T(8,128)(2,1)}, bf16[512,512]{1,0:T(8,128)(2,1)}, u32[]{:S(2)}, u32[]{:S(2)}) collective-permute-start(bf16[512,512]{1,0:T(8,128)(2,1)} %get-tuple-element.20), channel_id=1, source_target_pairs={{0,15},{1,0},{2,1},{3,2},{4,3},{5,4},{6,5},{7,6},{8,7},{9,8},{10,9... | collective-permute-start | bytes 1572872 | tf_op jit(solution)/shard_map/ppermute | solution.py:17
  26.8 20.7 %collective-permute-start.2 = (bf16[512,512]{1,0:T(8,128)(2,1)}, bf16[512,512]{1,0:T(8,128)(2,1)}, u32[]{:S(2)}, u32[]{:S(2)}) collective-permute-start(bf16[512,512]{1,0:T(8,128)(2,1)} %get-tuple-element.14), channel_id=1, source_target_pairs={{0,15},{1,0},{2,1},{3,2},{4,3},{5,4},{6,5},{7,6},{8,7},{9,8},{10,9... | collective-permute-start | bytes 1572872 | tf_op jit(solution)/shard_map/ppermute | solution.py:17
  33.0 1.1 %copy-start.1 = (f32[768,512]{1,0:T(8,128)}, f32[768,512]{1,0:T(8,128)S(1)}, u32[]{:S(2)}) copy-start(f32[768,512]{1,0:T(8,128)S(1)} %get-tuple-element.13.refs_4_) | copy-start | bytes 4718596
  34.2 1.1 %copy-start.3 = (f32[768,512]{1,0:T(8,128)}, f32[768,512]{1,0:T(8,128)S(1)}, u32[]{:S(2)}) copy-start(f32[768,512]{1,0:T(8,128)S(1)} %get-tuple-element.18.refs_9_) | copy-start | bytes 4718596
  36.9 0.5 copy-start.8
  39.4 10.6 %collective-permute-start.6 = (f32[1]{0:T(128)}, f32[1]{0:T(128)}, u32[]{:S(2)}, u32[]{:S(2)}) collective-permute-start(f32[1]{0:T(128)} %bitcast), channel_id=1, source_target_pairs={{0,1},{1,0},{2,3},{3,2},{4,5},{5,4},{6,7},{7,6},{8,9},{9,8},{10,11... | collective-permute-start | bytes 20 | tf_op jit(solution)/shard_map/ppermute | solution.py:26
  40.7 1.4 %copy-start.4 = (f32[768,512]{1,0:T(8,128)S(1)}, f32[768,512]{1,0:T(8,128)}, u32[]{:S(2)}) copy-start(f32[768,512]{1,0:T(8,128)} %copy-done.3) | copy-start | bytes 4718596
  42.2 5.3 %copy-start.2 = (f32[768,512]{1,0:T(8,128)S(1)}, f32[768,512]{1,0:T(8,128)}, u32[]{:S(2)}) copy-start(f32[768,512]{1,0:T(8,128)} %copy-done.1) | copy-start | bytes 4718596
  50.6 3.6 %collective-permute-start.7 = (f32[1]{0:T(128)}, f32[1]{0:T(128)}, u32[]{:S(2)}, u32[]{:S(2)}) collective-permute-start(f32[1]{0:T(128)} %add.12), channel_id=1, source_target_pairs={{0,2},{1,3},{2,0},{3,1},{4,6},{5,7},{6,4},{7,5},{8,10},{9,11},{10,... | collective-permute-start | bytes 20 | tf_op jit(solution)/shard_map/ppermute | solution.py:26
  54.9 3.6 %collective-permute-start.8 = (f32[1]{0:T(128)}, f32[1]{0:T(128)}, u32[]{:S(2)}, u32[]{:S(2)}) collective-permute-start(f32[1]{0:T(128)} %add.13), channel_id=1, source_target_pairs={{0,4},{1,5},{2,6},{3,7},{4,0},{5,1},{6,2},{7,3},{8,12},{9,13},{10,... | collective-permute-start | bytes 20 | tf_op jit(solution)/shard_map/ppermute | solution.py:26
  59.1 4.5 %collective-permute-start.9 = (f32[1]{0:T(128)}, f32[1]{0:T(128)}, u32[]{:S(2)}, u32[]{:S(2)}) collective-permute-start(f32[1]{0:T(128)} %add.14), channel_id=1, source_target_pairs={{0,8},{1,9},{2,10},{3,11},{4,12},{5,13},{6,14},{7,15},{8,0},{9,1},... | collective-permute-start | bytes 20 | tf_op jit(solution)/shard_map/ppermute | solution.py:26

commit v2 on v0

v2 whole, which is shorter than its diff:
```python
import functools

import jax
import jax.numpy as jnp
from jax import lax
from jax.experimental import pallas as pl
from jax.experimental.pallas import tpu as pltpu
from jax.sharding import PartitionSpec as P

CAP = 4
RING = ("row", "col")
SMEM = pl.BlockSpec(memory_space=pltpu.SMEM)
VMEM = pl.BlockSpec(memory_space=pltpu.VMEM)
HBM = pl.BlockSpec(memory_space=pltpu.HBM)
MIB = 1024 * 1024


def permute(value, pairs):
    return lax.ppermute(value, RING, pairs)


def ring_sum(value):
    n, cols = lax.axis_size(RING), lax.axis_size("col")
    if n & (n - 1) or cols & (cols - 1):
        return lax.psum(value, RING)
    steps = [1] + [cols << k for k in range((n // cols).bit_length() - 1)] + [2 << k for k in range(cols.bit_length() - 2)]
    for step in steps:
        value = value + permute(value, [(i, i ^ step) for i in range(n)])
    return value


def rank(bits, rows, order, first):
    count = 0
    for r in range(rows):
        named = lax.rem(lax.shift_right_logical(bits, r), 2)
        order[first + jnp.where(named > 0, jnp.minimum(count, CAP), CAP)] = r
        count = count + named


def clear(ref, count, value):
    for q in range(count):
        ref[q] = value


def copy_in(source, target, sem):
    copy = pltpu.make_async_copy(source, target, sem)
    copy.start()
    return copy


def spread_kernel(total_rows, cols_hbm, keep_hbm, flag, x_hbm, own, outer, inner, table, meta,
                  cols, keep, x, slots_of, order, sem):
    rows, slots = cols.shape
    block = x.shape[-1]
    wide = 3 * rows
    across = rows + 2 * CAP
    lists = [copy_in(cols_hbm, cols, sem.at[0]), copy_in(keep_hbm, keep, sem.at[1])]
    blocks = [copy_in(x_hbm.at[i], x.at[i], sem.at[2 + i]) for i in range(rows)]
    clear(slots_of, rows * wide, -1)
    for copy in lists:
        copy.wait()
    base = cols[0, 0]
    odd = lax.rem(lax.div(base, rows), 2)
    ahead = jnp.where(odd == 1, 0, rows)
    behind = jnp.where(odd == 1, 2 * rows, rows) - (total_rows - rows)
    bits = 0
    for i in range(rows):
        for s in range(slots):
            rel = cols[i, s] - base
            rel = jnp.where(rel < 0, rel + total_rows, rel)
            rel = rel + jnp.where(rel >= 2 * rows, behind, jnp.where(rel >= rows, ahead, 0))
            slots_of[i * wide + rel] = 2 * s + keep[i, s]
            bits = bits | lax.shift_left(1, rel)
    rank(lax.shift_right_logical(bits, rows), rows, order, 0)
    rank(lax.shift_right_logical(bits, 2 * rows), rows, order, CAP + 1)
    for c in range(2 * CAP):
        meta[c] = order[c + c // CAP]
    meta[2 * CAP] = base
    meta[2 * CAP + 1] = flag[0]
    for i in range(rows):
        span = pl.ds(i * block, block)
        blocks[i].wait()
        for k in range(rows):
            code = slots_of[i * wide + k]
            table[i * across + k] = code
            own[span, pl.ds(k * block, block)] = x[i, lax.shift_right_logical(code, 1)]
        for first, target, start, shift in ((0, outer, rows, 0), (CAP + 1, inner, 2 * rows, CAP)):
            for c in range(CAP):
                code = slots_of[i * wide + start + order[first + c]]
                table[i * across + rows + shift + c] = code
                value = x[i, lax.shift_right_logical(jnp.maximum(code, 0), 1)]
                target[span, pl.ds(c * block, block)] = jnp.where(code >= 0, value, jnp.zeros_like(value))


def pack_kernel(meta, cols_outer, own, outer, far_out, near_out, asked, order, stage, sem):
    rows, slots = cols_outer.shape
    block = own.shape[0] // rows
    half = CAP * block
    base = meta[2 * CAP]
    bits = 0
    for i in range(rows):
        for s in range(slots):
            rel = cols_outer[i, s] - base
            bits = bits | lax.shift_left(1, jnp.where((rel >= 0) & (rel < rows), rel, rows))
    rank(bits, rows, order, 0)
    copies = []
    for a in range(CAP):
        asked[a] = order[a]
        span = pl.ds(a * block, block)
        row = pl.ds(pl.multiple_of(order[a] * block, block), block)
        stage[span, 0:half] = outer[row, :]
        for b in range(CAP):
            column = pl.ds(pl.multiple_of(order[b] * block, block), block)
            stage[span, pl.ds(half + b * block, block)] = own[row, column]
        copies.append(copy_in(stage.at[span, 0:half], far_out.at[span, :], sem.at[0]))
        copies.append(copy_in(stage.at[span, half:2 * half], near_out.at[span, :], sem.at[1]))
    count = 0
    for r in range(rows):
        left = 1 - lax.rem(lax.shift_right_logical(bits, r), 2)
        asked[CAP + jnp.where(left > 0, jnp.minimum(count, rows - CAP), rows - CAP)] = r
        count = count + left
    for copy in copies:
        copy.wait()


def signs(meta):
    on = meta[2 * CAP + 1] == 1
    return jnp.where(on, 0.0, 2.0), jnp.where(on, 1.0, -1.0)


def diagonal(square):
    n = square.shape[-1]
    on = lax.broadcasted_iota(jnp.int32, (n, n), 0) == lax.broadcasted_iota(jnp.int32, (n, n), 1)
    return jnp.sum(jnp.where(on, square, 0.0))


def kept(code):
    return lax.rem(jnp.maximum(code, 0), 2).astype(jnp.float32)


def give(stage, out, i, code, sem):
    copy = pltpu.make_async_copy(stage, out.at[i, lax.shift_right_logical(jnp.maximum(code, 0), 1)], sem)

    @pl.when(code >= 0)
    def _():
        copy.start()

    def wait():
        @pl.when(code >= 0)
        def _():
            copy.wait()
    return wait


def near_kernel(meta, own, outer, base_near):
    twice, sign = signs(meta)
    base_near[...] = (twice * outer[...].astype(jnp.float32)
                      + sign * jnp.dot(own[...], outer[...], preferred_element_type=jnp.float32))


def own_kernel(table, meta, asked, meta_inner, own, outer, inner, got_own_hbm, got_far_hbm, out, base_far, turned, trace,
               got_own, got_far, square, side, stage, sem, sem_base, sem_got):
    rows = stage.shape[0]
    block = own.shape[0] // rows
    across = rows + 2 * CAP
    half = CAP * block
    twice, sign = signs(meta)
    left = own[...]
    arrive = []
    for c in range(CAP):
        row = pl.ds(pl.multiple_of(meta[CAP + c] * block, block), block)
        span = pl.ds(c * block, block)
        arrive.append(copy_in(got_far_hbm.at[row, :], got_far.at[span, :], sem_got))
        for d in range(CAP):
            column = pl.ds(pl.multiple_of(meta[CAP + d] * block, block), block)
            arrive.append(copy_in(got_own_hbm.at[row, column], got_own.at[span, pl.ds(d * block, block)], sem_got))
    square[...] = twice * left.astype(jnp.float32) + sign * jnp.dot(left, left, preferred_element_type=jnp.float32)
    for r in range(CAP):
        for c in range(CAP):
            value = outer[pl.ds(pl.multiple_of(asked[c] * block, block), block), pl.ds(r * block, block)]
            turned[pl.ds(r * block, block), pl.ds(c * block, block)] = value.astype(jnp.float32).T.astype(turned.dtype)
    copies = []
    for copy in arrive:
        copy.wait()
    part = sign * jnp.dot(inner[...], got_far[...], preferred_element_type=jnp.float32)
    for c in range(CAP):
        place = pl.ds(pl.multiple_of(meta_inner[CAP + c] * block, block), block)
        square[:, place] = square[:, place] + part[:, c * block:(c + 1) * block]
    for c in range(CAP):
        place = pl.ds(pl.multiple_of(asked[c] * block, block), block)
        copies.append(copy_in(square.at[:, place], base_far.at[:, pl.ds(c * block, block)], sem_base))
    total = jnp.zeros((block, block), jnp.float32)
    for i in range(rows):
        span = pl.ds(i * block, block)
        total = total + kept(table[i * across + i]) * square[span, span]
    trace[0] = diagonal(total)
    side[...] = (twice * inner[...].astype(jnp.float32)
                 + sign * (jnp.dot(left, inner[...], preferred_element_type=jnp.float32)
                           + jnp.dot(inner[...], got_own[...], preferred_element_type=jnp.float32)))
    waits = []
    for i in range(rows):
        span = pl.ds(i * block, block)
        for e in range(rows - CAP):
            k = asked[CAP + e]
            code = table[i * across + k]
            value = square[span, pl.ds(pl.multiple_of(k * block, block), block)]
            stage[i, CAP + e] = (kept(code) * value).astype(stage.dtype)
            waits.append(give(stage.at[i, CAP + e], out, i, code, sem))
        for c in range(CAP):
            code = table[i * across + rows + CAP + c]
            stage[i, c] = (kept(code) * side[span, pl.ds(c * block, block)]).astype(stage.dtype)
            waits.append(give(stage.at[i, c], out, i, code, sem))
    for wait in waits:
        wait()
    for copy in copies:
        copy.wait()


def trace_kernel(rows, table, meta, asked, turned, far_hbm, trace_own, trace, far, sem):
    block = turned.shape[0] // CAP
    across = rows + 2 * CAP
    copy_in(far_hbm, far, sem).wait()
    total = jnp.zeros((8, block), jnp.float32)
    for c in range(CAP):
        mine = asked[c]
        column = pl.ds(c * block, block)
        part = far[:, column].astype(jnp.float32) * turned[:, column].astype(jnp.float32)
        total = total + kept(table[mine * across + mine]) * jnp.sum(part.reshape(CAP * block // 8, 8, block), axis=0)
    value = (trace_own[0] + signs(meta)[1] * jnp.sum(total)) * (1.0 / total_count(rows, block))
    trace[...] = jnp.full(trace.shape, value, jnp.float32)


def total_count(rows, block):
    return rows * block * lax.axis_size(RING)


def last_kernel(table, meta, asked, outer, base_far, base_near, far, near, _, out,
                got, base, stage, sem, sem_base, sem_got):
    rows = stage.shape[0]
    block = outer.shape[0] // rows
    across = rows + 2 * CAP
    half = CAP * block
    arrive = [copy_in(source, got.at[t], sem_got) for t, source in enumerate((far, near))]
    copies = [copy_in(source, base.at[t], sem_base.at[t]) for t, source in enumerate((base_far, base_near))]
    sign = signs(meta)[1].astype(outer.dtype)
    waits = []
    for copy in arrive:
        copy.wait()
    chunk = rows // 2
    for t in range(2):
        right = got[t] * sign
        copies[t].wait()
        for first in range(0, rows, chunk):
            tall = pl.ds(first * block, chunk * block)
            value = base[t, tall, :] + jnp.dot(outer[tall, :], right, preferred_element_type=jnp.float32)
            codes = {}
            for i in range(first, first + chunk):
                for c in range(CAP):
                    code = table[i * across + (asked[c] if t == 0 else rows + c)]
                    codes[i, c] = code
                    low = (i - first) * block
                    stage[i, t * CAP + c] = (kept(code) * value[low:low + block, c * block:(c + 1) * block]).astype(stage.dtype)
            for (i, c), code in codes.items():
                waits.append(give(stage.at[i, t * CAP + c], out, i, code, sem))
    for wait in waits:
        wait()


def body(x, cols, keep, flag):
    rows, slots, block = x.shape[0], x.shape[1], x.shape[2]
    n = lax.axis_size(RING)
    total_rows = rows * n
    bf16, f32, i32 = x.dtype, jnp.float32, jnp.int32
    wide, narrow, across = rows * block, CAP * block, rows + 2 * CAP
    dma = pltpu.SemaphoreType.DMA

    def ints(*shape):
        return pltpu.SMEM(shape, i32)

    def call(kernel, outs, in_specs, scratch, mib, aliases=None, first=None):
        def run(*refs):
            kernel(*(() if first is None else (first,)), *refs)
        return pl.pallas_call(
            run, out_shape=[(pltpu.HBM if len(o) > 3 else jax.ShapeDtypeStruct)(*o[:2]) for o in outs], in_specs=in_specs,
            out_specs=[o[2] for o in outs], scratch_shapes=scratch, name=kernel.__name__,
            input_output_aliases=aliases or {},
            cost_estimate=pl.CostEstimate(flops=1, bytes_accessed=1, transcendentals=0),
            compiler_params=pltpu.CompilerParams(vmem_limit_bytes=mib * MIB))

    inside = [(i, i ^ 1) for i in range(n)]
    upward = [(i, (i + 1) % n) for i in range(1, n, 2)]
    outside = upward + [(b, a) for a, b in upward]
    hbm = functools.partial(pltpu.with_memory_space_constraint, memory_space=pltpu.HBM)
    barrier = lax.optimization_barrier

    cols_outer = permute(cols, outside)
    own, outer, inner, table, meta = call(
        spread_kernel,
        [((wide, wide), bf16, VMEM), ((wide, narrow), bf16, VMEM), ((wide, narrow), bf16, VMEM),
         ((rows * across,), i32, SMEM), ((2 * CAP + 2,), i32, SMEM)],
        [HBM] * 2 + [SMEM, HBM], [ints(rows, slots), ints(rows, slots), pltpu.VMEM(x.shape, bf16), ints(rows * 3 * rows),
                    ints(2 * (CAP + 1)), dma((2 + rows,))], 16, first=total_rows)(hbm(cols), hbm(keep), flag, hbm(x))
    far_out, near_out, asked = call(
        pack_kernel,
        [((narrow, narrow), bf16, HBM), ((narrow, narrow), bf16, HBM), ((CAP + rows - CAP + 1,), i32, SMEM)],
        [SMEM] * 2 + [VMEM] * 2, [ints(CAP + 1), pltpu.VMEM((narrow, 2 * narrow), bf16), dma((2,))], 16,
    )(meta, cols_outer, own, outer)
    far = permute(far_out, outside)
    meta, asked = barrier((meta, asked))
    base_near, = call(near_kernel, [((wide, narrow), f32, VMEM)], [SMEM] + [VMEM] * 2, [], 12)(meta, own, outer)
    base_near, own_there, inner_there, meta_there = barrier((base_near, own, inner, meta))
    got_own, got_far, meta_inner = (permute(v, inside) for v in (own_there, inner_there, meta_there))
    out, base_far, turned, trace_own = call(
        own_kernel,
        [(x.shape, bf16, HBM), ((wide, narrow), f32, HBM, True), ((narrow, narrow), bf16, VMEM), ((1,), f32, SMEM)],
        [SMEM] * 4 + [VMEM] * 3 + [HBM] * 2,
        [pltpu.VMEM((narrow, narrow), bf16), pltpu.VMEM((narrow, narrow), bf16), pltpu.VMEM((wide, wide), f32),
         pltpu.VMEM((wide, narrow), f32), pltpu.VMEM((rows, rows, block, block), bf16), dma, dma, dma], 24,
    )(table, meta, asked, meta_inner, own, outer, inner, got_own, got_far)
    partial, = call(
        trace_kernel, [((8, block), f32, VMEM)], [SMEM] * 3 + [VMEM, HBM, SMEM],
        [pltpu.VMEM((narrow, narrow), bf16), dma], 12, first=rows)(table, meta, asked, turned, far, trace_own)
    near_out, partial = barrier((near_out, partial))
    near = permute(near_out, outside)
    total = ring_sum(partial)
    out, total = barrier((out, total))
    out, = call(
        last_kernel, [(x.shape, bf16, HBM)], [SMEM] * 3 + [VMEM] + [HBM] * 5,
        [pltpu.VMEM((2, narrow, narrow), bf16), pltpu.VMEM((2, wide, narrow), f32),
         pltpu.VMEM((rows, 2 * CAP, block, block), bf16), dma, dma((2,)), dma], 24, {8: 0},
    )(table, meta, asked, outer, hbm(base_far), base_near, far, near, out)
    return out, total[0, :1]


def solution(mesh):
    placed = (
        P(("groups", "row", "col"), None, None, None),
        P(("groups", "row", "col"), None),
        P(("groups", "row", "col"), None),
        P("groups"),
    )
    return jax.shard_map(
        body,
        mesh=mesh,
        in_specs=placed,
        out_specs=(P(("groups", "row", "col"), None, None, None), P("groups")),
        check_vma=False,
    )
```

time: 318 us -> 48.3 us (0.15)
  local copies, waits for them, and re-layouts: 122 us -> 0.51 us
  matrix products: 63.7 us -> 0 us
  other arithmetic: 49.3 us -> 0.01 us
  blocking collectives: 37.9 us -> 0 us
  Pallas kernels: 0 us -> 17.9 us
  loops' own time: 11.9 us -> 0 us
  between operations: 5.19 us -> 1.35 us
    dot_general x12 -> x0, matrix products: 63.7 us -> none  [the longest x6 34.1 us: square_row(): jnp.einsum('tsu,tubc->tbsc', selector, right_rows, preferred_element_type...]
    gather x20 -> x0, local copies, waits for them, and re-layouts: 49 us -> none  [the longest x6 36.5 us: square_row(): right_rows = jnp.take(source_vals, source_rows, axis=0)]
    dot_general x6 -> x0, local copies, waits for them, and re-layouts: 39.6 us -> none  [square_row(): product = jnp.dot(left_flat, stacked, preferred_element_type=jnp.float32)]
    psum x1 -> x0, blocking collectives: 37.9 us -> none  [body(): trace_total = lax.psum(trace_term, ('row', 'col'))]
    select_n x24 -> x0, other arithmetic: 37.4 us -> none  [the longest x12 30.5 us: square_row(): right_rows = jnp.take(source_vals, source_rows, axis=0)]
    while x6 -> x0, local copies, waits for them, and re-layouts: 27.1 us -> none
    pallas_call x0 -> x6, Pallas kernels: none -> 17.9 us  [the longest x1 6.87 us: body(): call(own_kernel, [(x.shape, bf16, HBM), ((wide, narrow), f32, HBM, True),...]
    another operation x1 -> x0, loops' own time: 11.9 us -> none  [body(): square = lax.map(square_row, row_ids)]
  transfers between devices with their start and end apart: 6 -> 10, of which waited for: 3 -> 6; matrix products, arithmetic and copies ran while one was open for 5% -> 1% of each run, Pallas kernels for 0% -> 20%
where the time goes in v2:
time: 48.3 us; the launch traced here: 48.1 us
  Pallas kernels  17.9 us (37%)
  waiting for transfers between devices  16.2 us (34%)
  starting transfers between devices  12.2 us (25%)
  between operations  1.35 us (3%)
  local copies, waits for them, and re-layouts  0.51 us (1%)
    ppermute x10, waiting for transfers between devices, permute(): return lax.ppermute(value, RING, pairs)  16.2 us
    ppermute x10, starting transfers between devices, permute(): return lax.ppermute(value, RING, pairs)  12.2 us
    pallas_call x1, Pallas kernels, body(): call(own_kernel, [(x.shape, bf16, HBM), ((wide, narrow), f32, HBM, True),...  6.87 us
    pallas_call x1, Pallas kernels, body(): call(last_kernel, [(x.shape, bf16, HBM)], [SMEM] * 3 + [VMEM] + [HBM] * 5...  3.94 us
    pallas_call x1, Pallas kernels, body(): call(spread_kernel, [((wide, wide), bf16, VMEM), ((wide, narrow), bf16, V...  2.55 us
    pallas_call x1, Pallas kernels, body(): call(pack_kernel, [((narrow, narrow), bf16, HBM), ((narrow, narrow), bf16...  1.75 us
    pallas_call x1, Pallas kernels, body(): call(trace_kernel, [((8, block), f32, VMEM)], [SMEM] * 3 + [VMEM, HBM, SM...  1.51 us
    pallas_call x1, Pallas kernels, body(): call(near_kernel, [((wide, narrow), f32, VMEM)], [SMEM] + [VMEM] * 2, [],...  1.31 us
  transfers between devices with their start and end apart: 10, of which 6 were waited for; matrix products, arithmetic and copies ran while one was open for 1% of the time, Pallas kernels for 20%

profile of v2, /device:TPU:0, one launch (start us, length us, event | category | flops | bytes accessed | tf_op | source)
XLA Modules:
  0.0 48.1 jit_solution(106868459155354079)
XLA Ops:
  0.6 5.5 %collective-permute-start = (s32[6,12]{1,0:T(8,128)}, s32[6,12]{1,0:T(8,128)S(1)}, u32[]{:S(2)}, u32[]{:S(2)}) collective-permute-start(s32[6,12]{1,0:T(8,128)} %refs_0_.1), channel_id=1, source_target_pairs={{1,2},{3,4},{5,6},{7,8},{9,10},{11,12},{13,14},{15,0},{2,1},{4,3},... | collective-permute-start | bytes 872 | tf_op jit(solution)/shard_map/ppermute | solution.py:19
  6.8 2.5 %spread_kernel.1 = (bf16[768,768]{1,0:T(8,128)(2,1)S(1)}, bf16[768,512]{1,0:T(8,128)(2,1)S(1)}, bf16[768,512]{1,0:T(8,128)(2,1)S(1)}, s32[84]{0:T(128)S(1)}, s32[10]{0:T(128)S(1)}) custom-call(s32[6,12]{1,0:T(8,128)} %refs_0_.1, s32[6,12]{1,0:T(8,128)} %refs_1_.1, s32[1]{0:T(128)S(6)} %copy.8.refs_2_, bf16[6,12,128,128]{3,2,1,0:T(8,128)(2,1)} %refs_3_.1), custom_call_target="tpu_custom_call" | custom-call | flops 1 | bytes 1 | tf_op jit(solution)/shard_map/spread_kernel/pallas_call | solution.py:297
  9.3 0.0 collective-permute-done.refs_1_
  9.3 1.7 %pack_kernel.1 = (bf16[512,512]{1,0:T(8,128)(2,1)S(1)}, bf16[512,512]{1,0:T(8,128)(2,1)S(1)}, s32[7]{0:T(128)S(1)}) custom-call(s32[10]{0:T(128)S(1)} %get-tuple-element.32.refs_0_.refs_1_, s32[6,12]{1,0:T(8,128)S(1)} %collective-permute-done.refs_1_, bf16[768,768]{1,0:T(8,128)(2,1)S(1)} %get-tuple-element.33.refs_2_.refs_1_.refs_4_, ...), custom_call_target="tpu_custom_call" | custom-call | flops 1 | bytes 1 | tf_op jit(solution)/shard_map/pack_kernel/pallas_call | solution.py:303
  11.1 1.3 %near_kernel.1.refs_5_ = f32[768,512]{1,0:T(8,128)S(1)} custom-call(s32[10]{0:T(128)S(1)} %get-tuple-element.32.refs_0_.refs_1_, bf16[768,768]{1,0:T(8,128)(2,1)S(1)} %get-tuple-element.33.refs_2_.refs_1_.refs_4_, bf16[768,512]{1,0:T(8,128)(2,1)S(1)} %get-tuple-element.27.refs_3_.refs_2_.refs_5_), custom_call_target="tpu_custom_call" | custom-call | flops 1 | bytes 1 | tf_op jit(solution)/shard_map/near_kernel/pallas_call | solution.py:310
  12.4 0.1 collective-permute-start.2
  12.5 0.5 %collective-permute-start.3 = (bf16[768,512]{1,0:T(8,128)(2,1)S(1)}, bf16[768,512]{1,0:T(8,128)(2,1)S(1)}, u32[]{:S(2)}, u32[]{:S(2)}) collective-permute-start(bf16[768,512]{1,0:T(8,128)(2,1)S(1)} %get-tuple-element.34.refs_6_), channel_id=1, source_target_pairs={{0,1},{1,0},{2,3},{3,2},{4,5},{5,4},{6,7},{7,6},{8,9},{9,8},{10,11... | collective-permute-start | bytes 2359304 | tf_op jit(solution)/shard_map/ppermute | solution.py:19
  13.0 2.7 %collective-permute-start.4 = (bf16[512,512]{1,0:T(8,128)(2,1)S(1)}, bf16[512,512]{1,0:T(8,128)(2,1)S(1)}, u32[]{:S(2)}, u32[]{:S(2)}) collective-permute-start(bf16[512,512]{1,0:T(8,128)(2,1)S(1)} %get-tuple-element.37), channel_id=1, source_target_pairs={{1,2},{3,4},{5,6},{7,8},{9,10},{11,12},{13,14},{15,0},{2,1},{4,3},... | collective-permute-start | bytes 1572872 | tf_op jit(solution)/shard_map/ppermute | solution.py:19
  15.7 0.0 collective-permute-start.1
  15.7 1.1 %collective-permute-done.1.refs_3_ = s32[10]{0:T(128)S(1)} collective-permute-done((s32[10]{0:T(128)S(1)}, s32[10]{0:T(128)S(1)}, u32[]{:S(2)}, u32[]{:S(2)}) %collective-permute-start.1) | collective-permute-done | bytes 72 | tf_op jit(solution)/shard_map/ppermute | solution.py:19
  16.8 0.0 collective-permute-done.3.refs_8_
  16.8 0.0 collective-permute-done.2.refs_7_
  16.8 6.9 %own_kernel.1 = (bf16[6,12,128,128]{3,2,1,0:T(8,128)(2,1)}, f32[768,512]{1,0:T(8,128)}, bf16[512,512]{1,0:T(8,128)(2,1)S(1)}, f32[1]{0:T(128)}) custom-call(s32[84]{0:T(128)S(1)} %get-tuple-element.24.refs_0_, s32[10]{0:T(128)S(1)} %get-tuple-element.32.refs_0_.refs_1_, s32[7]{0:T(128)S(1)} %get-tuple-element.30.refs_2_, ...), custom_call_target="tpu_custom_call" | custom-call | flops 1 | bytes 1 | tf_op jit(solution)/shard_map/own_kernel/pallas_call | solution.py:313
  23.7 0.7 %collective-permute-done.4.refs_4_.refs_6_ = bf16[512,512]{1,0:T(8,128)(2,1)S(1)} collective-permute-done((bf16[512,512]{1,0:T(8,128)(2,1)S(1)}, bf16[512,512]{1,0:T(8,128)(2,1)S(1)}, u32[]{:S(2)}, u32[]{:S(2)}) %collective-permute-start.4) | collective-permute-done | bytes 524320 | tf_op jit(solution)/shard_map/ppermute | solution.py:19
  24.4 1.5 %trace_kernel.1 = f32[8,128]{1,0:T(8,128)S(1)} custom-call(s32[84]{0:T(128)S(1)} %get-tuple-element.24.refs_0_, s32[10]{0:T(128)S(1)} %get-tuple-element.32.refs_0_.refs_1_, s32[7]{0:T(128)S(1)} %get-tuple-element.30.refs_2_, bf16[512,512]{1,0:T(8,128)(2,1)S(1)} %get-tuple-element.39.refs_3_, bf16[512,512]{1,0:T(8,128)(2,1)S(1)} %collective-permute-done.4.refs_4_.refs_6_, ...), custom_call_target="tpu_custom_call" | custom-call | flops 1 | bytes 1 | tf_op jit(solution)/shard_map/trace_kernel/pallas_call | solution.py:320
  25.9 2.8 %collective-permute-start.5 = (bf16[512,512]{1,0:T(8,128)(2,1)S(1)}, bf16[512,512]{1,0:T(8,128)(2,1)S(1)}, u32[]{:S(2)}, u32[]{:S(2)}) collective-permute-start(bf16[512,512]{1,0:T(8,128)(2,1)S(1)} %get-tuple-element.41), channel_id=1, source_target_pairs={{1,2},{3,4},{5,6},{7,8},{9,10},{11,12},{13,14},{15,0},{2,1},{4,3},... | collective-permute-start | bytes 1572872 | tf_op jit(solution)/shard_map/ppermute | solution.py:19
  28.7 0.3 collective-permute-start.6
  28.9 0.9 %collective-permute-done.6 = f32[8,128]{1,0:T(8,128)S(1)} collective-permute-done((f32[8,128]{1,0:T(8,128)S(1)}, f32[8,128]{1,0:T(8,128)S(1)}, u32[]{:S(2)}, u32[]{:S(2)}) %collective-permute-start.6) | collective-permute-done | bytes 4128 | tf_op jit(solution)/shard_map/ppermute | solution.py:19
  29.9 0.2 collective-permute-start.7
  30.1 5.5 %collective-permute-done.7 = f32[8,128]{1,0:T(8,128)S(1)} collective-permute-done((f32[8,128]{1,0:T(8,128)S(1)}, f32[8,128]{1,0:T(8,128)S(1)}, u32[]{:S(2)}, u32[]{:S(2)}) %collective-permute-start.7) | collective-permute-done | bytes 4128 | tf_op jit(solution)/shard_map/ppermute | solution.py:19
  35.5 0.0 collective-permute-start.8
  35.5 4.5 %collective-permute-done.8 = f32[8,128]{1,0:T(8,128)S(1)} collective-permute-done((f32[8,128]{1,0:T(8,128)S(1)}, f32[8,128]{1,0:T(8,128)S(1)}, u32[]{:S(2)}, u32[]{:S(2)}) %collective-permute-start.8) | collective-permute-done | bytes 4128 | tf_op jit(solution)/shard_map/ppermute | solution.py:19
  40.0 0.1 collective-permute-start.9
  40.2 3.5 %collective-permute-done.9 = f32[8,128]{1,0:T(8,128)S(1)} collective-permute-done((f32[8,128]{1,0:T(8,128)S(1)}, f32[8,128]{1,0:T(8,128)S(1)}, u32[]{:S(2)}, u32[]{:S(2)}) %collective-permute-start.9) | collective-permute-done | bytes 4128 | tf_op jit(solution)/shard_map/ppermute | solution.py:19
  43.7 0.5 %slice.3 = f32[1,1]{1,0:T(1,128)} slice(f32[8,128]{1,0:T(8,128)S(1)} %add.15), slice={[0:1], [0:1]} | slice | bytes 8 | tf_op jit(solution)/shard_map/slice | solution.py:332
  44.2 0.0 collective-permute-done.5.refs_7_
  44.2 3.9 %last_kernel.1 = bf16[6,12,128,128]{3,2,1,0:T(8,128)(2,1)} custom-call(s32[84]{0:T(128)S(1)} %get-tuple-element.24.refs_0_, s32[10]{0:T(128)S(1)} %get-tuple-element.32.refs_0_.refs_1_, s32[7]{0:T(128)S(1)} %get-tuple-element.30.refs_2_, bf16[768,512]{1,0:T(8,128)(2,1)S(1)} %get-tuple-element.27.refs_3_.refs_2_.refs_5_, ...), custom_call_target="tpu_custom_call", output_to_operand_aliasing={{}: (8, {})} | custom-call | flops 1 | bytes 1 | tf_op jit(solution)/shard_map/last_kernel/pallas_call | solution.py:327
  (4 shorter events, 0.0 us)
Async XLA Ops:
  0.6 8.7 %collective-permute-start = (s32[6,12]{1,0:T(8,128)}, s32[6,12]{1,0:T(8,128)S(1)}, u32[]{:S(2)}, u32[]{:S(2)}) collective-permute-start(s32[6,12]{1,0:T(8,128)} %refs_0_.1), channel_id=1, source_target_pairs={{1,2},{3,4},{5,6},{7,8},{9,10},{11,12},{13,14},{15,0},{2,1},{4,3},... | collective-permute-start | bytes 872 | tf_op jit(solution)/shard_map/ppermute | solution.py:19
  12.4 4.4 %collective-permute-start.2 = (bf16[768,768]{1,0:T(8,128)(2,1)S(1)}, bf16[768,768]{1,0:T(8,128)(2,1)S(1)}, u32[]{:S(2)}, u32[]{:S(2)}) collective-permute-start(bf16[768,768]{1,0:T(8,128)(2,1)S(1)} %get-tuple-element.33.refs_2_.refs_1_.refs_4_), channel_id=1, source_target_pairs={{0,1},{1,0},{2,3},{3,2},{4,5},{5,4},{6,7},{7,6},{8,9},{9,8},{10,11... | collective-permute-start | bytes 3538952 | tf_op jit(solution)/shard_map/ppermute | solution.py:19
  12.5 4.3 %collective-permute-start.3 = (bf16[768,512]{1,0:T(8,128)(2,1)S(1)}, bf16[768,512]{1,0:T(8,128)(2,1)S(1)}, u32[]{:S(2)}, u32[]{:S(2)}) collective-permute-start(bf16[768,512]{1,0:T(8,128)(2,1)S(1)} %get-tuple-element.34.refs_6_), channel_id=1, source_target_pairs={{0,1},{1,0},{2,3},{3,2},{4,5},{5,4},{6,7},{7,6},{8,9},{9,8},{10,11... | collective-permute-start | bytes 2359304 | tf_op jit(solution)/shard_map/ppermute | solution.py:19
  13.0 11.4 %collective-permute-start.4 = (bf16[512,512]{1,0:T(8,128)(2,1)S(1)}, bf16[512,512]{1,0:T(8,128)(2,1)S(1)}, u32[]{:S(2)}, u32[]{:S(2)}) collective-permute-start(bf16[512,512]{1,0:T(8,128)(2,1)S(1)} %get-tuple-element.37), channel_id=1, source_target_pairs={{1,2},{3,4},{5,6},{7,8},{9,10},{11,12},{13,14},{15,0},{2,1},{4,3},... | collective-permute-start | bytes 1572872 | tf_op jit(solution)/shard_map/ppermute | solution.py:19
  15.7 1.1 %collective-permute-start.1 = (s32[10]{0:T(128)S(1)}, s32[10]{0:T(128)S(1)}, u32[]{:S(2)}, u32[]{:S(2)}) collective-permute-start(s32[10]{0:T(128)S(1)} %get-tuple-element.32.refs_0_.refs_1_), channel_id=1, source_target_pairs={{0,1},{1,0},{2,3},{3,2},{4,5},{5,4},{6,7},{7,6},{8,9},{9,8},{10,11... | collective-permute-start | bytes 128 | tf_op jit(solution)/shard_map/ppermute | solution.py:19
  25.9 18.3 %collective-permute-start.5 = (bf16[512,512]{1,0:T(8,128)(2,1)S(1)}, bf16[512,512]{1,0:T(8,128)(2,1)S(1)}, u32[]{:S(2)}, u32[]{:S(2)}) collective-permute-start(bf16[512,512]{1,0:T(8,128)(2,1)S(1)} %get-tuple-element.41), channel_id=1, source_target_pairs={{1,2},{3,4},{5,6},{7,8},{9,10},{11,12},{13,14},{15,0},{2,1},{4,3},... | collective-permute-start | bytes 1572872 | tf_op jit(solution)/shard_map/ppermute | solution.py:19
  28.7 1.2 %collective-permute-start.6 = (f32[8,128]{1,0:T(8,128)S(1)}, f32[8,128]{1,0:T(8,128)S(1)}, u32[]{:S(2)}, u32[]{:S(2)}) collective-permute-start(f32[8,128]{1,0:T(8,128)S(1)} %trace_kernel.1), channel_id=1, source_target_pairs={{0,1},{1,0},{2,3},{3,2},{4,5},{5,4},{6,7},{7,6},{8,9},{9,8},{10,11... | collective-permute-start | bytes 12296 | tf_op jit(solution)/shard_map/ppermute | solution.py:19
  29.9 5.7 %collective-permute-start.7 = (f32[8,128]{1,0:T(8,128)S(1)}, f32[8,128]{1,0:T(8,128)S(1)}, u32[]{:S(2)}, u32[]{:S(2)}) collective-permute-start(f32[8,128]{1,0:T(8,128)S(1)} %add.12), channel_id=1, source_target_pairs={{0,4},{1,5},{2,6},{3,7},{4,0},{5,1},{6,2},{7,3},{8,12},{9,13},{10,... | collective-permute-start | bytes 12296 | tf_op jit(solution)/shard_map/ppermute | solution.py:19
  35.5 4.5 %collective-permute-start.8 = (f32[8,128]{1,0:T(8,128)S(1)}, f32[8,128]{1,0:T(8,128)S(1)}, u32[]{:S(2)}, u32[]{:S(2)}) collective-permute-start(f32[8,128]{1,0:T(8,128)S(1)} %add.13), channel_id=1, source_target_pairs={{0,8},{1,9},{2,10},{3,11},{4,12},{5,13},{6,14},{7,15},{8,0},{9,1},... | collective-permute-start | bytes 12296 | tf_op jit(solution)/shard_map/ppermute | solution.py:19
  40.0 3.6 %collective-permute-start.9 = (f32[8,128]{1,0:T(8,128)S(1)}, f32[8,128]{1,0:T(8,128)S(1)}, u32[]{:S(2)}, u32[]{:S(2)}) collective-permute-start(f32[8,128]{1,0:T(8,128)S(1)} %add.14), channel_id=1, source_target_pairs={{0,2},{1,3},{2,0},{3,1},{4,6},{5,7},{6,4},{7,5},{8,10},{9,11},{10,... | collective-permute-start | bytes 12296 | tf_op jit(solution)/shard_map/ppermute | solution.py:19

commit v3 on v2

--- a/solution.py
+++ b/solution.py
@@ -19,14 +19,15 @@
     return lax.ppermute(value, RING, pairs)
 
 
-def ring_sum(value):
+def ring_steps():
     n, cols = lax.axis_size(RING), lax.axis_size("col")
-    if n & (n - 1) or cols & (cols - 1):
-        return lax.psum(value, RING)
-    steps = [1] + [cols << k for k in range((n // cols).bit_length() - 1)] + [2 << k for k in range(cols.bit_length() - 2)]
-    for step in steps:
-        value = value + permute(value, [(i, i ^ step) for i in range(n)])
-    return value
+    if n & (n - 1) or cols & (cols - 1) or cols < 4:
+        return None
+    return [1] + [cols << k for k in range((n // cols).bit_length() - 1)] + [2 << k for k in range(cols.bit_length() - 2)]
+
+
+def partner(value, step):
+    return permute(value, [(i, i ^ step) for i in range(lax.axis_size(RING))])
 
 
 def rank(bits, rows, order, first):
@@ -92,10 +93,9 @@
                 target[span, pl.ds(c * block, block)] = jnp.where(code >= 0, value, jnp.zeros_like(value))
 
 
-def pack_kernel(meta, cols_outer, own, outer, far_out, near_out, asked, order, stage, sem):
+def pack_kernel(meta, cols_outer, own, outer, far_out, near_out, asked, order):
     rows, slots = cols_outer.shape
     block = own.shape[0] // rows
-    half = CAP * block
     base = meta[2 * CAP]
     bits = 0
     for i in range(rows):
@@ -103,24 +103,19 @@
             rel = cols_outer[i, s] - base
             bits = bits | lax.shift_left(1, jnp.where((rel >= 0) & (rel < rows), rel, rows))
     rank(bits, rows, order, 0)
-    copies = []
     for a in range(CAP):
         asked[a] = order[a]
         span = pl.ds(a * block, block)
         row = pl.ds(pl.multiple_of(order[a] * block, block), block)
-        stage[span, 0:half] = outer[row, :]
+        far_out[span, :] = outer[row, :]
         for b in range(CAP):
             column = pl.ds(pl.multiple_of(order[b] * block, block), block)
-            stage[span, pl.ds(half + b * block, block)] = own[row, column]
-        copies.append(copy_in(stage.at[span, 0:half], far_out.at[span, :], sem.at[0]))
-        copies.append(copy_in(stage.at[span, half:2 * half], near_out.at[span, :], sem.at[1]))
+            near_out[span, pl.ds(b * block, block)] = own[row, column]
     count = 0
     for r in range(rows):
         left = 1 - lax.rem(lax.shift_right_logical(bits, r), 2)
         asked[CAP + jnp.where(left > 0, jnp.minimum(count, rows - CAP), rows - CAP)] = r
         count = count + left
-    for copy in copies:
-        copy.wait()
 
 
 def signs(meta):
@@ -152,39 +147,56 @@
     return wait
 
 
-def near_kernel(meta, own, outer, base_near):
-    twice, sign = signs(meta)
-    base_near[...] = (twice * outer[...].astype(jnp.float32)
-                      + sign * jnp.dot(own[...], outer[...], preferred_element_type=jnp.float32))
-
-
-def own_kernel(table, meta, asked, meta_inner, own, outer, inner, got_own_hbm, got_far_hbm, out, base_far, turned, trace,
-               got_own, got_far, square, side, stage, sem, sem_base, sem_got):
-    rows = stage.shape[0]
+def own_kernel(table, meta, asked, cols_inner, own, outer, inner, x_inner, out, base_far, base_near, turned, trace,
+               got_own, got_far, square, side, stage, slots_of, order, sem, sem_base, sem_got):
+    rows, slots = cols_inner.shape
     block = own.shape[0] // rows
     across = rows + 2 * CAP
-    half = CAP * block
     twice, sign = signs(meta)
     left = own[...]
+    left_signed = left * sign.astype(left.dtype)
+    inner_signed = inner[...] * sign.astype(left.dtype)
+    wide = 2 * rows + 1
+    clear(slots_of, rows * wide, -1)
+    mine, theirs = meta[2 * CAP], cols_inner[0, 0]
+    bits = 0
+    for i in range(rows):
+        for s in range(slots):
+            near = cols_inner[i, s] - theirs
+            far = cols_inner[i, s] - mine
+            far = jnp.where((far >= 0) & (far < rows), far, rows)
+            bits = bits | lax.shift_left(1, far)
+            slots_of[i * wide + jnp.where((near >= 0) & (near < rows), near, rows + far)] = s
+    rank(bits, rows, order, 0)
     arrive = []
-    for c in range(CAP):
-        row = pl.ds(pl.multiple_of(meta[CAP + c] * block, block), block)
-        span = pl.ds(c * block, block)
-        arrive.append(copy_in(got_far_hbm.at[row, :], got_far.at[span, :], sem_got))
-        for d in range(CAP):
-            column = pl.ds(pl.multiple_of(meta[CAP + d] * block, block), block)
-            arrive.append(copy_in(got_own_hbm.at[row, column], got_own.at[span, pl.ds(d * block, block)], sem_got))
-    square[...] = twice * left.astype(jnp.float32) + sign * jnp.dot(left, left, preferred_element_type=jnp.float32)
+    for r in range(CAP):
+        row = meta[CAP + r]
+        span = pl.ds(r * block, block)
+        for c in range(CAP):
+            place = pl.ds(c * block, block)
+            slot = slots_of[row * wide + meta[CAP + c]]
+            arrive.append(copy_in(x_inner.at[row, jnp.maximum(slot, 0)], got_own.at[span, place], sem_got))
+            slot = slots_of[row * wide + rows + order[c]]
+            far_slot = jnp.maximum(slot, 0)
+            arrive.append(copy_in(x_inner.at[row, far_slot], got_far.at[span, place], sem_got))
+    base_near[...] = (twice * outer[...].astype(jnp.float32)
+                      + jnp.dot(left_signed, outer[...], preferred_element_type=jnp.float32))
+    square[...] = twice * left.astype(jnp.float32) + jnp.dot(left_signed, left, preferred_element_type=jnp.float32)
     for r in range(CAP):
         for c in range(CAP):
             value = outer[pl.ds(pl.multiple_of(asked[c] * block, block), block), pl.ds(r * block, block)]
-            turned[pl.ds(r * block, block), pl.ds(c * block, block)] = value.astype(jnp.float32).T.astype(turned.dtype)
+            turned[pl.ds(r * block, block), pl.ds(c * block, block)] = value.T
     copies = []
     for copy in arrive:
         copy.wait()
-    part = sign * jnp.dot(inner[...], got_far[...], preferred_element_type=jnp.float32)
+    for r in range(CAP):
+        for c in range(CAP):
+            @pl.when(slots_of[meta[CAP + r] * wide + rows + order[c]] < 0)
+            def _():
+                got_far[pl.ds(r * block, block), pl.ds(c * block, block)] = jnp.zeros((block, block), got_far.dtype)
+    part = jnp.dot(inner_signed, got_far[...], preferred_element_type=jnp.float32)
     for c in range(CAP):
-        place = pl.ds(pl.multiple_of(meta_inner[CAP + c] * block, block), block)
+        place = pl.ds(pl.multiple_of(order[c] * block, block), block)
         square[:, place] = square[:, place] + part[:, c * block:(c + 1) * block]
     for c in range(CAP):
         place = pl.ds(pl.multiple_of(asked[c] * block, block), block)
@@ -194,9 +206,9 @@
         span = pl.ds(i * block, block)
         total = total + kept(table[i * across + i]) * square[span, span]
     trace[0] = diagonal(total)
-    side[...] = (twice * inner[...].astype(jnp.float32)
-                 + sign * (jnp.dot(left, inner[...], preferred_element_type=jnp.float32)
-                           + jnp.dot(inner[...], got_own[...], preferred_element_type=jnp.float32)))
+    side[...] = twice * inner[...].astype(jnp.float32) + jnp.dot(
+        jnp.concatenate([left_signed, inner_signed], axis=1), jnp.concatenate([inner[...], got_own[...]], axis=0),
+        preferred_element_type=jnp.float32)
     waits = []
     for i in range(rows):
         span = pl.ds(i * block, block)
@@ -234,36 +246,38 @@
     return rows * block * lax.axis_size(RING)
 
 
-def last_kernel(table, meta, asked, outer, base_far, base_near, far, near, _, out,
-                got, base, stage, sem, sem_base, sem_got):
-    rows = stage.shape[0]
+def finish_half(near, rows, table, meta, asked, outer, base_hbm, got_hbm, out, got, base, stage, sem, sem_base, sem_got):
     block = outer.shape[0] // rows
     across = rows + 2 * CAP
-    half = CAP * block
-    arrive = [copy_in(source, got.at[t], sem_got) for t, source in enumerate((far, near))]
-    copies = [copy_in(source, base.at[t], sem_base.at[t]) for t, source in enumerate((base_far, base_near))]
-    sign = signs(meta)[1].astype(outer.dtype)
+    arrive = copy_in(got_hbm, got, sem_got)
+    copy = copy_in(base_hbm, base, sem_base)
+    arrive.wait()
+    right = got[...] * signs(meta)[1].astype(got.dtype)
+    copy.wait()
     waits = []
-    for copy in arrive:
-        copy.wait()
     chunk = rows // 2
-    for t in range(2):
-        right = got[t] * sign
-        copies[t].wait()
-        for first in range(0, rows, chunk):
-            tall = pl.ds(first * block, chunk * block)
-            value = base[t, tall, :] + jnp.dot(outer[tall, :], right, preferred_element_type=jnp.float32)
-            codes = {}
-            for i in range(first, first + chunk):
-                for c in range(CAP):
-                    code = table[i * across + (asked[c] if t == 0 else rows + c)]
-                    codes[i, c] = code
-                    low = (i - first) * block
-                    stage[i, t * CAP + c] = (kept(code) * value[low:low + block, c * block:(c + 1) * block]).astype(stage.dtype)
-            for (i, c), code in codes.items():
-                waits.append(give(stage.at[i, t * CAP + c], out, i, code, sem))
+    for first in range(0, rows, chunk):
+        tall = pl.ds(first * block, chunk * block)
+        value = base[tall, :] + jnp.dot(outer[tall, :], right, preferred_element_type=jnp.float32)
+        codes = {}
+        for i in range(first, first + chunk):
+            low = (i - first) * block
+            for c in range(CAP):
+                code = table[i * across + (rows + c if near else asked[c])]
+                codes[i, c] = code
+                stage[i, c] = (kept(code) * value[low:low + block, c * block:(c + 1) * block]).astype(stage.dtype)
+        for (i, c), code in codes.items():
+            waits.append(give(stage.at[i, c], out, i, code, sem))
     for wait in waits:
         wait()
+
+
+def far_kernel(rows, table, meta, asked, outer, base, far, _, out, *scratch):
+    finish_half(False, rows, table, meta, asked, outer, base, far, out, *scratch)
+
+
+def last_kernel(rows, table, meta, asked, outer, base, near, _, out, *scratch):
+    finish_half(True, rows, table, meta, asked, outer, base, near, out, *scratch)
 
 
 def body(x, cols, keep, flag):
@@ -293,6 +307,8 @@
     hbm = functools.partial(pltpu.with_memory_space_constraint, memory_space=pltpu.HBM)
     barrier = lax.optimization_barrier
 
+    x_inner = permute(x, inside)
+    cols_inner = permute(cols, inside)
     cols_outer = permute(cols, outside)
     own, outer, inner, table, meta = call(
         spread_kernel,
@@ -302,34 +318,46 @@
                     ints(2 * (CAP + 1)), dma((2 + rows,))], 16, first=total_rows)(hbm(cols), hbm(keep), flag, hbm(x))
     far_out, near_out, asked = call(
         pack_kernel,
-        [((narrow, narrow), bf16, HBM), ((narrow, narrow), bf16, HBM), ((CAP + rows - CAP + 1,), i32, SMEM)],
-        [SMEM] * 2 + [VMEM] * 2, [ints(CAP + 1), pltpu.VMEM((narrow, 2 * narrow), bf16), dma((2,))], 16,
+        [((narrow, narrow), bf16, VMEM), ((narrow, narrow), bf16, VMEM), ((CAP + rows - CAP + 1,), i32, SMEM)],
+        [SMEM] * 2 + [VMEM] * 2, [ints(CAP + 1)], 16,
     )(meta, cols_outer, own, outer)
     far = permute(far_out, outside)
-    meta, asked = barrier((meta, asked))
-    base_near, = call(near_kernel, [((wide, narrow), f32, VMEM)], [SMEM] + [VMEM] * 2, [], 12)(meta, own, outer)
-    base_near, own_there, inner_there, meta_there = barrier((base_near, own, inner, meta))
-    got_own, got_far, meta_inner = (permute(v, inside) for v in (own_there, inner_there, meta_there))
-    out, base_far, turned, trace_own = call(
+    out, base_far, base_near, turned, trace_own = call(
         own_kernel,
-        [(x.shape, bf16, HBM), ((wide, narrow), f32, HBM, True), ((narrow, narrow), bf16, VMEM), ((1,), f32, SMEM)],
-        [SMEM] * 4 + [VMEM] * 3 + [HBM] * 2,
+        [(x.shape, bf16, HBM), ((wide, narrow), f32, HBM, True), ((wide, narrow), f32, VMEM),
+         ((narrow, narrow), bf16, VMEM), ((1,), f32, SMEM)],
+        [SMEM] * 4 + [VMEM] * 3 + [HBM],
         [pltpu.VMEM((narrow, narrow), bf16), pltpu.VMEM((narrow, narrow), bf16), pltpu.VMEM((wide, wide), f32),
-         pltpu.VMEM((wide, narrow), f32), pltpu.VMEM((rows, rows, block, block), bf16), dma, dma, dma], 24,
-    )(table, meta, asked, meta_inner, own, outer, inner, got_own, got_far)
+         pltpu.VMEM((wide, narrow), f32), pltpu.VMEM((rows, rows, block, block), bf16), ints(rows * (2 * rows + 1)),
+         ints(CAP + 1), dma, dma, dma], 24)(table, meta, asked, cols_inner, own, outer, inner, x_inner)
     partial, = call(
         trace_kernel, [((8, block), f32, VMEM)], [SMEM] * 3 + [VMEM, HBM, SMEM],
         [pltpu.VMEM((narrow, narrow), bf16), dma], 12, first=rows)(table, meta, asked, turned, far, trace_own)
     near_out, partial = barrier((near_out, partial))
     near = permute(near_out, outside)
-    total = ring_sum(partial)
-    out, total = barrier((out, total))
-    out, = call(
-        last_kernel, [(x.shape, bf16, HBM)], [SMEM] * 3 + [VMEM] + [HBM] * 5,
-        [pltpu.VMEM((2, narrow, narrow), bf16), pltpu.VMEM((2, wide, narrow), f32),
-         pltpu.VMEM((rows, 2 * CAP, block, block), bf16), dma, dma((2,)), dma], 24, {8: 0},
-    )(table, meta, asked, outer, hbm(base_far), base_near, far, near, out)
-    return out, total[0, :1]
+    half_scratch = [pltpu.VMEM((narrow, narrow), bf16), pltpu.VMEM((wide, narrow), f32),
+                    pltpu.VMEM((rows, CAP, block, block), bf16), dma, dma, dma]
+
+    def half(kernel, base, got, out):
+        result, = call(
+            kernel, [(x.shape, bf16, HBM)], [SMEM] * 3 + [VMEM] + [HBM] * 3, half_scratch, 16, {6: 0}, first=rows,
+        )(table, meta, asked, outer, base, got, out)
+        return result
+
+    steps = ring_steps()
+    if steps is None:
+        total = lax.psum(partial, RING)
+        return half(last_kernel, base_near, near, half(far_kernel, hbm(base_far), far, out)), total[0, :1]
+    partial = partial + partner(partial, steps[0])
+    out, partial = barrier((out, partial))
+    out = half(far_kernel, hbm(base_far), far, out)
+    out, partial = barrier((out, partial))
+    for step in steps[1:-1]:
+        partial = partial + partner(partial, step)
+    ready, partial = barrier((out, partial))
+    out = half(last_kernel, base_near, near, ready)
+    other, out = barrier((partner(partial, steps[-1]), out))
+    return out, (partial + other)[0, :1]
 
 
 def solution(mesh):

time: 48.3 us -> 44.3 us (0.917)
  waiting for transfers between devices: 16.2 us -> 12 us
  Pallas kernels: 17.9 us -> 18.7 us
  starting transfers between devices: 12.2 us -> 11.5 us
    ppermute x10 -> x9, waiting for transfers between devices: 16.2 us -> 12 us  [permute(): return lax.ppermute(value, RING, pairs)]
    pallas_call x1, Pallas kernels: 6.87 us -> 7.78 us  [body(): call(own_kernel, [(x.shape, bf16, HBM), ((wide, narrow), f32, HBM, True),...]
    ppermute x10 -> x9, starting transfers between devices: 12.2 us -> 11.5 us  [permute(): return lax.ppermute(value, RING, pairs)]
  transfers between devices with their start and end apart: 10 -> 9, of which waited for: 6 -> 5; matrix products, arithmetic and copies ran while one was open for 1% -> 0% of each run, Pallas kernels for 20% -> 39%
where the time goes in v3:
time: 44.3 us; the launch traced here: 44.1 us
  Pallas kernels  18.7 us (42%)
  waiting for transfers between devices  12 us (27%)
  starting transfers between devices  11.5 us (26%)
  between operations  1.37 us (3%)
  local copies, waits for them, and re-layouts  0.52 us (1%)
    ppermute x9, waiting for transfers between devices, permute(): return lax.ppermute(value, RING, pairs)  12 us
    ppermute x9, starting transfers between devices, permute(): return lax.ppermute(value, RING, pairs)  11.5 us
    pallas_call x1, Pallas kernels, body(): call(own_kernel, [(x.shape, bf16, HBM), ((wide, narrow), f32, HBM, True),...  7.78 us
    pallas_call x2, Pallas kernels, half(): call(kernel, [(x.shape, bf16, HBM)], [SMEM] * 3 + [VMEM] + [HBM] * 3, hal...  5.36 us
    pallas_call x1, Pallas kernels, body(): call(spread_kernel, [((wide, wide), bf16, VMEM), ((wide, narrow), bf16, V...  2.55 us
    pallas_call x1, Pallas kernels, body(): call(trace_kernel, [((8, block), f32, VMEM)], [SMEM] * 3 + [VMEM, HBM, SM...  1.51 us
    pallas_call x1, Pallas kernels, body(): call(pack_kernel, [((narrow, narrow), bf16, VMEM), ((narrow, narrow), bf1...  1.5 us
  transfers between devices with their start and end apart: 9, of which 5 were waited for; matrix products, arithmetic and copies ran while one was open for 0% of the time, Pallas kernels for 39%

profile of v3, /device:TPU:0, one launch (start us, length us, event | category | flops | bytes accessed | tf_op | source)
XLA Modules:
  0.0 44.1 jit_solution(6393098150947113740)
XLA Ops:
  0.6 0.0 copy-start
  0.6 0.5 %collective-permute-start.2 = (bf16[6,12,128,128]{3,2,1,0:T(8,128)(2,1)}, bf16[6,12,128,128]{3,2,1,0:T(8,128)(2,1)S(1)}, u32[]{:S(2)}, u32[]{:S(2)}) collective-permute-start(bf16[6,12,128,128]{3,2,1,0:T(8,128)(2,1)} %refs_3_.1), channel_id=1, source_target_pairs={{0,1},{1,0},{2,3},{3,2},{4,5},{5,4},{6,7},{7,6},{8,9},{9,8},{10,11... | collective-permute-start | bytes 7077896 | tf_op jit(solution)/shard_map/ppermute | solution.py:19
  1.2 5.6 %collective-permute-start = (s32[6,12]{1,0:T(8,128)}, s32[6,12]{1,0:T(8,128)S(1)}, u32[]{:S(2)}, u32[]{:S(2)}) collective-permute-start(s32[6,12]{1,0:T(8,128)} %refs_0_.1), channel_id=1, source_target_pairs={{1,2},{3,4},{5,6},{7,8},{9,10},{11,12},{13,14},{15,0},{2,1},{4,3},... | collective-permute-start | bytes 872 | tf_op jit(solution)/shard_map/ppermute | solution.py:19
  7.4 2.5 %spread_kernel.1 = (bf16[768,768]{1,0:T(8,128)(2,1)S(1)}, bf16[768,512]{1,0:T(8,128)(2,1)S(1)}, bf16[768,512]{1,0:T(8,128)(2,1)S(1)}, s32[84]{0:T(128)S(1)}, s32[10]{0:T(128)S(1)}) custom-call(s32[6,12]{1,0:T(8,128)} %refs_0_.1, s32[6,12]{1,0:T(8,128)} %refs_1_.1, s32[1]{0:T(128)S(6)} %copy.10.refs_2_, bf16[6,12,128,128]{3,2,1,0:T(8,128)(2,1)} %refs_3_.1), custom_call_target="tpu_custom_call" | custom-call | flops 1 | bytes 1 | tf_op jit(solution)/shard_map/spread_kernel/pallas_call | solution.py:313
  10.0 0.0 collective-permute-done.refs_1_
  10.0 1.5 %pack_kernel.1 = (bf16[512,512]{1,0:T(8,128)(2,1)S(1)}, bf16[512,512]{1,0:T(8,128)(2,1)S(1)}, s32[7]{0:T(128)S(1)}) custom-call(s32[10]{0:T(128)S(1)} %get-tuple-element.26.refs_0_.refs_1_, s32[6,12]{1,0:T(8,128)S(1)} %collective-permute-done.refs_1_, bf16[768,768]{1,0:T(8,128)(2,1)S(1)} %get-tuple-element.27.refs_2_.refs_4_, ...), custom_call_target="tpu_custom_call" | custom-call | flops 1 | bytes 1 | tf_op jit(solution)/shard_map/pack_kernel/pallas_call | solution.py:319
  11.5 2.8 %collective-permute-start.3 = (bf16[512,512]{1,0:T(8,128)(2,1)S(1)}, bf16[512,512]{1,0:T(8,128)(2,1)S(1)}, u32[]{:S(2)}, u32[]{:S(2)}) collective-permute-start(bf16[512,512]{1,0:T(8,128)(2,1)S(1)} %get-tuple-element.32), channel_id=1, source_target_pairs={{1,2},{3,4},{5,6},{7,8},{9,10},{11,12},{13,14},{15,0},{2,1},{4,3},... | collective-permute-start | bytes 1572872 | tf_op jit(solution)/shard_map/ppermute | solution.py:19
  14.3 0.0 copy-done
  14.3 0.0 collective-permute-start.1
  14.3 1.2 %collective-permute-done.1.refs_3_ = s32[6,12]{1,0:T(8,128)S(1)} collective-permute-done((s32[6,12]{1,0:T(8,128)S(1)}, s32[6,12]{1,0:T(8,128)S(1)}, u32[]{:S(2)}, u32[]{:S(2)}) %collective-permute-start.1) | collective-permute-done | bytes 320 | tf_op jit(solution)/shard_map/ppermute | solution.py:19
  15.5 0.0 collective-permute-done.2.refs_7_
  15.5 7.8 %own_kernel.1 = (bf16[6,12,128,128]{3,2,1,0:T(8,128)(2,1)}, f32[768,512]{1,0:T(8,128)}, f32[768,512]{1,0:T(8,128)S(1)}, bf16[512,512]{1,0:T(8,128)(2,1)S(1)}, f32[1]{0:T(128)}) custom-call(s32[84]{0:T(128)S(1)} %get-tuple-element.25.refs_0_, s32[10]{0:T(128)S(1)} %get-tuple-element.26.refs_0_.refs_1_, s32[7]{0:T(128)S(1)} %get-tuple-element.29.refs_2_, ...), custom_call_target="tpu_custom_call" | custom-call | flops 1 | bytes 1 | tf_op jit(solution)/shard_map/own_kernel/pallas_call | solution.py:325
  23.3 0.0 collective-permute-done.3.refs_4_.refs_5_
  23.3 1.5 %trace_kernel.1 = f32[8,128]{1,0:T(8,128)S(1)} custom-call(s32[84]{0:T(128)S(1)} %get-tuple-element.25.refs_0_, s32[10]{0:T(128)S(1)} %get-tuple-element.26.refs_0_.refs_1_, s32[7]{0:T(128)S(1)} %get-tuple-element.29.refs_2_, bf16[512,512]{1,0:T(8,128)(2,1)S(1)} %get-tuple-element.35.refs_3_, bf16[512,512]{1,0:T(8,128)(2,1)S(1)} %collective-permute-done.3.refs_4_.refs_5_, ...), custom_call_target="tpu_custom_call" | custom-call | flops 1 | bytes 1 | tf_op jit(solution)/shard_map/trace_kernel/pallas_call | solution.py:333
  24.8 2.5 %collective-permute-start.8 = (bf16[512,512]{1,0:T(8,128)(2,1)S(1)}, bf16[512,512]{1,0:T(8,128)(2,1)S(1)}, u32[]{:S(2)}, u32[]{:S(2)}) collective-permute-start(bf16[512,512]{1,0:T(8,128)(2,1)S(1)} %get-tuple-element.44), channel_id=1, source_target_pairs={{1,2},{3,4},{5,6},{7,8},{9,10},{11,12},{13,14},{15,0},{2,1},{4,3},... | collective-permute-start | bytes 1572872 | tf_op jit(solution)/shard_map/ppermute | solution.py:19
  27.3 0.0 collective-permute-start.4
  27.3 1.2 %collective-permute-done.4 = f32[8,128]{1,0:T(8,128)S(1)} collective-permute-done((f32[8,128]{1,0:T(8,128)S(1)}, f32[8,128]{1,0:T(8,128)S(1)}, u32[]{:S(2)}, u32[]{:S(2)}) %collective-permute-start.4) | collective-permute-done | bytes 4128 | tf_op jit(solution)/shard_map/ppermute | solution.py:19
  28.5 3.3 %far_kernel.1.refs_6_ = bf16[6,12,128,128]{3,2,1,0:T(8,128)(2,1)} custom-call(s32[84]{0:T(128)S(1)} %get-tuple-element.25.refs_0_, s32[10]{0:T(128)S(1)} %get-tuple-element.26.refs_0_.refs_1_, s32[7]{0:T(128)S(1)} %get-tuple-element.29.refs_2_, bf16[768,512]{1,0:T(8,128)(2,1)S(1)} %get-tuple-element.28.refs_3_.refs_5_, ...), custom_call_target="tpu_custom_call", output_to_operand_aliasing={{}: (6, {})} | custom-call | flops 1 | bytes 1 | tf_op jit(solution)/shard_map/far_kernel/pallas_call | solution.py:342
  31.8 0.1 collective-permute-start.5
  31.9 3.6 %collective-permute-done.5 = f32[8,128]{1,0:T(8,128)S(1)} collective-permute-done((f32[8,128]{1,0:T(8,128)S(1)}, f32[8,128]{1,0:T(8,128)S(1)}, u32[]{:S(2)}, u32[]{:S(2)}) %collective-permute-start.5) | collective-permute-done | bytes 4128 | tf_op jit(solution)/shard_map/ppermute | solution.py:19
  35.5 0.0 collective-permute-start.6
  35.5 4.5 %collective-permute-done.6 = f32[8,128]{1,0:T(8,128)S(1)} collective-permute-done((f32[8,128]{1,0:T(8,128)S(1)}, f32[8,128]{1,0:T(8,128)S(1)}, u32[]{:S(2)}, u32[]{:S(2)}) %collective-permute-start.6) | collective-permute-done | bytes 4128 | tf_op jit(solution)/shard_map/ppermute | solution.py:19
  40.0 0.0 collective-permute-start.7
  40.0 0.0 collective-permute-done.8.refs_5_
  40.0 2.0 %last_kernel.1 = bf16[6,12,128,128]{3,2,1,0:T(8,128)(2,1)} custom-call(s32[84]{0:T(128)S(1)} %get-tuple-element.25.refs_0_, s32[10]{0:T(128)S(1)} %get-tuple-element.26.refs_0_.refs_1_, s32[7]{0:T(128)S(1)} %get-tuple-element.29.refs_2_, bf16[768,512]{1,0:T(8,128)(2,1)S(1)} %get-tuple-element.28.refs_3_.refs_5_, ...), custom_call_target="tpu_custom_call", output_to_operand_aliasing={{}: (6, {})} | custom-call | flops 1 | bytes 1 | tf_op jit(solution)/shard_map/last_kernel/pallas_call | solution.py:342
  42.0 1.6 %collective-permute-done.7 = f32[8,128]{1,0:T(8,128)S(1)} collective-permute-done((f32[8,128]{1,0:T(8,128)S(1)}, f32[8,128]{1,0:T(8,128)S(1)}, u32[]{:S(2)}, u32[]{:S(2)}) %collective-permute-start.7) | collective-permute-done | bytes 4128 | tf_op jit(solution)/shard_map/ppermute | solution.py:19
  43.6 0.5 %slice.3 = f32[1,1]{1,0:T(1,128)} slice(f32[8,128]{1,0:T(8,128)S(1)} %add.15), slice={[0:1], [0:1]} | slice | bytes 8 | tf_op jit(solution)/shard_map/slice | solution.py:360
  (4 shorter events, 0.0 us)
Async XLA Ops:
  0.6 13.7 %copy-start = (s32[6,12]{1,0:T(8,128)S(1)}, s32[6,12]{1,0:T(8,128)}, u32[]{:S(2)}) copy-start(s32[6,12]{1,0:T(8,128)} %refs_0_.1) | copy-start | bytes 868
  0.6 14.8 %collective-permute-start.2 = (bf16[6,12,128,128]{3,2,1,0:T(8,128)(2,1)}, bf16[6,12,128,128]{3,2,1,0:T(8,128)(2,1)S(1)}, u32[]{:S(2)}, u32[]{:S(2)}) collective-permute-start(bf16[6,12,128,128]{3,2,1,0:T(8,128)(2,1)} %refs_3_.1), channel_id=1, source_target_pairs={{0,1},{1,0},{2,3},{3,2},{4,5},{5,4},{6,7},{7,6},{8,9},{9,8},{10,11... | collective-permute-start | bytes 7077896 | tf_op jit(solution)/shard_map/ppermute | solution.py:19
  1.2 8.8 %collective-permute-start = (s32[6,12]{1,0:T(8,128)}, s32[6,12]{1,0:T(8,128)S(1)}, u32[]{:S(2)}, u32[]{:S(2)}) collective-permute-start(s32[6,12]{1,0:T(8,128)} %refs_0_.1), channel_id=1, source_target_pairs={{1,2},{3,4},{5,6},{7,8},{9,10},{11,12},{13,14},{15,0},{2,1},{4,3},... | collective-permute-start | bytes 872 | tf_op jit(solution)/shard_map/ppermute | solution.py:19
  11.5 11.7 %collective-permute-start.3 = (bf16[512,512]{1,0:T(8,128)(2,1)S(1)}, bf16[512,512]{1,0:T(8,128)(2,1)S(1)}, u32[]{:S(2)}, u32[]{:S(2)}) collective-permute-start(bf16[512,512]{1,0:T(8,128)(2,1)S(1)} %get-tuple-element.32), channel_id=1, source_target_pairs={{1,2},{3,4},{5,6},{7,8},{9,10},{11,12},{13,14},{15,0},{2,1},{4,3},... | collective-permute-start | bytes 1572872 | tf_op jit(solution)/shard_map/ppermute | solution.py:19
  14.3 1.2 %collective-permute-start.1 = (s32[6,12]{1,0:T(8,128)S(1)}, s32[6,12]{1,0:T(8,128)S(1)}, u32[]{:S(2)}, u32[]{:S(2)}) collective-permute-start(s32[6,12]{1,0:T(8,128)S(1)} %copy-done), channel_id=1, source_target_pairs={{0,1},{1,0},{2,3},{3,2},{4,5},{5,4},{6,7},{7,6},{8,9},{9,8},{10,11... | collective-permute-start | bytes 872 | tf_op jit(solution)/shard_map/ppermute | solution.py:19
  24.8 15.2 %collective-permute-start.8 = (bf16[512,512]{1,0:T(8,128)(2,1)S(1)}, bf16[512,512]{1,0:T(8,128)(2,1)S(1)}, u32[]{:S(2)}, u32[]{:S(2)}) collective-permute-start(bf16[512,512]{1,0:T(8,128)(2,1)S(1)} %get-tuple-element.44), channel_id=1, source_target_pairs={{1,2},{3,4},{5,6},{7,8},{9,10},{11,12},{13,14},{15,0},{2,1},{4,3},... | collective-permute-start | bytes 1572872 | tf_op jit(solution)/shard_map/ppermute | solution.py:19
  27.3 1.2 %collective-permute-start.4 = (f32[8,128]{1,0:T(8,128)S(1)}, f32[8,128]{1,0:T(8,128)S(1)}, u32[]{:S(2)}, u32[]{:S(2)}) collective-permute-start(f32[8,128]{1,0:T(8,128)S(1)} %trace_kernel.1), channel_id=1, source_target_pairs={{0,1},{1,0},{2,3},{3,2},{4,5},{5,4},{6,7},{7,6},{8,9},{9,8},{10,11... | collective-permute-start | bytes 12296 | tf_op jit(solution)/shard_map/ppermute | solution.py:19
  31.8 3.7 %collective-permute-start.5 = (f32[8,128]{1,0:T(8,128)S(1)}, f32[8,128]{1,0:T(8,128)S(1)}, u32[]{:S(2)}, u32[]{:S(2)}) collective-permute-start(f32[8,128]{1,0:T(8,128)S(1)} %add.12), channel_id=1, source_target_pairs={{0,4},{1,5},{2,6},{3,7},{4,0},{5,1},{6,2},{7,3},{8,12},{9,13},{10,... | collective-permute-start | bytes 12296 | tf_op jit(solution)/shard_map/ppermute | solution.py:19
  35.5 4.5 %collective-permute-start.6 = (f32[8,128]{1,0:T(8,128)S(1)}, f32[8,128]{1,0:T(8,128)S(1)}, u32[]{:S(2)}, u32[]{:S(2)}) collective-permute-start(f32[8,128]{1,0:T(8,128)S(1)} %add.13), channel_id=1, source_target_pairs={{0,8},{1,9},{2,10},{3,11},{4,12},{5,13},{6,14},{7,15},{8,0},{9,1},... | collective-permute-start | bytes 12296 | tf_op jit(solution)/shard_map/ppermute | solution.py:19
  40.0 3.6 %collective-permute-start.7 = (f32[8,128]{1,0:T(8,128)S(1)}, f32[8,128]{1,0:T(8,128)S(1)}, u32[]{:S(2)}, u32[]{:S(2)}) collective-permute-start(f32[8,128]{1,0:T(8,128)S(1)} %add.14), channel_id=1, source_target_pairs={{0,2},{1,3},{2,0},{3,1},{4,6},{5,7},{6,4},{7,5},{8,10},{9,11},{10,... | collective-permute-start | bytes 12296 | tf_op jit(solution)/shard_map/ppermute | solution.py:19

commit v4 on v3

--- a/solution.py
+++ b/solution.py
@@ -148,7 +148,7 @@
 
 
 def own_kernel(table, meta, asked, cols_inner, own, outer, inner, x_inner, out, base_far, base_near, turned, trace,
-               got_own, got_far, square, side, stage, slots_of, order, sem, sem_base, sem_got):
+               got_own, got_far, square, side, stage, slots_of, order, sem, sem_got):
     rows, slots = cols_inner.shape
     block = own.shape[0] // rows
     across = rows + 2 * CAP
@@ -186,7 +186,6 @@
         for c in range(CAP):
             value = outer[pl.ds(pl.multiple_of(asked[c] * block, block), block), pl.ds(r * block, block)]
             turned[pl.ds(r * block, block), pl.ds(c * block, block)] = value.T
-    copies = []
     for copy in arrive:
         copy.wait()
     for r in range(CAP):
@@ -200,7 +199,7 @@
         square[:, place] = square[:, place] + part[:, c * block:(c + 1) * block]
     for c in range(CAP):
         place = pl.ds(pl.multiple_of(asked[c] * block, block), block)
-        copies.append(copy_in(square.at[:, place], base_far.at[:, pl.ds(c * block, block)], sem_base))
+        base_far[:, pl.ds(c * block, block)] = square[:, place]
     total = jnp.zeros((block, block), jnp.float32)
     for i in range(rows):
         span = pl.ds(i * block, block)
@@ -224,8 +223,6 @@
             waits.append(give(stage.at[i, c], out, i, code, sem))
     for wait in waits:
         wait()
-    for copy in copies:
-        copy.wait()
 
 
 def trace_kernel(rows, table, meta, asked, turned, far_hbm, trace_own, trace, far, sem):
@@ -324,12 +321,12 @@
     far = permute(far_out, outside)
     out, base_far, base_near, turned, trace_own = call(
         own_kernel,
-        [(x.shape, bf16, HBM), ((wide, narrow), f32, HBM, True), ((wide, narrow), f32, VMEM),
+        [(x.shape, bf16, HBM), ((wide, narrow), f32, VMEM), ((wide, narrow), f32, VMEM),
          ((narrow, narrow), bf16, VMEM), ((1,), f32, SMEM)],
         [SMEM] * 4 + [VMEM] * 3 + [HBM],
         [pltpu.VMEM((narrow, narrow), bf16), pltpu.VMEM((narrow, narrow), bf16), pltpu.VMEM((wide, wide), f32),
          pltpu.VMEM((wide, narrow), f32), pltpu.VMEM((rows, rows, block, block), bf16), ints(rows * (2 * rows + 1)),
-         ints(CAP + 1), dma, dma, dma], 24)(table, meta, asked, cols_inner, own, outer, inner, x_inner)
+         ints(CAP + 1), dma, dma], 24)(table, meta, asked, cols_inner, own, outer, inner, x_inner)
     partial, = call(
         trace_kernel, [((8, block), f32, VMEM)], [SMEM] * 3 + [VMEM, HBM, SMEM],
         [pltpu.VMEM((narrow, narrow), bf16), dma], 12, first=rows)(table, meta, asked, turned, far, trace_own)
@@ -347,16 +344,16 @@
     steps = ring_steps()
     if steps is None:
         total = lax.psum(partial, RING)
-        return half(last_kernel, base_near, near, half(far_kernel, hbm(base_far), far, out)), total[0, :1]
+        return half(last_kernel, base_near, near, half(far_kernel, base_far, far, out)), total[0, :1]
     partial = partial + partner(partial, steps[0])
     out, partial = barrier((out, partial))
-    out = half(far_kernel, hbm(base_far), far, out)
+    out = half(far_kernel, base_far, far, out)
     out, partial = barrier((out, partial))
     for step in steps[1:-1]:
         partial = partial + partner(partial, step)
     ready, partial = barrier((out, partial))
     out = half(last_kernel, base_near, near, ready)
-    other, out = barrier((partner(partial, steps[-1]), out))
+    other, out = barrier((partner(partial, steps[-1] | 1), out))
     return out, (partial + other)[0, :1]
 
 

time: 44.3 us -> 42.5 us (0.959)
  Pallas kernels: 18.7 us -> 17.1 us
  waiting for transfers between devices: 12 us -> 11.5 us
    pallas_call x2, Pallas kernels: 5.36 us -> 4.09 us  [half(): call(kernel, [(x.shape, bf16, HBM)], [SMEM] * 3 + [VMEM] + [HBM] * 3, hal...]
    ppermute x9, waiting for transfers between devices: 12 us -> 11.5 us  [permute(): return lax.ppermute(value, RING, pairs)]
  transfers between devices with their start and end apart: 9 -> 9, of which waited for: 5 -> 5; matrix products, arithmetic and copies ran while one was open for 0% -> 0% of each run, Pallas kernels for 39% -> 37%
where the time goes in v4:
time: 42.5 us; the launch traced here: 42.3 us
  Pallas kernels  17.1 us (40%)
  starting transfers between devices  11.8 us (28%)
  waiting for transfers between devices  11.5 us (27%)
  between operations  1.37 us (3%)
  local copies, waits for them, and re-layouts  0.52 us (1%)
    ppermute x9, starting transfers between devices, permute(): return lax.ppermute(value, RING, pairs)  11.8 us
    ppermute x9, waiting for transfers between devices, permute(): return lax.ppermute(value, RING, pairs)  11.5 us
    pallas_call x1, Pallas kernels, body(): call(own_kernel, [(x.shape, bf16, HBM), ((wide, narrow), f32, VMEM), ((wi...  7.47 us
    pallas_call x2, Pallas kernels, half(): call(kernel, [(x.shape, bf16, HBM)], [SMEM] * 3 + [VMEM] + [HBM] * 3, hal...  4.09 us
    pallas_call x1, Pallas kernels, body(): call(spread_kernel, [((wide, wide), bf16, VMEM), ((wide, narrow), bf16, V...  2.55 us
    pallas_call x1, Pallas kernels, body(): call(trace_kernel, [((8, block), f32, VMEM)], [SMEM] * 3 + [VMEM, HBM, SM...  1.51 us
    pallas_call x1, Pallas kernels, body(): call(pack_kernel, [((narrow, narrow), bf16, VMEM), ((narrow, narrow), bf1...  1.5 us
  transfers between devices with their start and end apart: 9, of which 5 were waited for; matrix products, arithmetic and copies ran while one was open for 0% of the time, Pallas kernels for 37%

profile of v4, /device:TPU:0, one launch (start us, length us, event | category | flops | bytes accessed | tf_op | source)
XLA Modules:
  0.0 42.3 jit_solution(6204550291702694140)
XLA Ops:
  0.6 0.0 copy-start
  0.6 0.5 %collective-permute-start.2 = (bf16[6,12,128,128]{3,2,1,0:T(8,128)(2,1)}, bf16[6,12,128,128]{3,2,1,0:T(8,128)(2,1)S(1)}, u32[]{:S(2)}, u32[]{:S(2)}) collective-permute-start(bf16[6,12,128,128]{3,2,1,0:T(8,128)(2,1)} %refs_3_.1), channel_id=1, source_target_pairs={{0,1},{1,0},{2,3},{3,2},{4,5},{5,4},{6,7},{7,6},{8,9},{9,8},{10,11... | collective-permute-start | bytes 7077896 | tf_op jit(solution)/shard_map/ppermute | solution.py:19
  1.2 5.6 %collective-permute-start = (s32[6,12]{1,0:T(8,128)}, s32[6,12]{1,0:T(8,128)S(1)}, u32[]{:S(2)}, u32[]{:S(2)}) collective-permute-start(s32[6,12]{1,0:T(8,128)} %refs_0_.1), channel_id=1, source_target_pairs={{1,2},{3,4},{5,6},{7,8},{9,10},{11,12},{13,14},{15,0},{2,1},{4,3},... | collective-permute-start | bytes 872 | tf_op jit(solution)/shard_map/ppermute | solution.py:19
  7.4 2.5 %spread_kernel.1 = (bf16[768,768]{1,0:T(8,128)(2,1)S(1)}, bf16[768,512]{1,0:T(8,128)(2,1)S(1)}, bf16[768,512]{1,0:T(8,128)(2,1)S(1)}, s32[84]{0:T(128)S(1)}, s32[10]{0:T(128)S(1)}) custom-call(s32[6,12]{1,0:T(8,128)} %refs_0_.1, s32[6,12]{1,0:T(8,128)} %refs_1_.1, s32[1]{0:T(128)S(6)} %copy.10.refs_2_, bf16[6,12,128,128]{3,2,1,0:T(8,128)(2,1)} %refs_3_.1), custom_call_target="tpu_custom_call" | custom-call | flops 1 | bytes 1 | tf_op jit(solution)/shard_map/spread_kernel/pallas_call | solution.py:310
  10.0 0.0 collective-permute-done.refs_1_
  10.0 1.5 %pack_kernel.1 = (bf16[512,512]{1,0:T(8,128)(2,1)S(1)}, bf16[512,512]{1,0:T(8,128)(2,1)S(1)}, s32[7]{0:T(128)S(1)}) custom-call(s32[10]{0:T(128)S(1)} %get-tuple-element.26.refs_0_.refs_1_, s32[6,12]{1,0:T(8,128)S(1)} %collective-permute-done.refs_1_, bf16[768,768]{1,0:T(8,128)(2,1)S(1)} %get-tuple-element.27.refs_2_.refs_4_, ...), custom_call_target="tpu_custom_call" | custom-call | flops 1 | bytes 1 | tf_op jit(solution)/shard_map/pack_kernel/pallas_call | solution.py:316
  11.5 2.8 %collective-permute-start.3 = (bf16[512,512]{1,0:T(8,128)(2,1)S(1)}, bf16[512,512]{1,0:T(8,128)(2,1)S(1)}, u32[]{:S(2)}, u32[]{:S(2)}) collective-permute-start(bf16[512,512]{1,0:T(8,128)(2,1)S(1)} %get-tuple-element.32), channel_id=1, source_target_pairs={{1,2},{3,4},{5,6},{7,8},{9,10},{11,12},{13,14},{15,0},{2,1},{4,3},... | collective-permute-start | bytes 1572872 | tf_op jit(solution)/shard_map/ppermute | solution.py:19
  14.3 0.0 copy-done
  14.3 0.0 collective-permute-start.1
  14.3 1.2 %collective-permute-done.1.refs_3_ = s32[6,12]{1,0:T(8,128)S(1)} collective-permute-done((s32[6,12]{1,0:T(8,128)S(1)}, s32[6,12]{1,0:T(8,128)S(1)}, u32[]{:S(2)}, u32[]{:S(2)}) %collective-permute-start.1) | collective-permute-done | bytes 320 | tf_op jit(solution)/shard_map/ppermute | solution.py:19
  15.5 0.0 collective-permute-done.2.refs_7_
  15.5 7.5 %own_kernel.1 = (bf16[6,12,128,128]{3,2,1,0:T(8,128)(2,1)}, f32[768,512]{1,0:T(8,128)S(1)}, f32[768,512]{1,0:T(8,128)S(1)}, bf16[512,512]{1,0:T(8,128)(2,1)S(1)}, f32[1]{0:T(128)}) custom-call(s32[84]{0:T(128)S(1)} %get-tuple-element.25.refs_0_, s32[10]{0:T(128)S(1)} %get-tuple-element.26.refs_0_.refs_1_, s32[7]{0:T(128)S(1)} %get-tuple-element.29.refs_2_, ...), custom_call_target="tpu_custom_call" | custom-call | flops 1 | bytes 1 | tf_op jit(solution)/shard_map/own_kernel/pallas_call | solution.py:322
  23.0 0.0 collective-permute-done.3.refs_4_.refs_5_
  23.0 1.5 %trace_kernel.1 = f32[8,128]{1,0:T(8,128)S(1)} custom-call(s32[84]{0:T(128)S(1)} %get-tuple-element.25.refs_0_, s32[10]{0:T(128)S(1)} %get-tuple-element.26.refs_0_.refs_1_, s32[7]{0:T(128)S(1)} %get-tuple-element.29.refs_2_, bf16[512,512]{1,0:T(8,128)(2,1)S(1)} %get-tuple-element.35.refs_3_, bf16[512,512]{1,0:T(8,128)(2,1)S(1)} %collective-permute-done.3.refs_4_.refs_5_, ...), custom_call_target="tpu_custom_call" | custom-call | flops 1 | bytes 1 | tf_op jit(solution)/shard_map/trace_kernel/pallas_call | solution.py:330
  24.5 2.8 %collective-permute-start.8 = (bf16[512,512]{1,0:T(8,128)(2,1)S(1)}, bf16[512,512]{1,0:T(8,128)(2,1)S(1)}, u32[]{:S(2)}, u32[]{:S(2)}) collective-permute-start(bf16[512,512]{1,0:T(8,128)(2,1)S(1)} %get-tuple-element.44), channel_id=1, source_target_pairs={{1,2},{3,4},{5,6},{7,8},{9,10},{11,12},{13,14},{15,0},{2,1},{4,3},... | collective-permute-start | bytes 1572872 | tf_op jit(solution)/shard_map/ppermute | solution.py:19
  27.3 0.0 collective-permute-start.4
  27.3 1.2 %collective-permute-done.4 = f32[8,128]{1,0:T(8,128)S(1)} collective-permute-done((f32[8,128]{1,0:T(8,128)S(1)}, f32[8,128]{1,0:T(8,128)S(1)}, u32[]{:S(2)}, u32[]{:S(2)}) %collective-permute-start.4) | collective-permute-done | bytes 4128 | tf_op jit(solution)/shard_map/ppermute | solution.py:19
  28.5 2.1 %far_kernel.1.refs_6_ = bf16[6,12,128,128]{3,2,1,0:T(8,128)(2,1)} custom-call(s32[84]{0:T(128)S(1)} %get-tuple-element.25.refs_0_, s32[10]{0:T(128)S(1)} %get-tuple-element.26.refs_0_.refs_1_, s32[7]{0:T(128)S(1)} %get-tuple-element.29.refs_2_, bf16[768,512]{1,0:T(8,128)(2,1)S(1)} %get-tuple-element.28.refs_3_.refs_5_, ...), custom_call_target="tpu_custom_call", output_to_operand_aliasing={{}: (6, {})} | custom-call | flops 1 | bytes 1 | tf_op jit(solution)/shard_map/far_kernel/pallas_call | solution.py:339
  30.5 0.1 collective-permute-start.5
  30.6 3.6 %collective-permute-done.5 = f32[8,128]{1,0:T(8,128)S(1)} collective-permute-done((f32[8,128]{1,0:T(8,128)S(1)}, f32[8,128]{1,0:T(8,128)S(1)}, u32[]{:S(2)}, u32[]{:S(2)}) %collective-permute-start.5) | collective-permute-done | bytes 4128 | tf_op jit(solution)/shard_map/ppermute | solution.py:19
  34.2 0.0 collective-permute-start.6
  34.2 4.5 %collective-permute-done.6 = f32[8,128]{1,0:T(8,128)S(1)} collective-permute-done((f32[8,128]{1,0:T(8,128)S(1)}, f32[8,128]{1,0:T(8,128)S(1)}, u32[]{:S(2)}, u32[]{:S(2)}) %collective-permute-start.6) | collective-permute-done | bytes 4128 | tf_op jit(solution)/shard_map/ppermute | solution.py:19
  38.7 0.0 collective-permute-start.7
  38.7 0.0 collective-permute-done.8.refs_5_
  38.7 2.0 %last_kernel.1 = bf16[6,12,128,128]{3,2,1,0:T(8,128)(2,1)} custom-call(s32[84]{0:T(128)S(1)} %get-tuple-element.25.refs_0_, s32[10]{0:T(128)S(1)} %get-tuple-element.26.refs_0_.refs_1_, s32[7]{0:T(128)S(1)} %get-tuple-element.29.refs_2_, bf16[768,512]{1,0:T(8,128)(2,1)S(1)} %get-tuple-element.28.refs_3_.refs_5_, ...), custom_call_target="tpu_custom_call", output_to_operand_aliasing={{}: (6, {})} | custom-call | flops 1 | bytes 1 | tf_op jit(solution)/shard_map/last_kernel/pallas_call | solution.py:339
  40.8 1.0 %collective-permute-done.7 = f32[8,128]{1,0:T(8,128)S(1)} collective-permute-done((f32[8,128]{1,0:T(8,128)S(1)}, f32[8,128]{1,0:T(8,128)S(1)}, u32[]{:S(2)}, u32[]{:S(2)}) %collective-permute-start.7) | collective-permute-done | bytes 4128 | tf_op jit(solution)/shard_map/ppermute | solution.py:19
  41.8 0.5 %slice.3 = f32[1,1]{1,0:T(1,128)} slice(f32[8,128]{1,0:T(8,128)S(1)} %add.15), slice={[0:1], [0:1]} | slice | bytes 8 | tf_op jit(solution)/shard_map/slice | solution.py:357
  (4 shorter events, 0.0 us)
Async XLA Ops:
  0.6 13.7 %copy-start = (s32[6,12]{1,0:T(8,128)S(1)}, s32[6,12]{1,0:T(8,128)}, u32[]{:S(2)}) copy-start(s32[6,12]{1,0:T(8,128)} %refs_0_.1) | copy-start | bytes 868
  0.6 14.8 %collective-permute-start.2 = (bf16[6,12,128,128]{3,2,1,0:T(8,128)(2,1)}, bf16[6,12,128,128]{3,2,1,0:T(8,128)(2,1)S(1)}, u32[]{:S(2)}, u32[]{:S(2)}) collective-permute-start(bf16[6,12,128,128]{3,2,1,0:T(8,128)(2,1)} %refs_3_.1), channel_id=1, source_target_pairs={{0,1},{1,0},{2,3},{3,2},{4,5},{5,4},{6,7},{7,6},{8,9},{9,8},{10,11... | collective-permute-start | bytes 7077896 | tf_op jit(solution)/shard_map/ppermute | solution.py:19
  1.2 8.8 %collective-permute-start = (s32[6,12]{1,0:T(8,128)}, s32[6,12]{1,0:T(8,128)S(1)}, u32[]{:S(2)}, u32[]{:S(2)}) collective-permute-start(s32[6,12]{1,0:T(8,128)} %refs_0_.1), channel_id=1, source_target_pairs={{1,2},{3,4},{5,6},{7,8},{9,10},{11,12},{13,14},{15,0},{2,1},{4,3},... | collective-permute-start | bytes 872 | tf_op jit(solution)/shard_map/ppermute | solution.py:19
  11.5 11.5 %collective-permute-start.3 = (bf16[512,512]{1,0:T(8,128)(2,1)S(1)}, bf16[512,512]{1,0:T(8,128)(2,1)S(1)}, u32[]{:S(2)}, u32[]{:S(2)}) collective-permute-start(bf16[512,512]{1,0:T(8,128)(2,1)S(1)} %get-tuple-element.32), channel_id=1, source_target_pairs={{1,2},{3,4},{5,6},{7,8},{9,10},{11,12},{13,14},{15,0},{2,1},{4,3},... | collective-permute-start | bytes 1572872 | tf_op jit(solution)/shard_map/ppermute | solution.py:19
  14.3 1.2 %collective-permute-start.1 = (s32[6,12]{1,0:T(8,128)S(1)}, s32[6,12]{1,0:T(8,128)S(1)}, u32[]{:S(2)}, u32[]{:S(2)}) collective-permute-start(s32[6,12]{1,0:T(8,128)S(1)} %copy-done), channel_id=1, source_target_pairs={{0,1},{1,0},{2,3},{3,2},{4,5},{5,4},{6,7},{7,6},{8,9},{9,8},{10,11... | collective-permute-start | bytes 872 | tf_op jit(solution)/shard_map/ppermute | solution.py:19
  24.5 14.2 %collective-permute-start.8 = (bf16[512,512]{1,0:T(8,128)(2,1)S(1)}, bf16[512,512]{1,0:T(8,128)(2,1)S(1)}, u32[]{:S(2)}, u32[]{:S(2)}) collective-permute-start(bf16[512,512]{1,0:T(8,128)(2,1)S(1)} %get-tuple-element.44), channel_id=1, source_target_pairs={{1,2},{3,4},{5,6},{7,8},{9,10},{11,12},{13,14},{15,0},{2,1},{4,3},... | collective-permute-start | bytes 1572872 | tf_op jit(solution)/shard_map/ppermute | solution.py:19
  27.3 1.2 %collective-permute-start.4 = (f32[8,128]{1,0:T(8,128)S(1)}, f32[8,128]{1,0:T(8,128)S(1)}, u32[]{:S(2)}, u32[]{:S(2)}) collective-permute-start(f32[8,128]{1,0:T(8,128)S(1)} %trace_kernel.1), channel_id=1, source_target_pairs={{0,1},{1,0},{2,3},{3,2},{4,5},{5,4},{6,7},{7,6},{8,9},{9,8},{10,11... | collective-permute-start | bytes 12296 | tf_op jit(solution)/shard_map/ppermute | solution.py:19
  30.5 3.7 %collective-permute-start.5 = (f32[8,128]{1,0:T(8,128)S(1)}, f32[8,128]{1,0:T(8,128)S(1)}, u32[]{:S(2)}, u32[]{:S(2)}) collective-permute-start(f32[8,128]{1,0:T(8,128)S(1)} %add.12), channel_id=1, source_target_pairs={{0,4},{1,5},{2,6},{3,7},{4,0},{5,1},{6,2},{7,3},{8,12},{9,13},{10,... | collective-permute-start | bytes 12296 | tf_op jit(solution)/shard_map/ppermute | solution.py:19
  34.2 4.5 %collective-permute-start.6 = (f32[8,128]{1,0:T(8,128)S(1)}, f32[8,128]{1,0:T(8,128)S(1)}, u32[]{:S(2)}, u32[]{:S(2)}) collective-permute-start(f32[8,128]{1,0:T(8,128)S(1)} %add.13), channel_id=1, source_target_pairs={{0,8},{1,9},{2,10},{3,11},{4,12},{5,13},{6,14},{7,15},{8,0},{9,1},... | collective-permute-start | bytes 12296 | tf_op jit(solution)/shard_map/ppermute | solution.py:19
  38.7 3.0 %collective-permute-start.7 = (f32[8,128]{1,0:T(8,128)S(1)}, f32[8,128]{1,0:T(8,128)S(1)}, u32[]{:S(2)}, u32[]{:S(2)}) collective-permute-start(f32[8,128]{1,0:T(8,128)S(1)} %add.14), channel_id=1, source_target_pairs={{0,3},{1,2},{2,1},{3,0},{4,7},{5,6},{6,5},{7,4},{8,11},{9,10},{10,... | collective-permute-start | bytes 12296 | tf_op jit(solution)/shard_map/ppermute | solution.py:19

commit v5 on v4

--- a/solution.py
+++ b/solution.py
@@ -225,10 +225,9 @@
         wait()
 
 
-def trace_kernel(rows, table, meta, asked, turned, far_hbm, trace_own, trace, far, sem):
+def trace_kernel(rows, table, meta, asked, turned, far, trace_own, trace):
     block = turned.shape[0] // CAP
     across = rows + 2 * CAP
-    copy_in(far_hbm, far, sem).wait()
     total = jnp.zeros((8, block), jnp.float32)
     for c in range(CAP):
         mine = asked[c]
@@ -243,14 +242,10 @@
     return rows * block * lax.axis_size(RING)
 
 
-def finish_half(near, rows, table, meta, asked, outer, base_hbm, got_hbm, out, got, base, stage, sem, sem_base, sem_got):
+def finish_half(near, rows, table, meta, asked, outer, base, got, out, stage, sem):
     block = outer.shape[0] // rows
     across = rows + 2 * CAP
-    arrive = copy_in(got_hbm, got, sem_got)
-    copy = copy_in(base_hbm, base, sem_base)
-    arrive.wait()
     right = got[...] * signs(meta)[1].astype(got.dtype)
-    copy.wait()
     waits = []
     chunk = rows // 2
     for first in range(0, rows, chunk):
@@ -328,16 +323,15 @@
          pltpu.VMEM((wide, narrow), f32), pltpu.VMEM((rows, rows, block, block), bf16), ints(rows * (2 * rows + 1)),
          ints(CAP + 1), dma, dma], 24)(table, meta, asked, cols_inner, own, outer, inner, x_inner)
     partial, = call(
-        trace_kernel, [((8, block), f32, VMEM)], [SMEM] * 3 + [VMEM, HBM, SMEM],
-        [pltpu.VMEM((narrow, narrow), bf16), dma], 12, first=rows)(table, meta, asked, turned, far, trace_own)
+        trace_kernel, [((8, block), f32, VMEM)], [SMEM] * 3 + [VMEM, VMEM, SMEM],
+        [], 12, first=rows)(table, meta, asked, turned, far, trace_own)
     near_out, partial = barrier((near_out, partial))
     near = permute(near_out, outside)
-    half_scratch = [pltpu.VMEM((narrow, narrow), bf16), pltpu.VMEM((wide, narrow), f32),
-                    pltpu.VMEM((rows, CAP, block, block), bf16), dma, dma, dma]
+    half_scratch = [pltpu.VMEM((rows, CAP, block, block), bf16), dma]
 
     def half(kernel, base, got, out):
         result, = call(
-            kernel, [(x.shape, bf16, HBM)], [SMEM] * 3 + [VMEM] + [HBM] * 3, half_scratch, 16, {6: 0}, first=rows,
+            kernel, [(x.shape, bf16, HBM)], [SMEM] * 3 + [VMEM] * 3 + [HBM], half_scratch, 16, {6: 0}, first=rows,
         )(table, meta, asked, outer, base, got, out)
         return result
 

time: 42.5 us -> 42.3 us (level)
  transfers between devices with their start and end apart: 9 -> 9, of which waited for: 5 -> 6; matrix products, arithmetic and copies ran while one was open for 0% -> 0% of each run, Pallas kernels for 37% -> 36%
where the time goes in v5:
time: 42.3 us; the launch traced here: 42.2 us
  Pallas kernels  16.7 us (39%)
  starting transfers between devices  11.8 us (28%)
  waiting for transfers between devices  11.7 us (28%)
  between operations  1.37 us (3%)
  local copies, waits for them, and re-layouts  0.52 us (1%)
    ppermute x9, starting transfers between devices, permute(): return lax.ppermute(value, RING, pairs)  11.8 us
    ppermute x9, waiting for transfers between devices, permute(): return lax.ppermute(value, RING, pairs)  11.7 us
    pallas_call x1, Pallas kernels, body(): call(own_kernel, [(x.shape, bf16, HBM), ((wide, narrow), f32, VMEM), ((wi...  7.42 us
    pallas_call x2, Pallas kernels, half(): call(kernel, [(x.shape, bf16, HBM)], [SMEM] * 3 + [VMEM] * 3 + [HBM], hal...  3.77 us
    pallas_call x1, Pallas kernels, body(): call(spread_kernel, [((wide, wide), bf16, VMEM), ((wide, narrow), bf16, V...  2.55 us
    pallas_call x1, Pallas kernels, body(): call(pack_kernel, [((narrow, narrow), bf16, VMEM), ((narrow, narrow), bf1...  1.5 us
    pallas_call x1, Pallas kernels, body(): call(trace_kernel, [((8, block), f32, VMEM)], [SMEM] * 3 + [VMEM, VMEM, S...  1.47 us
  transfers between devices with their start and end apart: 9, of which 6 were waited for; matrix products, arithmetic and copies ran while one was open for 0% of the time, Pallas kernels for 36%

profile of v5, /device:TPU:0, one launch (start us, length us, event | category | flops | bytes accessed | tf_op | source)
XLA Modules:
  0.0 42.2 jit_solution(230207444661748221)
XLA Ops:
  0.6 0.0 copy-start
  0.6 0.5 %collective-permute-start.2 = (bf16[6,12,128,128]{3,2,1,0:T(8,128)(2,1)}, bf16[6,12,128,128]{3,2,1,0:T(8,128)(2,1)S(1)}, u32[]{:S(2)}, u32[]{:S(2)}) collective-permute-start(bf16[6,12,128,128]{3,2,1,0:T(8,128)(2,1)} %refs_3_.1), channel_id=1, source_target_pairs={{0,1},{1,0},{2,3},{3,2},{4,5},{5,4},{6,7},{7,6},{8,9},{9,8},{10,11... | collective-permute-start | bytes 7077896 | tf_op jit(solution)/shard_map/ppermute | solution.py:19
  1.2 5.6 %collective-permute-start = (s32[6,12]{1,0:T(8,128)}, s32[6,12]{1,0:T(8,128)S(1)}, u32[]{:S(2)}, u32[]{:S(2)}) collective-permute-start(s32[6,12]{1,0:T(8,128)} %refs_0_.1), channel_id=1, source_target_pairs={{1,2},{3,4},{5,6},{7,8},{9,10},{11,12},{13,14},{15,0},{2,1},{4,3},... | collective-permute-start | bytes 872 | tf_op jit(solution)/shard_map/ppermute | solution.py:19
  7.4 2.5 %spread_kernel.1 = (bf16[768,768]{1,0:T(8,128)(2,1)S(1)}, bf16[768,512]{1,0:T(8,128)(2,1)S(1)}, bf16[768,512]{1,0:T(8,128)(2,1)S(1)}, s32[84]{0:T(128)S(1)}, s32[10]{0:T(128)S(1)}) custom-call(s32[6,12]{1,0:T(8,128)} %refs_0_.1, s32[6,12]{1,0:T(8,128)} %refs_1_.1, s32[1]{0:T(128)S(6)} %copy.10.refs_2_, bf16[6,12,128,128]{3,2,1,0:T(8,128)(2,1)} %refs_3_.1), custom_call_target="tpu_custom_call" | custom-call | flops 1 | bytes 1 | tf_op jit(solution)/shard_map/spread_kernel/pallas_call | solution.py:305
  10.0 0.0 collective-permute-done.refs_1_
  10.0 1.5 %pack_kernel.1 = (bf16[512,512]{1,0:T(8,128)(2,1)S(1)}, bf16[512,512]{1,0:T(8,128)(2,1)S(1)}, s32[7]{0:T(128)S(1)}) custom-call(s32[10]{0:T(128)S(1)} %get-tuple-element.26.refs_0_.refs_1_, s32[6,12]{1,0:T(8,128)S(1)} %collective-permute-done.refs_1_, bf16[768,768]{1,0:T(8,128)(2,1)S(1)} %get-tuple-element.27.refs_2_.refs_4_, ...), custom_call_target="tpu_custom_call" | custom-call | flops 1 | bytes 1 | tf_op jit(solution)/shard_map/pack_kernel/pallas_call | solution.py:311
  11.5 2.8 %collective-permute-start.3 = (bf16[512,512]{1,0:T(8,128)(2,1)S(1)}, bf16[512,512]{1,0:T(8,128)(2,1)S(1)}, u32[]{:S(2)}, u32[]{:S(2)}) collective-permute-start(bf16[512,512]{1,0:T(8,128)(2,1)S(1)} %get-tuple-element.32), channel_id=1, source_target_pairs={{1,2},{3,4},{5,6},{7,8},{9,10},{11,12},{13,14},{15,0},{2,1},{4,3},... | collective-permute-start | bytes 1572872 | tf_op jit(solution)/shard_map/ppermute | solution.py:19
  14.3 0.0 copy-done
  14.3 0.0 collective-permute-start.1
  14.3 1.2 %collective-permute-done.1.refs_3_ = s32[6,12]{1,0:T(8,128)S(1)} collective-permute-done((s32[6,12]{1,0:T(8,128)S(1)}, s32[6,12]{1,0:T(8,128)S(1)}, u32[]{:S(2)}, u32[]{:S(2)}) %collective-permute-start.1) | collective-permute-done | bytes 320 | tf_op jit(solution)/shard_map/ppermute | solution.py:19
  15.5 0.0 collective-permute-done.2.refs_7_
  15.5 7.4 %own_kernel.1 = (bf16[6,12,128,128]{3,2,1,0:T(8,128)(2,1)}, f32[768,512]{1,0:T(8,128)S(1)}, f32[768,512]{1,0:T(8,128)S(1)}, bf16[512,512]{1,0:T(8,128)(2,1)S(1)}, f32[1]{0:T(128)}) custom-call(s32[84]{0:T(128)S(1)} %get-tuple-element.25.refs_0_, s32[10]{0:T(128)S(1)} %get-tuple-element.26.refs_0_.refs_1_, s32[7]{0:T(128)S(1)} %get-tuple-element.29.refs_2_, ...), custom_call_target="tpu_custom_call" | custom-call | flops 1 | bytes 1 | tf_op jit(solution)/shard_map/own_kernel/pallas_call | solution.py:317
  22.9 0.1 collective-permute-done.3.refs_4_.refs_5_
  23.0 1.5 %trace_kernel.1 = f32[8,128]{1,0:T(8,128)S(1)} custom-call(s32[84]{0:T(128)S(1)} %get-tuple-element.25.refs_0_, s32[10]{0:T(128)S(1)} %get-tuple-element.26.refs_0_.refs_1_, s32[7]{0:T(128)S(1)} %get-tuple-element.29.refs_2_, bf16[512,512]{1,0:T(8,128)(2,1)S(1)} %get-tuple-element.35.refs_3_, bf16[512,512]{1,0:T(8,128)(2,1)S(1)} %collective-permute-done.3.refs_4_.refs_5_, ...), custom_call_target="tpu_custom_call" | custom-call | flops 1 | bytes 1 | tf_op jit(solution)/shard_map/trace_kernel/pallas_call | solution.py:325
  24.5 2.8 %collective-permute-start.8 = (bf16[512,512]{1,0:T(8,128)(2,1)S(1)}, bf16[512,512]{1,0:T(8,128)(2,1)S(1)}, u32[]{:S(2)}, u32[]{:S(2)}) collective-permute-start(bf16[512,512]{1,0:T(8,128)(2,1)S(1)} %get-tuple-element.44), channel_id=1, source_target_pairs={{1,2},{3,4},{5,6},{7,8},{9,10},{11,12},{13,14},{15,0},{2,1},{4,3},... | collective-permute-start | bytes 1572872 | tf_op jit(solution)/shard_map/ppermute | solution.py:19
  27.3 0.0 collective-permute-start.4
  27.3 1.2 %collective-permute-done.4 = f32[8,128]{1,0:T(8,128)S(1)} collective-permute-done((f32[8,128]{1,0:T(8,128)S(1)}, f32[8,128]{1,0:T(8,128)S(1)}, u32[]{:S(2)}, u32[]{:S(2)}) %collective-permute-start.4) | collective-permute-done | bytes 4128 | tf_op jit(solution)/shard_map/ppermute | solution.py:19
  28.4 1.9 %far_kernel.1.refs_6_ = bf16[6,12,128,128]{3,2,1,0:T(8,128)(2,1)} custom-call(s32[84]{0:T(128)S(1)} %get-tuple-element.25.refs_0_, s32[10]{0:T(128)S(1)} %get-tuple-element.26.refs_0_.refs_1_, s32[7]{0:T(128)S(1)} %get-tuple-element.29.refs_2_, bf16[768,512]{1,0:T(8,128)(2,1)S(1)} %get-tuple-element.28.refs_3_.refs_5_, ...), custom_call_target="tpu_custom_call", output_to_operand_aliasing={{}: (6, {})} | custom-call | flops 1 | bytes 1 | tf_op jit(solution)/shard_map/far_kernel/pallas_call | solution.py:333
  30.3 0.1 collective-permute-start.5
  30.4 3.7 %collective-permute-done.5 = f32[8,128]{1,0:T(8,128)S(1)} collective-permute-done((f32[8,128]{1,0:T(8,128)S(1)}, f32[8,128]{1,0:T(8,128)S(1)}, u32[]{:S(2)}, u32[]{:S(2)}) %collective-permute-start.5) | collective-permute-done | bytes 4128 | tf_op jit(solution)/shard_map/ppermute | solution.py:19
  34.1 0.0 collective-permute-start.6
  34.1 4.5 %collective-permute-done.6 = f32[8,128]{1,0:T(8,128)S(1)} collective-permute-done((f32[8,128]{1,0:T(8,128)S(1)}, f32[8,128]{1,0:T(8,128)S(1)}, u32[]{:S(2)}, u32[]{:S(2)}) %collective-permute-start.6) | collective-permute-done | bytes 4128 | tf_op jit(solution)/shard_map/ppermute | solution.py:19
  38.6 0.0 collective-permute-start.7
  38.6 0.0 collective-permute-done.8.refs_5_
  38.6 1.9 %last_kernel.1 = bf16[6,12,128,128]{3,2,1,0:T(8,128)(2,1)} custom-call(s32[84]{0:T(128)S(1)} %get-tuple-element.25.refs_0_, s32[10]{0:T(128)S(1)} %get-tuple-element.26.refs_0_.refs_1_, s32[7]{0:T(128)S(1)} %get-tuple-element.29.refs_2_, bf16[768,512]{1,0:T(8,128)(2,1)S(1)} %get-tuple-element.28.refs_3_.refs_5_, ...), custom_call_target="tpu_custom_call", output_to_operand_aliasing={{}: (6, {})} | custom-call | flops 1 | bytes 1 | tf_op jit(solution)/shard_map/last_kernel/pallas_call | solution.py:333
  40.5 1.1 %collective-permute-done.7 = f32[8,128]{1,0:T(8,128)S(1)} collective-permute-done((f32[8,128]{1,0:T(8,128)S(1)}, f32[8,128]{1,0:T(8,128)S(1)}, u32[]{:S(2)}, u32[]{:S(2)}) %collective-permute-start.7) | collective-permute-done | bytes 4128 | tf_op jit(solution)/shard_map/ppermute | solution.py:19
  41.6 0.5 %slice.3 = f32[1,1]{1,0:T(1,128)} slice(f32[8,128]{1,0:T(8,128)S(1)} %add.15), slice={[0:1], [0:1]} | slice | bytes 8 | tf_op jit(solution)/shard_map/slice | solution.py:351
  (4 shorter events, 0.0 us)
Async XLA Ops:
  0.6 13.7 %copy-start = (s32[6,12]{1,0:T(8,128)S(1)}, s32[6,12]{1,0:T(8,128)}, u32[]{:S(2)}) copy-start(s32[6,12]{1,0:T(8,128)} %refs_0_.1) | copy-start | bytes 868
  0.6 14.8 %collective-permute-start.2 = (bf16[6,12,128,128]{3,2,1,0:T(8,128)(2,1)}, bf16[6,12,128,128]{3,2,1,0:T(8,128)(2,1)S(1)}, u32[]{:S(2)}, u32[]{:S(2)}) collective-permute-start(bf16[6,12,128,128]{3,2,1,0:T(8,128)(2,1)} %refs_3_.1), channel_id=1, source_target_pairs={{0,1},{1,0},{2,3},{3,2},{4,5},{5,4},{6,7},{7,6},{8,9},{9,8},{10,11... | collective-permute-start | bytes 7077896 | tf_op jit(solution)/shard_map/ppermute | solution.py:19
  1.2 8.8 %collective-permute-start = (s32[6,12]{1,0:T(8,128)}, s32[6,12]{1,0:T(8,128)S(1)}, u32[]{:S(2)}, u32[]{:S(2)}) collective-permute-start(s32[6,12]{1,0:T(8,128)} %refs_0_.1), channel_id=1, source_target_pairs={{1,2},{3,4},{5,6},{7,8},{9,10},{11,12},{13,14},{15,0},{2,1},{4,3},... | collective-permute-start | bytes 872 | tf_op jit(solution)/shard_map/ppermute | solution.py:19
  11.5 11.5 %collective-permute-start.3 = (bf16[512,512]{1,0:T(8,128)(2,1)S(1)}, bf16[512,512]{1,0:T(8,128)(2,1)S(1)}, u32[]{:S(2)}, u32[]{:S(2)}) collective-permute-start(bf16[512,512]{1,0:T(8,128)(2,1)S(1)} %get-tuple-element.32), channel_id=1, source_target_pairs={{1,2},{3,4},{5,6},{7,8},{9,10},{11,12},{13,14},{15,0},{2,1},{4,3},... | collective-permute-start | bytes 1572872 | tf_op jit(solution)/shard_map/ppermute | solution.py:19
  14.3 1.2 %collective-permute-start.1 = (s32[6,12]{1,0:T(8,128)S(1)}, s32[6,12]{1,0:T(8,128)S(1)}, u32[]{:S(2)}, u32[]{:S(2)}) collective-permute-start(s32[6,12]{1,0:T(8,128)S(1)} %copy-done), channel_id=1, source_target_pairs={{0,1},{1,0},{2,3},{3,2},{4,5},{5,4},{6,7},{7,6},{8,9},{9,8},{10,11... | collective-permute-start | bytes 872 | tf_op jit(solution)/shard_map/ppermute | solution.py:19
  24.5 14.1 %collective-permute-start.8 = (bf16[512,512]{1,0:T(8,128)(2,1)S(1)}, bf16[512,512]{1,0:T(8,128)(2,1)S(1)}, u32[]{:S(2)}, u32[]{:S(2)}) collective-permute-start(bf16[512,512]{1,0:T(8,128)(2,1)S(1)} %get-tuple-element.44), channel_id=1, source_target_pairs={{1,2},{3,4},{5,6},{7,8},{9,10},{11,12},{13,14},{15,0},{2,1},{4,3},... | collective-permute-start | bytes 1572872 | tf_op jit(solution)/shard_map/ppermute | solution.py:19
  27.3 1.2 %collective-permute-start.4 = (f32[8,128]{1,0:T(8,128)S(1)}, f32[8,128]{1,0:T(8,128)S(1)}, u32[]{:S(2)}, u32[]{:S(2)}) collective-permute-start(f32[8,128]{1,0:T(8,128)S(1)} %trace_kernel.1), channel_id=1, source_target_pairs={{0,1},{1,0},{2,3},{3,2},{4,5},{5,4},{6,7},{7,6},{8,9},{9,8},{10,11... | collective-permute-start | bytes 12296 | tf_op jit(solution)/shard_map/ppermute | solution.py:19
  30.3 3.8 %collective-permute-start.5 = (f32[8,128]{1,0:T(8,128)S(1)}, f32[8,128]{1,0:T(8,128)S(1)}, u32[]{:S(2)}, u32[]{:S(2)}) collective-permute-start(f32[8,128]{1,0:T(8,128)S(1)} %add.12), channel_id=1, source_target_pairs={{0,4},{1,5},{2,6},{3,7},{4,0},{5,1},{6,2},{7,3},{8,12},{9,13},{10,... | collective-permute-start | bytes 12296 | tf_op jit(solution)/shard_map/ppermute | solution.py:19
  34.1 4.5 %collective-permute-start.6 = (f32[8,128]{1,0:T(8,128)S(1)}, f32[8,128]{1,0:T(8,128)S(1)}, u32[]{:S(2)}, u32[]{:S(2)}) collective-permute-start(f32[8,128]{1,0:T(8,128)S(1)} %add.13), channel_id=1, source_target_pairs={{0,8},{1,9},{2,10},{3,11},{4,12},{5,13},{6,14},{7,15},{8,0},{9,1},... | collective-permute-start | bytes 12296 | tf_op jit(solution)/shard_map/ppermute | solution.py:19
  38.6 3.0 %collective-permute-start.7 = (f32[8,128]{1,0:T(8,128)S(1)}, f32[8,128]{1,0:T(8,128)S(1)}, u32[]{:S(2)}, u32[]{:S(2)}) collective-permute-start(f32[8,128]{1,0:T(8,128)S(1)} %add.14), channel_id=1, source_target_pairs={{0,3},{1,2},{2,1},{3,0},{4,7},{5,6},{6,5},{7,4},{8,11},{9,10},{10,... | collective-permute-start | bytes 12296 | tf_op jit(solution)/shard_map/ppermute | solution.py:19

commit v6 on v5

--- a/solution.py
+++ b/solution.py
@@ -185,7 +185,8 @@
     for r in range(CAP):
         for c in range(CAP):
             value = outer[pl.ds(pl.multiple_of(asked[c] * block, block), block), pl.ds(r * block, block)]
-            turned[pl.ds(r * block, block), pl.ds(c * block, block)] = value.T
+            weight = sign * kept(table[asked[c] * across + asked[c]])
+            turned[pl.ds(r * block, block), pl.ds(c * block, block)] = (value * weight.astype(value.dtype)).T
     for copy in arrive:
         copy.wait()
     for r in range(CAP):
@@ -225,17 +226,11 @@
         wait()
 
 
-def trace_kernel(rows, table, meta, asked, turned, far, trace_own, trace):
-    block = turned.shape[0] // CAP
-    across = rows + 2 * CAP
-    total = jnp.zeros((8, block), jnp.float32)
-    for c in range(CAP):
-        mine = asked[c]
-        column = pl.ds(c * block, block)
-        part = far[:, column].astype(jnp.float32) * turned[:, column].astype(jnp.float32)
-        total = total + kept(table[mine * across + mine]) * jnp.sum(part.reshape(CAP * block // 8, 8, block), axis=0)
-    value = (trace_own[0] + signs(meta)[1] * jnp.sum(total)) * (1.0 / total_count(rows, block))
-    trace[...] = jnp.full(trace.shape, value, jnp.float32)
+def trace_kernel(rows, turned, far, trace_own, trace):
+    tall, block = turned.shape[0], turned.shape[0] // CAP
+    part = far[...].astype(jnp.float32) * turned[...].astype(jnp.float32)
+    value = trace_own[0] + jnp.sum(jnp.sum(part.reshape(tall // 8, 8, tall), axis=0))
+    trace[...] = jnp.full(trace.shape, value * (1.0 / total_count(rows, block)), jnp.float32)
 
 
 def total_count(rows, block):
@@ -323,8 +318,7 @@
          pltpu.VMEM((wide, narrow), f32), pltpu.VMEM((rows, rows, block, block), bf16), ints(rows * (2 * rows + 1)),
          ints(CAP + 1), dma, dma], 24)(table, meta, asked, cols_inner, own, outer, inner, x_inner)
     partial, = call(
-        trace_kernel, [((8, block), f32, VMEM)], [SMEM] * 3 + [VMEM, VMEM, SMEM],
-        [], 12, first=rows)(table, meta, asked, turned, far, trace_own)
+        trace_kernel, [((8, block), f32, VMEM)], [VMEM, VMEM, SMEM], [], 12, first=rows)(turned, far, trace_own)
     near_out, partial = barrier((near_out, partial))
     near = permute(near_out, outside)
     half_scratch = [pltpu.VMEM((rows, CAP, block, block), bf16), dma]

time: 42.3 us -> 41.7 us (0.986)
  Pallas kernels: 16.7 us -> 16.1 us
    pallas_call x1, Pallas kernels: 1.47 us -> 0.82 us  [body(): call(trace_kernel, [((8, block), f32, VMEM)], [VMEM, VMEM, SMEM], [], 12,...]
  transfers between devices with their start and end apart: 9 -> 9, of which waited for: 6 -> 6; matrix products, arithmetic and copies ran while one was open for 0% -> 0% of each run, Pallas kernels for 36% -> 37%
where the time goes in v6:
time: 41.7 us; the launch traced here: 41.5 us
  Pallas kernels  16.1 us (39%)
  starting transfers between devices  11.8 us (28%)
  waiting for transfers between devices  11.7 us (28%)
  between operations  1.37 us (3%)
  local copies, waits for them, and re-layouts  0.52 us (1%)
    ppermute x9, starting transfers between devices, permute(): return lax.ppermute(value, RING, pairs)  11.8 us
    ppermute x9, waiting for transfers between devices, permute(): return lax.ppermute(value, RING, pairs)  11.7 us
    pallas_call x1, Pallas kernels, body(): call(own_kernel, [(x.shape, bf16, HBM), ((wide, narrow), f32, VMEM), ((wi...  7.45 us
    pallas_call x2, Pallas kernels, half(): call(kernel, [(x.shape, bf16, HBM)], [SMEM] * 3 + [VMEM] * 3 + [HBM], hal...  3.76 us
    pallas_call x1, Pallas kernels, body(): call(spread_kernel, [((wide, wide), bf16, VMEM), ((wide, narrow), bf16, V...  2.55 us
    pallas_call x1, Pallas kernels, body(): call(pack_kernel, [((narrow, narrow), bf16, VMEM), ((narrow, narrow), bf1...  1.5 us
  transfers between devices with their start and end apart: 9, of which 6 were waited for; matrix products, arithmetic and copies ran while one was open for 0% of the time, Pallas kernels for 37%

profile of v6, /device:TPU:0, one launch (start us, length us, event | category | flops | bytes accessed | tf_op | source)
XLA Modules:
  0.0 41.5 jit_solution(8925423855822060423)
XLA Ops:
  0.6 0.0 copy-start
  0.6 0.5 %collective-permute-start.2 = (bf16[6,12,128,128]{3,2,1,0:T(8,128)(2,1)}, bf16[6,12,128,128]{3,2,1,0:T(8,128)(2,1)S(1)}, u32[]{:S(2)}, u32[]{:S(2)}) collective-permute-start(bf16[6,12,128,128]{3,2,1,0:T(8,128)(2,1)} %refs_3_.1), channel_id=1, source_target_pairs={{0,1},{1,0},{2,3},{3,2},{4,5},{5,4},{6,7},{7,6},{8,9},{9,8},{10,11... | collective-permute-start | bytes 7077896 | tf_op jit(solution)/shard_map/ppermute | solution.py:19
  1.2 5.6 %collective-permute-start = (s32[6,12]{1,0:T(8,128)}, s32[6,12]{1,0:T(8,128)S(1)}, u32[]{:S(2)}, u32[]{:S(2)}) collective-permute-start(s32[6,12]{1,0:T(8,128)} %refs_0_.1), channel_id=1, source_target_pairs={{1,2},{3,4},{5,6},{7,8},{9,10},{11,12},{13,14},{15,0},{2,1},{4,3},... | collective-permute-start | bytes 872 | tf_op jit(solution)/shard_map/ppermute | solution.py:19
  7.4 2.5 %spread_kernel.1 = (bf16[768,768]{1,0:T(8,128)(2,1)S(1)}, bf16[768,512]{1,0:T(8,128)(2,1)S(1)}, bf16[768,512]{1,0:T(8,128)(2,1)S(1)}, s32[84]{0:T(128)S(1)}, s32[10]{0:T(128)S(1)}) custom-call(s32[6,12]{1,0:T(8,128)} %refs_0_.1, s32[6,12]{1,0:T(8,128)} %refs_1_.1, s32[1]{0:T(128)S(6)} %copy.10.refs_2_, bf16[6,12,128,128]{3,2,1,0:T(8,128)(2,1)} %refs_3_.1), custom_call_target="tpu_custom_call" | custom-call | flops 1 | bytes 1 | tf_op jit(solution)/shard_map/spread_kernel/pallas_call | solution.py:300
  10.0 0.0 collective-permute-done.refs_1_
  10.0 1.5 %pack_kernel.1 = (bf16[512,512]{1,0:T(8,128)(2,1)S(1)}, bf16[512,512]{1,0:T(8,128)(2,1)S(1)}, s32[7]{0:T(128)S(1)}) custom-call(s32[10]{0:T(128)S(1)} %get-tuple-element.26.refs_0_.refs_1_, s32[6,12]{1,0:T(8,128)S(1)} %collective-permute-done.refs_1_, bf16[768,768]{1,0:T(8,128)(2,1)S(1)} %get-tuple-element.27.refs_2_.refs_4_, ...), custom_call_target="tpu_custom_call" | custom-call | flops 1 | bytes 1 | tf_op jit(solution)/shard_map/pack_kernel/pallas_call | solution.py:306
  11.5 2.8 %collective-permute-start.3 = (bf16[512,512]{1,0:T(8,128)(2,1)S(1)}, bf16[512,512]{1,0:T(8,128)(2,1)S(1)}, u32[]{:S(2)}, u32[]{:S(2)}) collective-permute-start(bf16[512,512]{1,0:T(8,128)(2,1)S(1)} %get-tuple-element.32), channel_id=1, source_target_pairs={{1,2},{3,4},{5,6},{7,8},{9,10},{11,12},{13,14},{15,0},{2,1},{4,3},... | collective-permute-start | bytes 1572872 | tf_op jit(solution)/shard_map/ppermute | solution.py:19
  14.3 0.0 copy-done
  14.3 0.0 collective-permute-start.1
  14.3 1.2 %collective-permute-done.1.refs_3_ = s32[6,12]{1,0:T(8,128)S(1)} collective-permute-done((s32[6,12]{1,0:T(8,128)S(1)}, s32[6,12]{1,0:T(8,128)S(1)}, u32[]{:S(2)}, u32[]{:S(2)}) %collective-permute-start.1) | collective-permute-done | bytes 320 | tf_op jit(solution)/shard_map/ppermute | solution.py:19
  15.5 0.0 collective-permute-done.2.refs_7_
  15.5 7.4 %own_kernel.1 = (bf16[6,12,128,128]{3,2,1,0:T(8,128)(2,1)}, f32[768,512]{1,0:T(8,128)S(1)}, f32[768,512]{1,0:T(8,128)S(1)}, bf16[512,512]{1,0:T(8,128)(2,1)S(1)}, f32[1]{0:T(128)}) custom-call(s32[84]{0:T(128)S(1)} %get-tuple-element.25.refs_0_, s32[10]{0:T(128)S(1)} %get-tuple-element.26.refs_0_.refs_1_, s32[7]{0:T(128)S(1)} %get-tuple-element.29.refs_2_, ...), custom_call_target="tpu_custom_call" | custom-call | flops 1 | bytes 1 | tf_op jit(solution)/shard_map/own_kernel/pallas_call | solution.py:312
  22.9 0.1 collective-permute-done.3.refs_1_.refs_5_
  23.0 0.8 %trace_kernel.1 = f32[8,128]{1,0:T(8,128)S(1)} custom-call(bf16[512,512]{1,0:T(8,128)(2,1)S(1)} %get-tuple-element.35.refs_0_, bf16[512,512]{1,0:T(8,128)(2,1)S(1)} %collective-permute-done.3.refs_1_.refs_5_, f32[1]{0:T(128)} %get-tuple-element.36.refs_2_), custom_call_target="tpu_custom_call" | custom-call | flops 1 | bytes 1 | tf_op jit(solution)/shard_map/trace_kernel/pallas_call | solution.py:320
  23.8 2.8 %collective-permute-start.8 = (bf16[512,512]{1,0:T(8,128)(2,1)S(1)}, bf16[512,512]{1,0:T(8,128)(2,1)S(1)}, u32[]{:S(2)}, u32[]{:S(2)}) collective-permute-start(bf16[512,512]{1,0:T(8,128)(2,1)S(1)} %get-tuple-element.44), channel_id=1, source_target_pairs={{1,2},{3,4},{5,6},{7,8},{9,10},{11,12},{13,14},{15,0},{2,1},{4,3},... | collective-permute-start | bytes 1572872 | tf_op jit(solution)/shard_map/ppermute | solution.py:19
  26.6 0.0 collective-permute-start.4
  26.6 1.2 %collective-permute-done.4 = f32[8,128]{1,0:T(8,128)S(1)} collective-permute-done((f32[8,128]{1,0:T(8,128)S(1)}, f32[8,128]{1,0:T(8,128)S(1)}, u32[]{:S(2)}, u32[]{:S(2)}) %collective-permute-start.4) | collective-permute-done | bytes 4128 | tf_op jit(solution)/shard_map/ppermute | solution.py:19
  27.8 1.9 %far_kernel.1.refs_6_ = bf16[6,12,128,128]{3,2,1,0:T(8,128)(2,1)} custom-call(s32[84]{0:T(128)S(1)} %get-tuple-element.25.refs_0_, s32[10]{0:T(128)S(1)} %get-tuple-element.26.refs_0_.refs_1_, s32[7]{0:T(128)S(1)} %get-tuple-element.29.refs_2_, bf16[768,512]{1,0:T(8,128)(2,1)S(1)} %get-tuple-element.28.refs_3_.refs_5_, ...), custom_call_target="tpu_custom_call", output_to_operand_aliasing={{}: (6, {})} | custom-call | flops 1 | bytes 1 | tf_op jit(solution)/shard_map/far_kernel/pallas_call | solution.py:327
  29.7 0.1 collective-permute-start.5
  29.7 3.7 %collective-permute-done.5 = f32[8,128]{1,0:T(8,128)S(1)} collective-permute-done((f32[8,128]{1,0:T(8,128)S(1)}, f32[8,128]{1,0:T(8,128)S(1)}, u32[]{:S(2)}, u32[]{:S(2)}) %collective-permute-start.5) | collective-permute-done | bytes 4128 | tf_op jit(solution)/shard_map/ppermute | solution.py:19
  33.4 0.0 collective-permute-start.6
  33.4 4.5 %collective-permute-done.6 = f32[8,128]{1,0:T(8,128)S(1)} collective-permute-done((f32[8,128]{1,0:T(8,128)S(1)}, f32[8,128]{1,0:T(8,128)S(1)}, u32[]{:S(2)}, u32[]{:S(2)}) %collective-permute-start.6) | collective-permute-done | bytes 4128 | tf_op jit(solution)/shard_map/ppermute | solution.py:19
  38.0 0.0 collective-permute-start.7
  38.0 0.0 collective-permute-done.8.refs_5_
  38.0 1.9 %last_kernel.1 = bf16[6,12,128,128]{3,2,1,0:T(8,128)(2,1)} custom-call(s32[84]{0:T(128)S(1)} %get-tuple-element.25.refs_0_, s32[10]{0:T(128)S(1)} %get-tuple-element.26.refs_0_.refs_1_, s32[7]{0:T(128)S(1)} %get-tuple-element.29.refs_2_, bf16[768,512]{1,0:T(8,128)(2,1)S(1)} %get-tuple-element.28.refs_3_.refs_5_, ...), custom_call_target="tpu_custom_call", output_to_operand_aliasing={{}: (6, {})} | custom-call | flops 1 | bytes 1 | tf_op jit(solution)/shard_map/last_kernel/pallas_call | solution.py:327
  39.9 1.1 %collective-permute-done.7 = f32[8,128]{1,0:T(8,128)S(1)} collective-permute-done((f32[8,128]{1,0:T(8,128)S(1)}, f32[8,128]{1,0:T(8,128)S(1)}, u32[]{:S(2)}, u32[]{:S(2)}) %collective-permute-start.7) | collective-permute-done | bytes 4128 | tf_op jit(solution)/shard_map/ppermute | solution.py:19
  41.0 0.5 %slice.3 = f32[1,1]{1,0:T(1,128)} slice(f32[8,128]{1,0:T(8,128)S(1)} %add.15), slice={[0:1], [0:1]} | slice | bytes 8 | tf_op jit(solution)/shard_map/slice | solution.py:345
  (4 shorter events, 0.0 us)
Async XLA Ops:
  0.6 13.7 %copy-start = (s32[6,12]{1,0:T(8,128)S(1)}, s32[6,12]{1,0:T(8,128)}, u32[]{:S(2)}) copy-start(s32[6,12]{1,0:T(8,128)} %refs_0_.1) | copy-start | bytes 868
  0.6 14.8 %collective-permute-start.2 = (bf16[6,12,128,128]{3,2,1,0:T(8,128)(2,1)}, bf16[6,12,128,128]{3,2,1,0:T(8,128)(2,1)S(1)}, u32[]{:S(2)}, u32[]{:S(2)}) collective-permute-start(bf16[6,12,128,128]{3,2,1,0:T(8,128)(2,1)} %refs_3_.1), channel_id=1, source_target_pairs={{0,1},{1,0},{2,3},{3,2},{4,5},{5,4},{6,7},{7,6},{8,9},{9,8},{10,11... | collective-permute-start | bytes 7077896 | tf_op jit(solution)/shard_map/ppermute | solution.py:19
  1.2 8.8 %collective-permute-start = (s32[6,12]{1,0:T(8,128)}, s32[6,12]{1,0:T(8,128)S(1)}, u32[]{:S(2)}, u32[]{:S(2)}) collective-permute-start(s32[6,12]{1,0:T(8,128)} %refs_0_.1), channel_id=1, source_target_pairs={{1,2},{3,4},{5,6},{7,8},{9,10},{11,12},{13,14},{15,0},{2,1},{4,3},... | collective-permute-start | bytes 872 | tf_op jit(solution)/shard_map/ppermute | solution.py:19
  11.5 11.5 %collective-permute-start.3 = (bf16[512,512]{1,0:T(8,128)(2,1)S(1)}, bf16[512,512]{1,0:T(8,128)(2,1)S(1)}, u32[]{:S(2)}, u32[]{:S(2)}) collective-permute-start(bf16[512,512]{1,0:T(8,128)(2,1)S(1)} %get-tuple-element.32), channel_id=1, source_target_pairs={{1,2},{3,4},{5,6},{7,8},{9,10},{11,12},{13,14},{15,0},{2,1},{4,3},... | collective-permute-start | bytes 1572872 | tf_op jit(solution)/shard_map/ppermute | solution.py:19
  14.3 1.2 %collective-permute-start.1 = (s32[6,12]{1,0:T(8,128)S(1)}, s32[6,12]{1,0:T(8,128)S(1)}, u32[]{:S(2)}, u32[]{:S(2)}) collective-permute-start(s32[6,12]{1,0:T(8,128)S(1)} %copy-done), channel_id=1, source_target_pairs={{0,1},{1,0},{2,3},{3,2},{4,5},{5,4},{6,7},{7,6},{8,9},{9,8},{10,11... | collective-permute-start | bytes 872 | tf_op jit(solution)/shard_map/ppermute | solution.py:19
  23.8 14.1 %collective-permute-start.8 = (bf16[512,512]{1,0:T(8,128)(2,1)S(1)}, bf16[512,512]{1,0:T(8,128)(2,1)S(1)}, u32[]{:S(2)}, u32[]{:S(2)}) collective-permute-start(bf16[512,512]{1,0:T(8,128)(2,1)S(1)} %get-tuple-element.44), channel_id=1, source_target_pairs={{1,2},{3,4},{5,6},{7,8},{9,10},{11,12},{13,14},{15,0},{2,1},{4,3},... | collective-permute-start | bytes 1572872 | tf_op jit(solution)/shard_map/ppermute | solution.py:19
  26.6 1.2 %collective-permute-start.4 = (f32[8,128]{1,0:T(8,128)S(1)}, f32[8,128]{1,0:T(8,128)S(1)}, u32[]{:S(2)}, u32[]{:S(2)}) collective-permute-start(f32[8,128]{1,0:T(8,128)S(1)} %trace_kernel.1), channel_id=1, source_target_pairs={{0,1},{1,0},{2,3},{3,2},{4,5},{5,4},{6,7},{7,6},{8,9},{9,8},{10,11... | collective-permute-start | bytes 12296 | tf_op jit(solution)/shard_map/ppermute | solution.py:19
  29.7 3.8 %collective-permute-start.5 = (f32[8,128]{1,0:T(8,128)S(1)}, f32[8,128]{1,0:T(8,128)S(1)}, u32[]{:S(2)}, u32[]{:S(2)}) collective-permute-start(f32[8,128]{1,0:T(8,128)S(1)} %add.12), channel_id=1, source_target_pairs={{0,4},{1,5},{2,6},{3,7},{4,0},{5,1},{6,2},{7,3},{8,12},{9,13},{10,... | collective-permute-start | bytes 12296 | tf_op jit(solution)/shard_map/ppermute | solution.py:19
  33.4 4.5 %collective-permute-start.6 = (f32[8,128]{1,0:T(8,128)S(1)}, f32[8,128]{1,0:T(8,128)S(1)}, u32[]{:S(2)}, u32[]{:S(2)}) collective-permute-start(f32[8,128]{1,0:T(8,128)S(1)} %add.13), channel_id=1, source_target_pairs={{0,8},{1,9},{2,10},{3,11},{4,12},{5,13},{6,14},{7,15},{8,0},{9,1},... | collective-permute-start | bytes 12296 | tf_op jit(solution)/shard_map/ppermute | solution.py:19
  38.0 3.0 %collective-permute-start.7 = (f32[8,128]{1,0:T(8,128)S(1)}, f32[8,128]{1,0:T(8,128)S(1)}, u32[]{:S(2)}, u32[]{:S(2)}) collective-permute-start(f32[8,128]{1,0:T(8,128)S(1)} %add.14), channel_id=1, source_target_pairs={{0,3},{1,2},{2,1},{3,0},{4,7},{5,6},{6,5},{7,4},{8,11},{9,10},{10,... | collective-permute-start | bytes 12296 | tf_op jit(solution)/shard_map/ppermute | solution.py:19

commit v7 on v6

--- a/solution.py
+++ b/solution.py
@@ -78,6 +78,7 @@
         meta[c] = order[c + c // CAP]
     meta[2 * CAP] = base
     meta[2 * CAP + 1] = flag[0]
+    table[rows * across] = flag[0]
     for i in range(rows):
         span = pl.ds(i * block, block)
         blocks[i].wait()
@@ -237,10 +238,10 @@
     return rows * block * lax.axis_size(RING)
 
 
-def finish_half(near, rows, table, meta, asked, outer, base, got, out, stage, sem):
+def finish_half(near, rows, table, asked, outer, base, got, out, stage, sem):
     block = outer.shape[0] // rows
     across = rows + 2 * CAP
-    right = got[...] * signs(meta)[1].astype(got.dtype)
+    right = got[...] * jnp.where(table[rows * across] == 1, 1.0, -1.0).astype(got.dtype)
     waits = []
     chunk = rows // 2
     for first in range(0, rows, chunk):
@@ -259,12 +260,12 @@
         wait()
 
 
-def far_kernel(rows, table, meta, asked, outer, base, far, _, out, *scratch):
-    finish_half(False, rows, table, meta, asked, outer, base, far, out, *scratch)
-
-
-def last_kernel(rows, table, meta, asked, outer, base, near, _, out, *scratch):
-    finish_half(True, rows, table, meta, asked, outer, base, near, out, *scratch)
+def far_kernel(rows, table, asked, outer, base, far, _, out, *scratch):
+    finish_half(False, rows, table, asked, outer, base, far, out, *scratch)
+
+
+def last_kernel(rows, table, asked, outer, base, near, _, out, *scratch):
+    finish_half(True, rows, table, asked, outer, base, near, out, *scratch)
 
 
 def body(x, cols, keep, flag):
@@ -300,7 +301,7 @@
     own, outer, inner, table, meta = call(
         spread_kernel,
         [((wide, wide), bf16, VMEM), ((wide, narrow), bf16, VMEM), ((wide, narrow), bf16, VMEM),
-         ((rows * across,), i32, SMEM), ((2 * CAP + 2,), i32, SMEM)],
+         ((rows * across + 1,), i32, SMEM), ((2 * CAP + 2,), i32, SMEM)],
         [HBM] * 2 + [SMEM, HBM], [ints(rows, slots), ints(rows, slots), pltpu.VMEM(x.shape, bf16), ints(rows * 3 * rows),
                     ints(2 * (CAP + 1)), dma((2 + rows,))], 16, first=total_rows)(hbm(cols), hbm(keep), flag, hbm(x))
     far_out, near_out, asked = call(
@@ -325,8 +326,8 @@
 
     def half(kernel, base, got, out):
         result, = call(
-            kernel, [(x.shape, bf16, HBM)], [SMEM] * 3 + [VMEM] * 3 + [HBM], half_scratch, 16, {6: 0}, first=rows,
-        )(table, meta, asked, outer, base, got, out)
+            kernel, [(x.shape, bf16, HBM)], [SMEM] * 2 + [VMEM] * 3 + [HBM], half_scratch, 16, {5: 0}, first=rows,
+        )(table, asked, outer, base, got, out)
         return result
 
     steps = ring_steps()

time: 41.7 us -> 41.7 us (level)
  no operation moved by 1% of the time
where the time goes in v7:
time: 41.7 us; the launch traced here: 41.5 us
  Pallas kernels  16.1 us (39%)
  starting transfers between devices  11.8 us (28%)
  waiting for transfers between devices  11.7 us (28%)
  between operations  1.37 us (3%)
  local copies, waits for them, and re-layouts  0.52 us (1%)
    ppermute x9, starting transfers between devices, permute(): return lax.ppermute(value, RING, pairs)  11.8 us
    ppermute x9, waiting for transfers between devices, permute(): return lax.ppermute(value, RING, pairs)  11.7 us
    pallas_call x1, Pallas kernels, body(): call(own_kernel, [(x.shape, bf16, HBM), ((wide, narrow), f32, VMEM), ((wi...  7.46 us
    pallas_call x2, Pallas kernels, half(): call(kernel, [(x.shape, bf16, HBM)], [SMEM] * 2 + [VMEM] * 3 + [HBM], hal...  3.73 us
    pallas_call x1, Pallas kernels, body(): call(spread_kernel, [((wide, wide), bf16, VMEM), ((wide, narrow), bf16, V...  2.55 us
    pallas_call x1, Pallas kernels, body(): call(pack_kernel, [((narrow, narrow), bf16, VMEM), ((narrow, narrow), bf1...  1.5 us
  transfers between devices with their start and end apart: 9, of which 6 were waited for; matrix products, arithmetic and copies ran while one was open for 0% of the time, Pallas kernels for 37%

profile of v7, /device:TPU:0, one launch (start us, length us, event | category | flops | bytes accessed | tf_op | source)
XLA Modules:
  0.0 41.5 jit_solution(6433694417987765570)
XLA Ops:
  0.6 0.0 copy-start
  0.6 0.5 %collective-permute-start.2 = (bf16[6,12,128,128]{3,2,1,0:T(8,128)(2,1)}, bf16[6,12,128,128]{3,2,1,0:T(8,128)(2,1)S(1)}, u32[]{:S(2)}, u32[]{:S(2)}) collective-permute-start(bf16[6,12,128,128]{3,2,1,0:T(8,128)(2,1)} %refs_3_.1), channel_id=1, source_target_pairs={{0,1},{1,0},{2,3},{3,2},{4,5},{5,4},{6,7},{7,6},{8,9},{9,8},{10,11... | collective-permute-start | bytes 7077896 | tf_op jit(solution)/shard_map/ppermute | solution.py:19
  1.2 5.6 %collective-permute-start = (s32[6,12]{1,0:T(8,128)}, s32[6,12]{1,0:T(8,128)S(1)}, u32[]{:S(2)}, u32[]{:S(2)}) collective-permute-start(s32[6,12]{1,0:T(8,128)} %refs_0_.1), channel_id=1, source_target_pairs={{1,2},{3,4},{5,6},{7,8},{9,10},{11,12},{13,14},{15,0},{2,1},{4,3},... | collective-permute-start | bytes 872 | tf_op jit(solution)/shard_map/ppermute | solution.py:19
  7.4 2.5 %spread_kernel.1 = (bf16[768,768]{1,0:T(8,128)(2,1)S(1)}, bf16[768,512]{1,0:T(8,128)(2,1)S(1)}, bf16[768,512]{1,0:T(8,128)(2,1)S(1)}, s32[85]{0:T(128)S(1)}, s32[10]{0:T(128)S(1)}) custom-call(s32[6,12]{1,0:T(8,128)} %refs_0_.1, s32[6,12]{1,0:T(8,128)} %refs_1_.1, s32[1]{0:T(128)S(6)} %copy.10.refs_2_, bf16[6,12,128,128]{3,2,1,0:T(8,128)(2,1)} %refs_3_.1), custom_call_target="tpu_custom_call" | custom-call | flops 1 | bytes 1 | tf_op jit(solution)/shard_map/spread_kernel/pallas_call | solution.py:301
  10.0 0.0 collective-permute-done.refs_1_
  10.0 1.5 %pack_kernel.1 = (bf16[512,512]{1,0:T(8,128)(2,1)S(1)}, bf16[512,512]{1,0:T(8,128)(2,1)S(1)}, s32[7]{0:T(128)S(1)}) custom-call(s32[10]{0:T(128)S(1)} %get-tuple-element.26.refs_0_.refs_1_, s32[6,12]{1,0:T(8,128)S(1)} %collective-permute-done.refs_1_, bf16[768,768]{1,0:T(8,128)(2,1)S(1)} %get-tuple-element.27.refs_2_.refs_4_, ...), custom_call_target="tpu_custom_call" | custom-call | flops 1 | bytes 1 | tf_op jit(solution)/shard_map/pack_kernel/pallas_call | solution.py:307
  11.5 2.8 %collective-permute-start.3 = (bf16[512,512]{1,0:T(8,128)(2,1)S(1)}, bf16[512,512]{1,0:T(8,128)(2,1)S(1)}, u32[]{:S(2)}, u32[]{:S(2)}) collective-permute-start(bf16[512,512]{1,0:T(8,128)(2,1)S(1)} %get-tuple-element.32), channel_id=1, source_target_pairs={{1,2},{3,4},{5,6},{7,8},{9,10},{11,12},{13,14},{15,0},{2,1},{4,3},... | collective-permute-start | bytes 1572872 | tf_op jit(solution)/shard_map/ppermute | solution.py:19
  14.3 0.0 copy-done
  14.3 0.0 collective-permute-start.1
  14.3 1.2 %collective-permute-done.1.refs_3_ = s32[6,12]{1,0:T(8,128)S(1)} collective-permute-done((s32[6,12]{1,0:T(8,128)S(1)}, s32[6,12]{1,0:T(8,128)S(1)}, u32[]{:S(2)}, u32[]{:S(2)}) %collective-permute-start.1) | collective-permute-done | bytes 320 | tf_op jit(solution)/shard_map/ppermute | solution.py:19
  15.5 0.0 collective-permute-done.2.refs_7_
  15.5 7.5 %own_kernel.1 = (bf16[6,12,128,128]{3,2,1,0:T(8,128)(2,1)}, f32[768,512]{1,0:T(8,128)S(1)}, f32[768,512]{1,0:T(8,128)S(1)}, bf16[512,512]{1,0:T(8,128)(2,1)S(1)}, f32[1]{0:T(128)}) custom-call(s32[85]{0:T(128)S(1)} %get-tuple-element.25.refs_0_, s32[10]{0:T(128)S(1)} %get-tuple-element.26.refs_0_.refs_1_, s32[7]{0:T(128)S(1)} %get-tuple-element.29.refs_2_.refs_1_, ...), custom_call_target="tpu_custom_call" | custom-call | flops 1 | bytes 1 | tf_op jit(solution)/shard_map/own_kernel/pallas_call | solution.py:313
  22.9 0.1 collective-permute-done.3.refs_1_.refs_4_
  23.0 0.8 %trace_kernel.1 = f32[8,128]{1,0:T(8,128)S(1)} custom-call(bf16[512,512]{1,0:T(8,128)(2,1)S(1)} %get-tuple-element.35.refs_0_, bf16[512,512]{1,0:T(8,128)(2,1)S(1)} %collective-permute-done.3.refs_1_.refs_4_, f32[1]{0:T(128)} %get-tuple-element.36.refs_2_), custom_call_target="tpu_custom_call" | custom-call | flops 1 | bytes 1 | tf_op jit(solution)/shard_map/trace_kernel/pallas_call | solution.py:321
  23.8 2.8 %collective-permute-start.8 = (bf16[512,512]{1,0:T(8,128)(2,1)S(1)}, bf16[512,512]{1,0:T(8,128)(2,1)S(1)}, u32[]{:S(2)}, u32[]{:S(2)}) collective-permute-start(bf16[512,512]{1,0:T(8,128)(2,1)S(1)} %get-tuple-element.44), channel_id=1, source_target_pairs={{1,2},{3,4},{5,6},{7,8},{9,10},{11,12},{13,14},{15,0},{2,1},{4,3},... | collective-permute-start | bytes 1572872 | tf_op jit(solution)/shard_map/ppermute | solution.py:19
  26.6 0.0 collective-permute-start.4
  26.6 1.2 %collective-permute-done.4 = f32[8,128]{1,0:T(8,128)S(1)} collective-permute-done((f32[8,128]{1,0:T(8,128)S(1)}, f32[8,128]{1,0:T(8,128)S(1)}, u32[]{:S(2)}, u32[]{:S(2)}) %collective-permute-start.4) | collective-permute-done | bytes 4128 | tf_op jit(solution)/shard_map/ppermute | solution.py:19
  27.8 1.9 %far_kernel.1.refs_5_ = bf16[6,12,128,128]{3,2,1,0:T(8,128)(2,1)} custom-call(s32[85]{0:T(128)S(1)} %get-tuple-element.25.refs_0_, s32[7]{0:T(128)S(1)} %get-tuple-element.29.refs_2_.refs_1_, bf16[768,512]{1,0:T(8,128)(2,1)S(1)} %get-tuple-element.28.refs_3_.refs_5_.refs_2_, ...), custom_call_target="tpu_custom_call", output_to_operand_aliasing={{}: (5, {})} | custom-call | flops 1 | bytes 1 | tf_op jit(solution)/shard_map/far_kernel/pallas_call | solution.py:328
  29.7 0.1 collective-permute-start.5
  29.7 3.7 %collective-permute-done.5 = f32[8,128]{1,0:T(8,128)S(1)} collective-permute-done((f32[8,128]{1,0:T(8,128)S(1)}, f32[8,128]{1,0:T(8,128)S(1)}, u32[]{:S(2)}, u32[]{:S(2)}) %collective-permute-start.5) | collective-permute-done | bytes 4128 | tf_op jit(solution)/shard_map/ppermute | solution.py:19
  33.4 0.0 collective-permute-start.6
  33.4 4.5 %collective-permute-done.6 = f32[8,128]{1,0:T(8,128)S(1)} collective-permute-done((f32[8,128]{1,0:T(8,128)S(1)}, f32[8,128]{1,0:T(8,128)S(1)}, u32[]{:S(2)}, u32[]{:S(2)}) %collective-permute-start.6) | collective-permute-done | bytes 4128 | tf_op jit(solution)/shard_map/ppermute | solution.py:19
  38.0 0.0 collective-permute-start.7
  38.0 0.0 collective-permute-done.8.refs_4_
  38.0 1.9 %last_kernel.1 = bf16[6,12,128,128]{3,2,1,0:T(8,128)(2,1)} custom-call(s32[85]{0:T(128)S(1)} %get-tuple-element.25.refs_0_, s32[7]{0:T(128)S(1)} %get-tuple-element.29.refs_2_.refs_1_, bf16[768,512]{1,0:T(8,128)(2,1)S(1)} %get-tuple-element.28.refs_3_.refs_5_.refs_2_, f32[768,512]{1,0:T(8,128)S(1)} %get-tuple-element.43.refs_3_, ...), custom_call_target="tpu_custom_call", output_to_operand_aliasing={{}: (5, {})} | custom-call | flops 1 | bytes 1 | tf_op jit(solution)/shard_map/last_kernel/pallas_call | solution.py:328
  39.8 1.2 %collective-permute-done.7 = f32[8,128]{1,0:T(8,128)S(1)} collective-permute-done((f32[8,128]{1,0:T(8,128)S(1)}, f32[8,128]{1,0:T(8,128)S(1)}, u32[]{:S(2)}, u32[]{:S(2)}) %collective-permute-start.7) | collective-permute-done | bytes 4128 | tf_op jit(solution)/shard_map/ppermute | solution.py:19
  41.0 0.5 %slice.3 = f32[1,1]{1,0:T(1,128)} slice(f32[8,128]{1,0:T(8,128)S(1)} %add.15), slice={[0:1], [0:1]} | slice | bytes 8 | tf_op jit(solution)/shard_map/slice | solution.py:346
  (4 shorter events, 0.0 us)
Async XLA Ops:
  0.6 13.7 %copy-start = (s32[6,12]{1,0:T(8,128)S(1)}, s32[6,12]{1,0:T(8,128)}, u32[]{:S(2)}) copy-start(s32[6,12]{1,0:T(8,128)} %refs_0_.1) | copy-start | bytes 868
  0.6 14.8 %collective-permute-start.2 = (bf16[6,12,128,128]{3,2,1,0:T(8,128)(2,1)}, bf16[6,12,128,128]{3,2,1,0:T(8,128)(2,1)S(1)}, u32[]{:S(2)}, u32[]{:S(2)}) collective-permute-start(bf16[6,12,128,128]{3,2,1,0:T(8,128)(2,1)} %refs_3_.1), channel_id=1, source_target_pairs={{0,1},{1,0},{2,3},{3,2},{4,5},{5,4},{6,7},{7,6},{8,9},{9,8},{10,11... | collective-permute-start | bytes 7077896 | tf_op jit(solution)/shard_map/ppermute | solution.py:19
  1.2 8.8 %collective-permute-start = (s32[6,12]{1,0:T(8,128)}, s32[6,12]{1,0:T(8,128)S(1)}, u32[]{:S(2)}, u32[]{:S(2)}) collective-permute-start(s32[6,12]{1,0:T(8,128)} %refs_0_.1), channel_id=1, source_target_pairs={{1,2},{3,4},{5,6},{7,8},{9,10},{11,12},{13,14},{15,0},{2,1},{4,3},... | collective-permute-start | bytes 872 | tf_op jit(solution)/shard_map/ppermute | solution.py:19
  11.5 11.5 %collective-permute-start.3 = (bf16[512,512]{1,0:T(8,128)(2,1)S(1)}, bf16[512,512]{1,0:T(8,128)(2,1)S(1)}, u32[]{:S(2)}, u32[]{:S(2)}) collective-permute-start(bf16[512,512]{1,0:T(8,128)(2,1)S(1)} %get-tuple-element.32), channel_id=1, source_target_pairs={{1,2},{3,4},{5,6},{7,8},{9,10},{11,12},{13,14},{15,0},{2,1},{4,3},... | collective-permute-start | bytes 1572872 | tf_op jit(solution)/shard_map/ppermute | solution.py:19
  14.3 1.2 %collective-permute-start.1 = (s32[6,12]{1,0:T(8,128)S(1)}, s32[6,12]{1,0:T(8,128)S(1)}, u32[]{:S(2)}, u32[]{:S(2)}) collective-permute-start(s32[6,12]{1,0:T(8,128)S(1)} %copy-done), channel_id=1, source_target_pairs={{0,1},{1,0},{2,3},{3,2},{4,5},{5,4},{6,7},{7,6},{8,9},{9,8},{10,11... | collective-permute-start | bytes 872 | tf_op jit(solution)/shard_map/ppermute | solution.py:19
  23.8 14.1 %collective-permute-start.8 = (bf16[512,512]{1,0:T(8,128)(2,1)S(1)}, bf16[512,512]{1,0:T(8,128)(2,1)S(1)}, u32[]{:S(2)}, u32[]{:S(2)}) collective-permute-start(bf16[512,512]{1,0:T(8,128)(2,1)S(1)} %get-tuple-element.44), channel_id=1, source_target_pairs={{1,2},{3,4},{5,6},{7,8},{9,10},{11,12},{13,14},{15,0},{2,1},{4,3},... | collective-permute-start | bytes 1572872 | tf_op jit(solution)/shard_map/ppermute | solution.py:19
  26.6 1.2 %collective-permute-start.4 = (f32[8,128]{1,0:T(8,128)S(1)}, f32[8,128]{1,0:T(8,128)S(1)}, u32[]{:S(2)}, u32[]{:S(2)}) collective-permute-start(f32[8,128]{1,0:T(8,128)S(1)} %trace_kernel.1), channel_id=1, source_target_pairs={{0,1},{1,0},{2,3},{3,2},{4,5},{5,4},{6,7},{7,6},{8,9},{9,8},{10,11... | collective-permute-start | bytes 12296 | tf_op jit(solution)/shard_map/ppermute | solution.py:19
  29.7 3.8 %collective-permute-start.5 = (f32[8,128]{1,0:T(8,128)S(1)}, f32[8,128]{1,0:T(8,128)S(1)}, u32[]{:S(2)}, u32[]{:S(2)}) collective-permute-start(f32[8,128]{1,0:T(8,128)S(1)} %add.12), channel_id=1, source_target_pairs={{0,4},{1,5},{2,6},{3,7},{4,0},{5,1},{6,2},{7,3},{8,12},{9,13},{10,... | collective-permute-start | bytes 12296 | tf_op jit(solution)/shard_map/ppermute | solution.py:19
  33.4 4.5 %collective-permute-start.6 = (f32[8,128]{1,0:T(8,128)S(1)}, f32[8,128]{1,0:T(8,128)S(1)}, u32[]{:S(2)}, u32[]{:S(2)}) collective-permute-start(f32[8,128]{1,0:T(8,128)S(1)} %add.13), channel_id=1, source_target_pairs={{0,8},{1,9},{2,10},{3,11},{4,12},{5,13},{6,14},{7,15},{8,0},{9,1},... | collective-permute-start | bytes 12296 | tf_op jit(solution)/shard_map/ppermute | solution.py:19
  38.0 3.0 %collective-permute-start.7 = (f32[8,128]{1,0:T(8,128)S(1)}, f32[8,128]{1,0:T(8,128)S(1)}, u32[]{:S(2)}, u32[]{:S(2)}) collective-permute-start(f32[8,128]{1,0:T(8,128)S(1)} %add.14), channel_id=1, source_target_pairs={{0,3},{1,2},{2,1},{3,0},{4,7},{5,6},{6,5},{7,4},{8,11},{9,10},{10,... | collective-permute-start | bytes 12296 | tf_op jit(solution)/shard_map/ppermute | solution.py:19
